TPU v7x, 32 devices: a whole 2x2x4 slice. The times are simulated.
32 devices in a mesh: dp: 8 (over y, x, core), side: 4 (over z).
Axes of the slice: x: 2, y: 2, z: 4, core: 2. Of those that a mesh axis runs over, the one named last changes fastest.
Arguments:
- hidden_in: bfloat16 [32, 512, 768], P(('dp', 'side')), may hold values from -6 to 6
- side_state: bfloat16 [32, 512, 96], P(('dp', 'side')), may hold values from -6 to 6
- lengths: int32 [32], P('dp'), may hold values from 16 to 512, as said below
- assign: int32 [32], P('dp'), may hold values from 0 to 3, as said below
- buckets: int32 [1023], replicated, may hold values from 0 to 31
- backbone_gain_attn: float32 [768], replicated, may hold values from 0.25 to 1.75
- backbone_query: bfloat16 [768, 768], replicated, may hold values from -0.109375 to 0.109375
- backbone_key: bfloat16 [768, 768], replicated, may hold values from -0.109375 to 0.109375
- backbone_value: bfloat16 [768, 768], replicated, may hold values from -0.21875 to 0.21875
- backbone_project: bfloat16 [768, 768], replicated, may hold values from -1.25 to 1.25
- backbone_rel: float32 [32, 12], replicated, may hold values from -4 to 4
- backbone_gain_ff: float32 [768], replicated, may hold values from 0.25 to 1.75
- backbone_ff_in: bfloat16 [768, 3072], replicated, may hold values from -0.21875 to 0.21875
- backbone_ff_out: bfloat16 [3072, 768], replicated, may hold values from -0.15625 to 0.15625
- down_weight: bfloat16 [768, 96], replicated, may hold values from -0.21875 to 0.21875
- gate_logit: float32 [96], replicated, may hold values from -6 to 6
- side_gain_attn: float32 [96], replicated, may hold values from 0.25 to 1.75
- side_query: bfloat16 [96, 96], replicated, may hold values from -0.4375 to 0.4375
- side_key: bfloat16 [96, 96], replicated, may hold values from -0.4375 to 0.4375
- side_value: bfloat16 [96, 96], replicated, may hold values from -0.625 to 0.625
- side_project: bfloat16 [96, 96], replicated, may hold values from -3.5 to 3.5
- side_rel: float32 [32, 12], replicated, may hold values from -4 to 4
- side_gain_ff: float32 [96], replicated, may hold values from 0.25 to 1.75
- side_ff_in: bfloat16 [96, 384], replicated, may hold values from -0.625 to 0.625
- side_ff_out: bfloat16 [384, 96], replicated, may hold values from -0.4375 to 0.4375
- cotangent: bfloat16 [32, 512, 96], P(('dp', 'side')), may hold values from -6 to 6
Outputs:
- side_out: bfloat16 [32, 512, 96], P(('dp', 'side'))
- grad_state: float32 [32, 512, 96], P(('dp', 'side'))
- grad_down: float32 [768, 96], replicated
- grad_gate: float32 [96], replicated
- grad_gain_attn: float32 [96], replicated
- grad_query: float32 [96, 96], replicated
- grad_key: float32 [96, 96], replicated
- grad_value: float32 [96, 96], replicated
- grad_project: float32 [96, 96], replicated
- grad_rel: float32 [32, 12], replicated
- grad_gain_ff: float32 [96], replicated
- grad_ff_in: float32 [96, 384], replicated
- grad_ff_out: float32 [384, 96], replicated
Inputs may be any that keep to these rules, and one draw needn't show every extreme that they name: `lengths`: each sequence has at least 16 real tokens; one sequence has exactly 512. Within each group of 4 sequences of one index of dp, assign is a permutation of the group's sequences (numbered in side order, the side device of sequence n being n). Every backbone device of the group holds at most 1 sequence of any one side device, and exactly 1 of some.
All inputs are finite; a program needn't handle non-finite values.
Results may differ from a plain program's by a relative error of at most 0.028.
Values may be sent and summed in bfloat16 or wider, within the bound.
No kernel may reach another device: no remote copies, remote signals or barrier semaphores. Data moves between devices by JAX's collectives and lax.ppermute only.
A program may use at most 192 MiB of HBM per device.

v0:
```python
import math

import jax
import jax.numpy as jnp
from jax import lax
from jax.sharding import PartitionSpec as P

D = 768
H = 12
DS = 96
SH = 12
L = 512
ROWS_DEV = 1


epsilon = 1e-06
masked_score = -1000000000.0


def normalize(rows):
    scale = lax.rsqrt(jnp.mean(rows * rows, axis=1, keepdims=True) + epsilon)
    return (rows * scale, scale)


def smooth_unit(values):
    return jax.nn.gelu(values, approximate=False)


def smooth_slope(values):
    normal_cdf = 0.5 * (1.0 + lax.erf(values * (1.0 / math.sqrt(2.0))))
    normal_pdf = jnp.exp(-0.5 * values * values) * (1.0 / math.sqrt(2.0 * math.pi))
    return normal_cdf + values * normal_pdf


def norm_backward(grad_normed, unit_rows, scale, gain):
    grad_unit = grad_normed * gain
    grad_gain = jnp.sum(grad_normed * unit_rows, axis=0)
    grad_rows = scale * (
        grad_unit - unit_rows * jnp.mean(grad_unit * unit_rows, axis=1, keepdims=True)
    )
    return (grad_gain, grad_rows)


def skew_rows(per_offset):
    head_count = per_offset.shape[0]
    padded = jnp.concatenate([per_offset, jnp.zeros((head_count, 1), per_offset.dtype)], axis=1)
    tiled = jnp.broadcast_to(padded[:, None, :], (head_count, L, 2 * L)).reshape(
        head_count, 2 * L * L
    )
    shifted = tiled[:, L - 1 : L - 1 + L * (2 * L - 1)].reshape(head_count, L, 2 * L - 1)
    return shifted[:, :, :L]


def position_bias(buckets, table):
    onehot = (buckets[:, None] == jnp.arange(table.shape[0], dtype=jnp.int32)[None, :]).astype(
        jnp.float32
    )
    per_offset = jnp.dot(
        table.T, onehot.T, precision=lax.Precision.HIGHEST, preferred_element_type=jnp.float32
    )
    return (skew_rows(per_offset), onehot)


def diagonal_totals(grid_values):
    head_count = grid_values.shape[0]
    widened = jnp.concatenate(
        [grid_values, jnp.zeros((head_count, L, L - 1), grid_values.dtype)], axis=2
    )
    widened = widened.reshape(head_count, L * (2 * L - 1))
    widened = jnp.concatenate(
        [widened, jnp.zeros((head_count, L), grid_values.dtype)], axis=1
    ).reshape(head_count, L, 2 * L)
    column_sums = jnp.sum(widened, axis=1, dtype=jnp.float32)
    return jnp.concatenate([column_sums[:, L + 1 :], column_sums[:, :L]], axis=1)


def split_heads(rows, head_count):
    return rows.reshape(L, head_count, rows.shape[1] // head_count)


def masked_scores(query_rows, key_rows, bias, length, head_count):
    scores = (
        jnp.einsum(
            "qhd,khd->hqk",
            split_heads(query_rows, head_count),
            split_heads(key_rows, head_count),
            preferred_element_type=jnp.float32,
        )
        + bias
    )
    visible = jnp.arange(L, dtype=jnp.int32)[None, None, :] < length
    return jnp.where(visible, scores, masked_score)


def attention_forward(query_rows, key_rows, value_rows, bias, length, head_count):
    scores = masked_scores(query_rows, key_rows, bias, length, head_count)
    row_max = jnp.max(scores, axis=2, keepdims=True)
    exponent = jnp.exp(scores - row_max)
    row_total = jnp.sum(exponent, axis=2, keepdims=True)
    probability = (exponent / row_total).astype(jnp.bfloat16)
    context = jnp.einsum(
        "hqk,khd->qhd",
        probability,
        split_heads(value_rows, head_count),
        preferred_element_type=jnp.float32,
    )
    return (context.reshape(L, -1).astype(jnp.bfloat16), row_max + jnp.log(row_total))


def attention_backward(diag_total, items, bias, head_count):
    query_rows, key_rows, value_rows, grad_context, log_total, length = items
    scores = masked_scores(query_rows, key_rows, bias, length, head_count)
    soft_probs = jnp.exp(scores - log_total)
    probability = soft_probs.astype(jnp.bfloat16)
    context_heads = split_heads(grad_context, head_count)
    grad_probs = jnp.einsum(
        "qhd,khd->hqk",
        context_heads,
        split_heads(value_rows, head_count),
        preferred_element_type=jnp.float32,
    )
    grad_scores = (
        soft_probs * (grad_probs - jnp.sum(grad_probs * soft_probs, axis=2, keepdims=True))
    ).astype(jnp.bfloat16)
    grad_query = jnp.einsum(
        "hqk,khd->qhd",
        grad_scores,
        split_heads(key_rows, head_count),
        preferred_element_type=jnp.float32,
    )
    grad_key = jnp.einsum(
        "hqk,qhd->khd",
        grad_scores,
        split_heads(query_rows, head_count),
        preferred_element_type=jnp.float32,
    )
    grad_value = jnp.einsum(
        "hqk,qhd->khd", probability, context_heads, preferred_element_type=jnp.float32
    )
    moved = tuple(
        (
            member.reshape(L, -1).astype(jnp.bfloat16)
            for member in (grad_query, grad_key, grad_value)
        )
    )
    return (diag_total + diagonal_totals(grad_scores), moved)


def route_tables(assign, side_rank, side_count, capacity):
    group_rows = assign.shape[0]
    slot_index = jnp.arange(group_rows, dtype=jnp.int32)
    slot_dest = assign // ROWS_DEV
    slot_source = slot_index // ROWS_DEV
    same_pair = (
        (slot_dest[:, None] == slot_dest[None, :])
        & (slot_source[:, None] == slot_source[None, :])
        & (slot_index[None, :] < slot_index[:, None])
    )
    slot_rank = jnp.sum(same_pair.astype(jnp.int32), axis=1)
    buffer_slots = jnp.arange(side_count * capacity, dtype=jnp.int32)
    send_position = lax.dynamic_slice_in_dim(
        slot_dest * capacity + slot_rank, side_rank * ROWS_DEV, ROWS_DEV
    )
    send_table = (buffer_slots[:, None] == send_position[None, :]).astype(jnp.bfloat16)
    wanted = side_rank * ROWS_DEV + jnp.arange(ROWS_DEV, dtype=jnp.int32)
    holder = (assign[None, :] == wanted[:, None]).astype(jnp.int32)
    recv_position = jnp.sum(holder * (slot_source * capacity + slot_rank)[None, :], axis=1)
    receive_table = (recv_position[:, None] == buffer_slots[None, :]).astype(jnp.bfloat16)
    slot_natural = lax.dynamic_slice_in_dim(assign, side_rank * ROWS_DEV, ROWS_DEV)
    return (send_table, receive_table, slot_natural)


def pack_rows(table, rows):
    return jnp.dot(table, rows, preferred_element_type=jnp.float32).astype(jnp.bfloat16)


def contract_rows(left_rows, right_rows):
    return jnp.einsum("ra,rb->ab", left_rows, right_rows, preferred_element_type=jnp.float32)


def times_transpose(rows, weight):
    return jnp.einsum("ra,ba->rb", rows, weight, preferred_element_type=jnp.float32)


def project(rows, weight):
    return jnp.dot(rows, weight, preferred_element_type=jnp.float32)


def shards(
    hidden_in,
    side_state,
    lengths,
    assign,
    buckets,
    backbone_gain_attn,
    backbone_query,
    backbone_key,
    backbone_value,
    backbone_project,
    backbone_rel,
    backbone_gain_ff,
    backbone_ff_in,
    backbone_ff_out,
    down_weight,
    gate_logit,
    side_gain_attn,
    side_query,
    side_key,
    side_value,
    side_project,
    side_rel,
    side_gain_ff,
    side_ff_in,
    side_ff_out,
    cotangent,
):
    side_count = lax.axis_size("side")
    side_rank = lax.axis_index("side")
    capacity = max(1, ROWS_DEV // side_count)
    send_table, receive_table, slot_natural = route_tables(assign, side_rank, side_count, capacity)
    group_index = jnp.arange(assign.shape[0], dtype=jnp.int32)
    slot_length = jnp.sum(
        jnp.where(slot_natural[:, None] == group_index[None, :], lengths[None, :], 0), axis=1
    )
    row_length = lax.dynamic_slice_in_dim(lengths, side_rank * ROWS_DEV, ROWS_DEV)
    backbone_bias, backbone_onehot = position_bias(buckets, backbone_rel)
    side_bias, side_onehot = position_bias(buckets, side_rel)
    flat_rows = hidden_in.reshape(ROWS_DEV * L, D).astype(jnp.float32)
    unit_rows, first_scale = normalize(flat_rows)
    normed_rows = (unit_rows * backbone_gain_attn).astype(jnp.bfloat16)
    query_all = project(normed_rows, backbone_query).astype(jnp.bfloat16).reshape(ROWS_DEV, L, D)
    key_all = project(normed_rows, backbone_key).astype(jnp.bfloat16).reshape(ROWS_DEV, L, D)
    value_all = project(normed_rows, backbone_value).astype(jnp.bfloat16).reshape(ROWS_DEV, L, D)
    context_all, backbone_total = lax.map(
        lambda items: attention_forward(items[0], items[1], items[2], backbone_bias, items[3], H),
        (query_all, key_all, value_all, slot_length),
    )
    stream = flat_rows + project(context_all.reshape(ROWS_DEV * L, D), backbone_project)
    unit_ff, second_scale = normalize(stream)
    normed_ff = (unit_ff * backbone_gain_ff).astype(jnp.bfloat16)
    inner_rows = smooth_unit(project(normed_ff, backbone_ff_in)).astype(jnp.bfloat16)
    hidden_rows = (stream + project(inner_rows, backbone_ff_out)).astype(jnp.bfloat16)
    taps = project(hidden_rows, down_weight).astype(jnp.bfloat16).reshape(ROWS_DEV, L * DS)
    outgoing = pack_rows(send_table, taps).reshape(side_count, capacity, L * DS)
    incoming = lax.all_to_all(outgoing, "side", split_axis=0, concat_axis=0, tiled=True)
    tap_values = pack_rows(receive_table, incoming.reshape(side_count * capacity, L * DS)).reshape(
        ROWS_DEV * L, DS
    )
    tap_float = tap_values.astype(jnp.float32)
    state_rows = side_state.reshape(ROWS_DEV * L, DS).astype(jnp.float32)
    gate_value = jax.nn.sigmoid(gate_logit)
    mixed_rows = gate_value * tap_float + (1.0 - gate_value) * state_rows
    unit_attn, scale_attn = normalize(mixed_rows)
    normed_attn = (unit_attn * side_gain_attn).astype(jnp.bfloat16)
    query_side = project(normed_attn, side_query).astype(jnp.bfloat16).reshape(ROWS_DEV, L, DS)
    key_side = project(normed_attn, side_key).astype(jnp.bfloat16).reshape(ROWS_DEV, L, DS)
    value_side = project(normed_attn, side_value).astype(jnp.bfloat16).reshape(ROWS_DEV, L, DS)
    context_side, log_total = lax.map(
        lambda items: attention_forward(items[0], items[1], items[2], side_bias, items[3], SH),
        (query_side, key_side, value_side, row_length),
    )
    context_flat = context_side.reshape(ROWS_DEV * L, DS)
    residual = mixed_rows + project(context_flat, side_project)
    unit_side_ff, scale_side_ff = normalize(residual)
    normed_side_ff = (unit_side_ff * side_gain_ff).astype(jnp.bfloat16)
    pre_act = project(normed_side_ff, side_ff_in)
    inner_side = smooth_unit(pre_act).astype(jnp.bfloat16)
    output = residual + project(inner_side, side_ff_out)
    grad_out = cotangent.reshape(ROWS_DEV * L, DS)
    grad_ff_out = contract_rows(inner_side, grad_out)
    grad_pre = (times_transpose(grad_out, side_ff_out) * smooth_slope(pre_act)).astype(jnp.bfloat16)
    grad_ff_in = contract_rows(normed_side_ff, grad_pre)
    grad_gain_ff, grad_resid_norm = norm_backward(
        times_transpose(grad_pre, side_ff_in), unit_side_ff, scale_side_ff, side_gain_ff
    )
    grad_resid = grad_out.astype(jnp.float32) + grad_resid_norm
    grad_attn = grad_resid.astype(jnp.bfloat16)
    grad_project = contract_rows(context_flat, grad_attn)
    grad_context = (
        times_transpose(grad_attn, side_project).astype(jnp.bfloat16).reshape(ROWS_DEV, L, DS)
    )

    def backward_step(diag_total, items):
        return attention_backward(diag_total, items, side_bias, SH)

    diag_zero = jnp.zeros((SH, 2 * L - 1), jnp.float32)
    diag_total, grad_heads = lax.scan(
        backward_step,
        diag_zero,
        (query_side, key_side, value_side, grad_context, log_total, row_length),
    )
    grad_rel = jnp.dot(
        side_onehot.T,
        diag_total.T,
        precision=lax.Precision.HIGHEST,
        preferred_element_type=jnp.float32,
    )
    grad_query_rows = grad_heads[0].reshape(ROWS_DEV * L, DS)
    grad_key_rows = grad_heads[1].reshape(ROWS_DEV * L, DS)
    grad_value_rows = grad_heads[2].reshape(ROWS_DEV * L, DS)
    grad_query = contract_rows(normed_attn, grad_query_rows)
    grad_key = contract_rows(normed_attn, grad_key_rows)
    grad_value = contract_rows(normed_attn, grad_value_rows)
    grad_normed = (
        times_transpose(grad_query_rows, side_query)
        + times_transpose(grad_key_rows, side_key)
        + times_transpose(grad_value_rows, side_value)
    )
    grad_gain_attn, grad_mixed_norm = norm_backward(
        grad_normed, unit_attn, scale_attn, side_gain_attn
    )
    grad_mixed = grad_resid + grad_mixed_norm
    grad_state = (1.0 - gate_value) * grad_mixed
    grad_gate = (
        jnp.sum(grad_mixed * (tap_float - state_rows), axis=0) * gate_value * (1.0 - gate_value)
    )
    grad_tap = (grad_mixed * gate_value).astype(jnp.bfloat16)
    returned = pack_rows(receive_table.T, grad_tap.reshape(ROWS_DEV, L * DS)).reshape(
        side_count, capacity, L * DS
    )
    arrived = lax.all_to_all(returned, "side", split_axis=0, concat_axis=0, tiled=True)
    slot_grads = pack_rows(send_table.T, arrived.reshape(side_count * capacity, L * DS)).reshape(
        ROWS_DEV * L, DS
    )
    grad_down = contract_rows(hidden_rows, slot_grads)
    summed = lax.psum(
        (
            grad_down,
            grad_gate,
            grad_gain_attn,
            grad_query,
            grad_key,
            grad_value,
            grad_project,
            grad_rel,
            grad_gain_ff,
            grad_ff_in,
            grad_ff_out,
        ),
        ("dp", "side"),
    )
    side_out = output.astype(jnp.bfloat16).reshape(ROWS_DEV, L, DS)
    return (side_out, grad_state.reshape(ROWS_DEV, L, DS)) + tuple(summed)


def solution(mesh):
    return jax.shard_map(
        shards,
        mesh=mesh,
        in_specs=(
            P(("dp", "side"), None, None),
            P(("dp", "side"), None, None),
            P("dp"),
            P("dp"),
            P(),
            P(),
            P(),
            P(),
            P(),
            P(),
            P(),
            P(),
            P(),
            P(),
            P(),
            P(),
            P(),
            P(),
            P(),
            P(),
            P(),
            P(),
            P(),
            P(),
            P(),
            P(("dp", "side"), None, None),
        ),
        out_specs=(
            P(("dp", "side"), None, None),
            P(("dp", "side"), None, None),
            P(),
            P(),
            P(),
            P(),
            P(),
            P(),
            P(),
            P(),
            P(),
            P(),
            P(),
        ),
        check_vma=False,
    )
```

profile of v0, /device:TPU:0, one launch (start us, length us, event | category | flops | bytes accessed | tf_op | source)
XLA Modules:
  0.0 994.3 jit_solution(10551048502859444195)
XLA Ops:
  12.7 11.5 %broadcast_in_dim.70 = f32[12,512,1024]{2,1,0:T(8,128)} broadcast(f32[12,1024]{1,0:T(8,128)S(1)} %concatenate.18), dimensions={0,2} | broadcast | bytes 25214976 | tf_op jit(solution)/shard_map/broadcast_in_dim | solution.py:47
  24.2 10.9 %pad.6 = f32[16,512,1024]{2,1,0:T(8,128)S(1)} pad(f32[12,512,1024]{2,1,0:T(8,128)} %broadcast_in_dim.70, f32[]{:T(128)} %constant.63.clone.1), padding=0_4x0_0x0_0 | pad | bytes 58720260
  35.1 39.7 %copy.144 = f32[2,8,512,1024]{3,1,2,0:T(8,128)} copy(f32[2,8,512,1024]{3,2,1,0:T(8,128)S(1)} %bitcast.152) | data formatting | bytes 67108864
  74.8 25.5 %slice.26 = f32[12,523776]{1,0:T(8,128)} slice(f32[12,524288]{1,0:T(8,128)} %bitcast.154), slice={[0:12], [511:524287]} | slice | bytes 50282496 | tf_op jit(solution)/shard_map/slice | solution.py:50
  100.3 41.6 %reshape.404 = f32[12,512,1023]{2,1,0:T(8,128)} reshape(f32[12,523776]{1,0:T(8,128)} %slice.26) | data formatting | bytes 50282496 | tf_op jit(solution)/shard_map/reshape | solution.py:50
  141.9 10.7 %slice.27 = f32[12,512,512]{2,1,0:T(8,128)} slice(f32[12,512,1023]{2,1,0:T(8,128)} %reshape.404), slice={[0:12], [0:512], [0:512]} | slice | bytes 25165824 | tf_op jit(solution)/shard_map/slice | solution.py:51
  152.6 12.7 %copy.138 = f32[12,512,512]{1,2,0:T(8,128)} copy(f32[12,512,512]{2,1,0:T(8,128)} %slice.27) | data formatting | bytes 25165824
  174.8 11.8 %add_select_fusion.1 = f32[12,512,512]{1,2,0:T(8,128)} fusion(f32[12,512,512]{1,2,0:T(8,128)} %copy.138, pred[512]{0:T(512)(128)(4,1)S(1)} %iota_compare_fusion.5, bf16[512,12,64]{0,2,1:T(8,128)(2,1)S(1)} %bitcast.157, bf16[512,12,64]{0,2,1:T(8,128)(2,1)S(1)} %bitcast.158), kind=kOutput, calls=%fused_computation.11 | convolution fusion | flops 408944640 | bytes 26739200 | tf_op jit(solution)/shard_map/while/body/eval_jaxpr/qhd,khd->hqk/dot_general | solution.py:83
  186.6 10.4 %fusion.133 = f32[12,512]{1,0:T(8,128)S(1)} fusion(f32[12,512,512]{1,2,0:T(8,128)} %add_select_fusion.1), kind=kOutput, calls=%fused_computation.212 | output fusion | flops 6291967 | bytes 12607488 | tf_op jit(solution)/shard_map/while/body/eval_jaxpr/sub | solution.py:98
  197.1 12.2 %fusion.25 = bf16[12,64,512]{2,1,0:T(8,128)(2,1)} fusion(bf16[512,12,64]{0,2,1:T(8,128)(2,1)S(1)} %bitcast.161, f32[12,512]{1,0:T(8,128)S(1)} %fusion.133, f32[12,512,512]{1,2,0:T(8,128)} %add_select_fusion.1), kind=kOutput, calls=%fused_computation.50 | convolution fusion | flops 412490240 | bytes 14180352 | tf_op jit(solution)/shard_map/while/body/eval_jaxpr/hqk,khd->qhd/dot_general | solution.py:101
  212.4 22.0 %add_convert_fusion = bf16[512,768]{1,0:T(8,128)(2,1)S(1)} fusion(f32[512,768]{1,0:T(8,128)} %get-tuple-element.120, bf16[3072,768]{1,0:T(8,128)(2,1)} %param.39, bf16[768,3072]{1,0:T(8,128)(2,1)} %param.38, f32[768]{0:T(1024)S(1)} %copy-done.27, f32[512]{0:T(512)S(1)} %add_rsqrt_fusion.2), kind=kOutput, calls=%fused_computation.44 | convolution fusion | flops 4936040448 | bytes 11801600 | tf_op jit(solution)/shard_map/dot_general | solution.py:186
  247.4 11.5 %broadcast_in_dim.75 = f32[12,512,1024]{2,1,0:T(8,128)} broadcast(f32[12,1024]{1,0:T(8,128)S(1)} %concatenate.19), dimensions={0,2} | broadcast | bytes 25214976 | tf_op jit(solution)/shard_map/broadcast_in_dim | solution.py:47
  259.0 10.9 %pad.7 = f32[16,512,1024]{2,1,0:T(8,128)S(1)} pad(f32[12,512,1024]{2,1,0:T(8,128)} %broadcast_in_dim.75, f32[]{:T(128)} %constant.63.clone.1), padding=0_4x0_0x0_0 | pad | bytes 58720260
  269.9 39.7 %copy.145 = f32[2,8,512,1024]{3,1,2,0:T(8,128)} copy(f32[2,8,512,1024]{3,2,1,0:T(8,128)S(1)} %bitcast.151) | data formatting | bytes 67108864
  309.6 25.5 %slice.28 = f32[12,523776]{1,0:T(8,128)} slice(f32[12,524288]{1,0:T(8,128)} %bitcast.155), slice={[0:12], [511:524287]} | slice | bytes 50282496 | tf_op jit(solution)/shard_map/slice | solution.py:50
  335.1 41.6 %reshape.412 = f32[12,512,1023]{2,1,0:T(8,128)} reshape(f32[12,523776]{1,0:T(8,128)} %slice.28) | data formatting | bytes 50282496 | tf_op jit(solution)/shard_map/reshape | solution.py:50
  376.7 10.7 %slice.29 = f32[12,512,512]{2,1,0:T(8,128)} slice(f32[12,512,1023]{2,1,0:T(8,128)} %reshape.412), slice={[0:12], [0:512], [0:512]} | slice | bytes 25165824 | tf_op jit(solution)/shard_map/slice | solution.py:51
  387.4 12.6 %copy.139 = f32[12,512,512]{1,2,0:T(8,128)} copy(f32[12,512,512]{2,1,0:T(8,128)} %slice.29) | data formatting | bytes 25165824
  446.7 9.0 concatenate.20.clone
  455.7 34.7 %reshape.421 = bf16[12,523776]{1,0:T(8,128)(2,1)} reshape(bf16[12,512,1023]{2,1,0:T(8,128)(2,1)} %concatenate.20.clone) | data formatting | bytes 25141248 | tf_op jit(solution)/shard_map/while/body/eval_jaxpr/reshape | solution.py:69
  499.0 35.9 %copy.146 = f32[2,8,512,1024]{3,2,1,0:T(8,128)} copy(f32[2,8,512,1024]{3,1,2,0:T(8,128)S(1)} %bitcast.153) | data formatting | bytes 67108864
  534.8 9.0 slice_reduce_fusion
  580.4 251.8 %all-reduce.9.cloned.1.call-done = (f32[96]{0:T(128)}, f32[96]{0:T(128)}, f32[96,96]{1,0:T(8,128)}, f32[96,96]{1,0:T(8,128)}, f32[96,96]{1,0:T(8,128)}, /*index=...) async-done(((f32[96]{0:T(128)}, f32[96]{0:T(128)}, f32[96,96]{1,0:T(8,128)}, f32[96,96]{1,0:T(8,128)}, f32[96,96]{1,0:T(8,128)}, /*index=5*/f32[96,96]{1,0:T(8,128)}, ...) | async-done | bytes 150160 | tf_op jit(solution)/shard_map/psum | solution.py:326
  832.1 139.8 %all-reduce.11.cloned.1.call-done = (f32[768,96]{0,1:T(8,128)}, f32[96,384]{1,0:T(8,128)}, f32[384,96]{0,1:T(8,128)}) async-done(((f32[768,96]{0,1:T(8,128)}, f32[96,384]{1,0:T(8,128)}, f32[384,96]{0,1:T(8,128)}), (f32[768,96]{0,1:T(8,128)}, f32[96,384]{1,0:T(8,128)}, f32[384,96]{0,1:T(8,128)})) %all-reduce.11.cloned.1.call-update) | async-done | bytes 589840 | tf_op jit(solution)/shard_map/psum | solution.py:326
  (187 shorter events, 137.6 us)
Async XLA Ops:
  7.2 202.1 %copy-start = (bf16[768,768]{1,0:T(8,128)(2,1)S(1)}, bf16[768,768]{1,0:T(8,128)(2,1)}, u32[]{:S(2)}) copy-start(bf16[768,768]{1,0:T(8,128)(2,1)} %param.35) | copy-start | bytes 3538948
  152.6 12.7 %copy-start.23 = (s32[4]{0:T(128)S(1)}, s32[4]{0:T(128)}, u32[]{:S(2)}) copy-start(s32[4]{0:T(128)} %param.29) | copy-start | bytes 52
  152.6 13.4 %copy-start.30 = (s32[4]{0:T(128)S(1)}, s32[4]{0:T(128)}, u32[]{:S(2)}) copy-start(s32[4]{0:T(128)} %param.28) | copy-start | bytes 52
  152.6 15.4 %copy-start.6 = (bf16[1,512,768]{2,1,0:T(8,128)(2,1)S(1)}, bf16[1,512,768]{2,1,0:T(8,128)(2,1)}, u32[]{:S(2)}) copy-start(bf16[1,512,768]{2,1,0:T(8,128)(2,1)} %param.26) | copy-start | bytes 2359300
  152.6 15.4 %copy-start.26 = (f32[768]{0:T(1024)S(1)}, f32[768]{0:T(1024)}, u32[]{:S(2)}) copy-start(f32[768]{0:T(1024)} %param.31) | copy-start | bytes 9220
  186.6 10.4 %copy-start.7 = (bf16[512,768]{0,1:T(8,128)(2,1)S(1)}, bf16[512,768]{0,1:T(8,128)(2,1)}, u32[]{:S(2)}) copy-start(bf16[512,768]{0,1:T(8,128)(2,1)} %copy.109) | copy-start | bytes 2359300
  197.0 15.3 %copy-start.27 = (f32[768]{0:T(1024)S(1)}, f32[768]{0:T(1024)}, u32[]{:S(2)}) copy-start(f32[768]{0:T(1024)} %param.37) | copy-start | bytes 9220
  212.4 22.1 %copy-start.10 = (bf16[768,96]{0,1:T(8,128)(2,1)S(1)}, bf16[768,96]{0,1:T(8,128)(2,1)}, u32[]{:S(2)}) copy-start(bf16[768,96]{0,1:T(8,128)(2,1)} %param.40) | copy-start | bytes 442372
  212.4 34.0 %copy-start.31 = (s32[4]{0:T(128)S(1)}, s32[4]{0:T(128)}, u32[]{:S(2)}) copy-start(s32[4]{0:T(128)} %param.28) | copy-start | bytes 52
  212.4 34.6 %copy-start.25 = (f32[32,12]{0,1:T(8,128)S(1)}, f32[32,12]{0,1:T(8,128)}, u32[]{:S(2)}) copy-start(f32[32,12]{0,1:T(8,128)} %param.47) | copy-start | bytes 4612
  212.4 34.6 %copy-start.29 = (s32[1023]{0:T(1024)S(1)}, s32[1023]{0:T(1024)}, u32[]{:S(2)}) copy-start(s32[1023]{0:T(1024)} %param.30) | copy-start | bytes 12280
  234.5 24.5 %copy-start.3 = (bf16[512,768]{1,0:T(8,128)(2,1)}, bf16[512,768]{1,0:T(8,128)(2,1)S(1)}, u32[]{:S(2)}) copy-start(bf16[512,768]{1,0:T(8,128)(2,1)S(1)} %add_convert_fusion) | copy-start | bytes 2359300
  240.1 162.7 %all-to-all-start = ((bf16[4,2,24576]{2,1,0:T(2,128)(2,1)}), bf16[4,2,24576]{2,1,0:T(2,128)(2,1)S(1)}, u32[]{:S(2)}, u32[]{:S(2)}) async-start(bf16[4,2,24576]{2,1,0:T(2,128)(2,1)} %reshape.433), calls=%async_computation | async-start | bytes 786432 | tf_op jit(solution)/shard_map/all_to_all | solution.py:245
  387.4 12.6 %copy-start.19 = (f32[96]{0:T(128)S(1)}, f32[96]{0:T(128)}, u32[]{:S(2)}) copy-start(f32[96]{0:T(128)} %param.42) | copy-start | bytes 1156
  387.4 12.8 %copy-start.32 = (f32[96]{0:T(128)S(1)}, f32[96]{0:T(128)}, u32[]{:S(2)}) copy-start(f32[96]{0:T(128)} %param.41) | copy-start | bytes 1156
  387.4 13.1 %copy-start.5 = (bf16[1,512,96]{1,2,0:T(8,128)(2,1)S(1)}, bf16[1,512,96]{1,2,0:T(8,128)(2,1)}, u32[]{:S(2)}) copy-start(bf16[1,512,96]{1,2,0:T(8,128)(2,1)} %param.27) | copy-start | bytes 294916
  400.2 11.5 %copy-start.22 = (f32[96]{0:T(128)}, f32[96]{0:T(128)S(1)}, u32[]{:S(2)}) copy-start(f32[96]{0:T(128)S(1)} %get-tuple-element.113) | copy-start | bytes 1156
  545.8 17.3 %slice-start = ((f32[12,1024]{1,0:T(8,128)}), f32[12,512]{1,0:T(8,128)S(1)}, s32[]{:S(2)}) async-start(f32[12,1024]{1,0:T(8,128)} %copy-done.9), calls=%async_computation.4 | async-start | bytes 65536 | tf_op jit(solution)/shard_map/while/body/eval_jaxpr/slice | solution.py:74
  545.8 32.6 %copy-start.4 = (bf16[512,768]{1,0:T(8,128)(2,1)S(1)}, bf16[512,768]{1,0:T(8,128)(2,1)}, u32[]{:S(2)}) copy-start(bf16[512,768]{1,0:T(8,128)(2,1)} %copy-done.3) | copy-start | bytes 2359300
  548.7 30.7 %copy-start.17 = (bf16[384,96]{0,1:T(8,128)(2,1)S(1)}, bf16[384,96]{0,1:T(8,128)(2,1)}, u32[]{:S(2)}) copy-start(bf16[384,96]{0,1:T(8,128)(2,1)} %param.50) | copy-start | bytes 221188
  551.3 435.9 %copy-start.1 = (bf16[768,768]{1,0:T(8,128)(2,1)S(1)}, bf16[768,768]{1,0:T(8,128)(2,1)}, u32[]{:S(2)}) copy-start(bf16[768,768]{1,0:T(8,128)(2,1)} %param.35) | copy-start | bytes 3538948
  558.0 16.2 %all-to-all-start.1 = ((bf16[4,2,24576]{2,1,0:T(2,128)(2,1)}), bf16[4,2,24576]{2,1,0:T(2,128)(2,1)S(1)}, u32[]{:S(2)}, u32[]{:S(2)}) async-start(bf16[4,2,24576]{2,1,0:T(2,128)(2,1)} %reshape.435), calls=%async_computation.1 | async-start | bytes 786432 | tf_op jit(solution)/shard_map/all_to_all | solution.py:321
  563.1 269.0 %all-reduce.9.cloned.1.call-start = ((), (), s32[]{:S(2)}) async-start(), calls=%async_computation.2 | async-start | bytes 412672 | tf_op jit(solution)/shard_map/psum | solution.py:326
  566.1 405.8 %all-reduce.11.cloned.1.call-start = ((), (), s32[]{:S(2)}) async-start(), calls=%async_computation.3 | async-start | bytes 1179648 | tf_op jit(solution)/shard_map/psum | solution.py:326
  (14 other events, 55.1 us)
Sparse Core Ops, SparseCore 0:
  571.5 260.5 all-reduce.8
  841.8 130.1 all-reduce.10
where the time goes:
time: 1010 us; the launch traced here: 994 us
  local copies, waits for them, and re-layouts  421 us (42%)
  waiting for transfers between devices  397 us (39%)
  matrix products  97.9 us (10%)
  other arithmetic  51.7 us (5%)
  between operations  15 us (1%)
  starting transfers between devices  11.4 us (1%)
    psum x2, waiting for transfers between devices, shards(): lax.psum((grad_down, grad_gate, grad_gain_attn, grad_query, grad_key, gra...  392 us
    unnamed x89, local copies, waits for them, and re-layouts  191 us
    reshape x2, local copies, waits for them, and re-layouts, skew_rows(): tiled[:, L - 1:L - 1 + L * (2 * L - 1)].reshape(head_count, L, 2 * L - 1)  83.2 us
    slice x2, local copies, waits for them, and re-layouts, skew_rows(): tiled[:, L - 1:L - 1 + L * (2 * L - 1)].reshape(head_count, L, 2 * L - 1)  51 us
    dot_general x12, matrix products, project(): return jnp.dot(rows, weight, preferred_element_type=jnp.float32)  36.7 us
    reshape x1, local copies, waits for them, and re-layouts, diagonal_totals(): widened = widened.reshape(head_count, L * (2 * L - 1))  34.7 us
    broadcast_in_dim x2, local copies, waits for them, and re-layouts, skew_rows(): jnp.broadcast_to(padded[:, None, :], (head_count, L, 2 * L))  23 us
    slice x2, local copies, waits for them, and re-layouts, skew_rows(): return shifted[:, :, :L]  21.4 us
  transfers between devices with their start and end apart: 4, of which 3 were waited for; matrix products, arithmetic and copies ran while one was open for 17% of the time, Pallas kernels for 0%

commit v1 on v0

v1 whole, which is shorter than its diff:
```python
import functools
import math

import jax
import jax.numpy as jnp
from jax import lax
from jax.experimental import pallas as pl
from jax.experimental.pallas import tpu as pltpu
from jax.sharding import PartitionSpec as P

D = 768
H = 12
HD = 64
FF = 3072
NB = 32
DS = 96
SH = 12
SHD = 8
FS = 384
L = 512
W = 128
TILE = 128

EPS = 1e-06
MASKED = -1e9
LIMIT = 60.0
F32 = jnp.float32
BF16 = jnp.bfloat16
VMEM_BYTES = 44 * 1024 * 1024


def dot(a, b, dims=((1,), (0,)), precision=None):
    return lax.dot_general(
        a, b, (dims, ((), ())), precision=precision, preferred_element_type=F32
    )


def dot_nt(a, b):
    return dot(a, b, ((1,), (1,)))


def dot_tn(a, b):
    return dot(a, b, ((0,), (0,)))


def normal_cdf(v):
    return 0.5 * (1.0 + lax.erf(v * (1.0 / math.sqrt(2.0))))


def offset_table(buckets, rel):
    rows = lax.broadcasted_iota(jnp.int32, (NB, 2 * L), 0)
    onehot = (rows == buckets).astype(F32)
    return dot(rel, onehot, precision=lax.Precision.HIGHEST)


def toeplitz(row):
    wide = jnp.broadcast_to(row, (TILE, 2 * L))
    return pltpu.roll(wide, 2 * L - (TILE - 1), 1, stride=1, stride_axis=0)


def bias_block(bias_ref, head, block):
    start = (L // TILE - 1 - block) * TILE
    return bias_ref[head, :, start : start + L]


def lane_group(shape, size):
    return lax.broadcasted_iota(jnp.int32, shape, len(shape) - 1) // size


def bounded(q, k, table, size, heads):
    rows = lax.broadcasted_iota(jnp.int32, (q.shape[1], W), 0) // size
    cols = lax.broadcasted_iota(jnp.int32, (q.shape[1], W), 1)
    pick = ((rows == cols) & (rows < heads)).astype(BF16)
    qf, kf = q.astype(F32), k.astype(F32)
    qn = jnp.max(dot((qf * qf).astype(BF16), pick), axis=0, keepdims=True)
    kn = jnp.max(dot((kf * kf).astype(BF16), pick), axis=0, keepdims=True)
    top = jnp.max(jnp.sqrt(qn) * jnp.sqrt(kn)) * 1.02
    return top + jnp.max(jnp.abs(table)) < LIMIT


def start_all(pairs, sems):
    copies = [pltpu.make_async_copy(src, dst, sems.at[n]) for n, (src, dst) in enumerate(pairs)]
    for copy in copies:
        copy.start()
    return copies


def backbone_kernel(
    lengths_ref, assign_ref, rel_hbm, bucket_hbm, x_hbm, gain1_hbm, wq_hbm, wk_hbm, wv_hbm, wo_hbm, gain2_hbm, w1_hbm,
    w2_hbm, wd_hbm,
    hidden_ref, taps_ref,
    rel, buckets, x_ref, gain1_ref, wq, wk, wv, wo, gain2_ref, w1, w2, wd, sems,
    normed, q_s, k_s, vx, ctx, bias, stream, inner,
):
    pairs = (
        (rel_hbm, rel), (bucket_hbm, buckets.at[0]), (x_hbm, x_ref), (gain1_hbm, gain1_ref.at[0]),
        (wq_hbm, wq), (wk_hbm, wk), (wv_hbm, wv), (wo_hbm, wo), (gain2_hbm, gain2_ref.at[0]),
        (w1_hbm, w1), (w2_hbm, w2), (wd_hbm, wd),
    )
    copies = start_all(pairs, sems)
    length = lengths_ref[assign_ref[lax.axis_index("side")]]

    copies[0].wait()
    copies[1].wait()
    table = offset_table(buckets[...], rel[...])
    for head in range(H):
        bias[head] = toeplitz(table[head : head + 1])
    copies[2].wait()
    copies[3].wait()
    x = x_ref[...].astype(F32)
    scale = lax.rsqrt(jnp.mean(x * x, axis=1, keepdims=True) + EPS)
    normed[...] = (x * scale * gain1_ref[...]).astype(BF16)
    copies[4].wait()
    q_s[...] = dot(normed[...], wq[...]).astype(BF16)
    copies[5].wait()
    k_s[...] = dot(normed[...], wk[...]).astype(BF16)
    copies[6].wait()
    live_row = lax.broadcasted_iota(jnp.int32, (L, 1), 0) < length
    value = dot(normed[...], wv[...])
    value = jnp.where(live_row, value, 0.0).astype(BF16)
    ones = jnp.where(live_row, 1.0, 0.0).astype(BF16)
    for pair in range(H // 2):
        vx[pair, :, :W] = value[:, pair * W : (pair + 1) * W]
        vx[pair, :, W:] = jnp.broadcast_to(ones, (L, W))
    low_half = lax.broadcasted_iota(jnp.int32, (L, W), 1) < HD
    low_row = lax.broadcasted_iota(jnp.int32, (TILE, W), 1) < HD
    live = lax.broadcasted_iota(jnp.int32, (1, L), 1) < length

    def attend(pair, stable):
        lanes = pl.ds(pl.multiple_of(pair * W, W), W)
        keys = k_s[:, lanes]
        for block in range(L // TILE):
            rows = slice(block * TILE, (block + 1) * TILE)
            query = q_s[rows, lanes]
            results = []
            for half in range(2):
                mine = low_row if half == 0 else jnp.logical_not(low_row)
                scores = dot_nt(jnp.where(mine, query, jnp.zeros_like(query)), keys)
                scores = scores + bias_block(bias, pair * 2 + half, block)
                if stable:
                    scores = jnp.where(live, scores, MASKED)
                    scores = scores - jnp.max(scores, axis=1, keepdims=True)
                results.append(dot(jnp.exp(scores).astype(BF16), vx[pair]))
            top = jnp.where(low_row, results[0][:, :W], results[1][:, :W])
            total = jnp.where(low_row, results[0][:, W:], results[1][:, W:])
            ctx[rows, lanes] = (top / total).astype(BF16)

    safe = bounded(q_s[...], k_s[...], table, HD, H)

    @pl.when(safe)
    def _():
        @pl.loop(0, H // 2)
        def _(pair):
            attend(pair, False)

    @pl.when(jnp.logical_not(safe))
    def _():
        @pl.loop(0, H // 2)
        def _(pair):
            attend(pair, True)

    copies[7].wait()
    copies[8].wait()
    flow = x_ref[...].astype(F32) + dot(ctx[...], wo[...])
    stream[...] = flow
    scale = lax.rsqrt(jnp.mean(flow * flow, axis=1, keepdims=True) + EPS)
    normed[...] = (flow * scale * gain2_ref[...]).astype(BF16)
    copies[9].wait()
    step = 256

    @pl.loop(0, FF // step)
    def _(n):
        cols = pl.ds(pl.multiple_of(n * step, step), step)
        pre = dot(normed[...], w1[:, cols])
        inner[:, cols] = (pre * normal_cdf(pre)).astype(BF16)

    copies[10].wait()
    for n in range(D // 256):
        cols = slice(n * 256, (n + 1) * 256)
        hidden_ref[:, cols] = (stream[:, cols] + dot(inner[...], w2[:, cols])).astype(BF16)
    copies[11].wait()
    taps_ref[...] = dot_nt(hidden_ref[...], wd[...]).astype(BF16)


def backbone(*args):
    smem = pl.BlockSpec(memory_space=pltpu.SMEM)
    vmem = pl.BlockSpec(memory_space=pltpu.VMEM)
    hbm = pl.BlockSpec(memory_space=pl.ANY)
    return pl.pallas_call(
        backbone_kernel,
        out_shape=(
            jax.ShapeDtypeStruct((L, D), BF16),
            jax.ShapeDtypeStruct((L, DS), BF16),
        ),
        in_specs=[smem, smem] + [hbm] * 12,
        out_specs=(vmem, vmem),
        scratch_shapes=[
            pltpu.VMEM((H, NB), F32),
            pltpu.VMEM((1, 2 * L), jnp.int32),
            pltpu.VMEM((L, D), BF16),
            pltpu.VMEM((1, D), F32),
            pltpu.VMEM((D, D), BF16),
            pltpu.VMEM((D, D), BF16),
            pltpu.VMEM((D, D), BF16),
            pltpu.VMEM((D, D), BF16),
            pltpu.VMEM((1, D), F32),
            pltpu.VMEM((D, FF), BF16),
            pltpu.VMEM((FF, D), BF16),
            pltpu.VMEM((DS, D), BF16),
            pltpu.SemaphoreType.DMA((12,)),
            pltpu.VMEM((L, D), BF16),
            pltpu.VMEM((L, D), BF16),
            pltpu.VMEM((L, D), BF16),
            pltpu.VMEM((H // 2, L, 2 * W), BF16),
            pltpu.VMEM((L, D), BF16),
            pltpu.VMEM((H, TILE, 2 * L), F32),
            pltpu.VMEM((L, D), F32),
            pltpu.VMEM((L, FF), BF16),
        ],
        compiler_params=pltpu.CompilerParams(vmem_limit_bytes=60 * 1024 * 1024),
        cost_estimate=pl.CostEstimate(
            flops=9_000_000_000, bytes_accessed=17_000_000, transcendentals=5_000_000
        ),
        name="backbone",
    )(*args)


DOWN0, QKV0, SMALL0, PROJ0, FFIN0, FFOUT0 = 0, 576, 864, 896, 992, 1280
PACK = 1568
HALF = PACK // 2


def side_kernel(
    count, lengths_ref, assign_ref, taps_ref, *rest
):
    moved_hbm = rest[:count]
    (
        bucket_hbm, rel_hbm, gate_hbm, gain1_hbm, gain2_hbm, wq_hbm, wk_hbm, wv_hbm, wo_hbm, w1_hbm, w2_hbm, hidden_hbm,
        out_ref, gstate_ref, keep_ref, send_ref,
        buckets, rel, gate_ref, gain1_ref, gain2_ref, wq_ref, wk_ref, wv_ref, wo_ref, w1_ref, w2_ref, hidden,
        moved, sems, wpad, bias, probs, q_s, k_s, v_s, top_s, sum_s, dcx, qt_s, dct_s, dq_s, dkt, dvt,
        diag, dtab, pack,
    ) = rest[count:]
    rank = lax.axis_index("side")
    seq = assign_ref[rank]
    pairs = (
        (bucket_hbm, buckets.at[0]), (rel_hbm, rel), (gate_hbm, gate_ref.at[0]), (gain1_hbm, gain1_ref.at[0]),
        (gain2_hbm, gain2_ref.at[0]), (wq_hbm, wq_ref), (wk_hbm, wk_ref), (wv_hbm, wv_ref), (wo_hbm, wo_ref),
        (w1_hbm, w1_ref), (w2_hbm, w2_ref), (hidden_hbm, hidden),
    )
    copies = start_all(pairs, sems)
    for step in range(count):

        @pl.when(lax.rem(rank + count - seq, count) == step)
        def _():
            pltpu.make_async_copy(moved_hbm[step], moved, sems.at[12]).start()

    for copy in copies[:-1]:
        copy.wait()
    length = lengths_ref[seq]
    wpad[...] = jnp.zeros_like(wpad)
    wpad[0, :, :DS] = wq_ref[...]
    wpad[1, :, :DS] = wk_ref[...]
    wpad[2, :, :DS] = wv_ref[...]
    wpad[3, :, :DS] = wo_ref[...].astype(F32).T.astype(BF16)
    table = offset_table(buckets[...], rel[...])
    for head in range(SH):
        bias[head] = toeplitz(table[head : head + 1])

    gate = jax.nn.sigmoid(gate_ref[...])
    gain1, gain2 = gain1_ref[...], gain2_ref[...]
    pltpu.make_async_copy(moved_hbm[0], moved, sems.at[12]).wait()
    tap = taps_ref[...].astype(F32)
    old = moved[0].astype(F32).T
    mixed = gate * tap + (1.0 - gate) * old
    scale1 = lax.rsqrt(jnp.mean(mixed * mixed, axis=1, keepdims=True) + EPS)
    unit1 = mixed * scale1
    normed1 = (unit1 * gain1).astype(BF16)
    lane = lax.broadcasted_iota(jnp.int32, (L, W), 1)
    live_row = lax.broadcasted_iota(jnp.int32, (L, W), 0) < length
    query = dot(normed1, wpad[0]).astype(BF16)
    key = dot(normed1, wpad[1]).astype(BF16)
    value = dot(normed1, wpad[2]).astype(BF16)
    one = jnp.ones((L, W), BF16)
    mask_key = jnp.where(live_row, 0.0, MASKED)
    q_s[...] = jnp.where(lane == DS, 1.0, query.astype(F32)).astype(BF16)
    k_s[...] = jnp.where(lane == DS, mask_key, key.astype(F32)).astype(BF16)
    v_s[:, :W] = value
    v_s[:, W:] = one
    safe = bounded(query, key, table, SHD, SH)
    head_of = lax.broadcasted_iota(jnp.int32, (TILE, W), 1) // SHD
    marker = lax.broadcasted_iota(jnp.int32, (TILE, W), 1) == DS
    zero_tile = jnp.zeros((TILE, W), BF16)
    blocks = [slice(b * TILE, (b + 1) * TILE) for b in range(L // TILE)]

    def attend(head, stable):
        mine = head_of == head
        for block, rows in enumerate(blocks):
            q_h = jnp.where(mine | marker, q_s[rows], zero_tile)
            scores = dot_nt(q_h, k_s[...]) + bias_block(bias, head, block)
            if stable:
                scores = scores - jnp.max(scores, axis=1, keepdims=True)
            weight = jnp.exp(scores).astype(BF16)
            probs[head, rows] = weight
            both = dot(weight, v_s[...])
            top_s[rows] = jnp.where(mine, both[:, :W], top_s[rows])
            sum_s[rows] = jnp.where(mine, both[:, W:], sum_s[rows])

    sum_s[...] = jnp.ones_like(sum_s)
    top_s[...] = jnp.zeros_like(top_s)

    @pl.when(safe)
    def _():
        @pl.loop(0, SH)
        def _(head):
            attend(head, False)

    @pl.when(jnp.logical_not(safe))
    def _():
        @pl.loop(0, SH)
        def _(head):
            attend(head, True)

    inverse = 1.0 / sum_s[...]
    context = top_s[...] * inverse
    context16 = context[:, :DS].astype(BF16)
    residual = mixed + dot(context16, wo_ref[...])
    scale2 = lax.rsqrt(jnp.mean(residual * residual, axis=1, keepdims=True) + EPS)
    unit2 = residual * scale2
    normed2 = (unit2 * gain2).astype(BF16)
    pre = dot(normed2, w1_ref[...])
    cdf = normal_cdf(pre)
    inner = (pre * cdf).astype(BF16)
    out_ref[...] = (residual + dot_nt(inner, w2_ref[...])).T.astype(BF16)

    cotangent = moved[1].astype(F32).T.astype(BF16)
    slope = cdf + pre * (jnp.exp(-0.5 * pre * pre) * (1.0 / math.sqrt(2.0 * math.pi)))
    d_pre = (dot(cotangent, w2_ref[...]) * slope).astype(BF16)
    g_ffout = dot_tn(cotangent, inner)
    g_ffin = dot_tn(normed2, d_pre)
    for n in range(FS // W):
        pack[FFIN0 + n * DS : FFIN0 + (n + 1) * DS] = g_ffin[:, n * W : (n + 1) * W]
        pack[FFOUT0 + n * DS : FFOUT0 + (n + 1) * DS] = g_ffout[:, n * W : (n + 1) * W]
    dy = dot_nt(d_pre, w1_ref[...])
    g_gain2 = jnp.sum(dy * unit2, axis=0, keepdims=True)
    dyg = dy * gain2
    d_resid = cotangent.astype(F32) + scale2 * (
        dyg - unit2 * jnp.mean(dyg * unit2, axis=1, keepdims=True)
    )
    d_attn = d_resid.astype(BF16)
    pack[PROJ0 : PROJ0 + DS] = jnp.zeros((DS, W), F32)
    pack[PROJ0 : PROJ0 + DS, :DS] = dot_tn(context16, d_attn)
    d_context = dot(d_attn, wpad[3]).astype(BF16)
    d_scaled = (d_context.astype(F32) * inverse).astype(BF16)
    product = d_scaled.astype(F32) * context
    r_head = lax.broadcasted_iota(jnp.int32, (W, W), 0) // SHD
    c_head = lax.broadcasted_iota(jnp.int32, (W, W), 1) // SHD
    same = (r_head == c_head).astype(F32)
    delta = dot(product, same, precision=lax.Precision.HIGHEST) * -0.25
    delta_hi = delta.astype(BF16).astype(F32)
    dcx[:, :W] = d_scaled
    dcx[:, W:] = jnp.where(lane % 2 == 0, delta_hi, delta - delta_hi).astype(BF16)
    d_scaled_t = d_scaled.astype(F32).T
    query_t = query.astype(F32).T
    for head in range(SH):
        rows = slice(head * SHD, (head + 1) * SHD)
        qt_s[head] = query_t[rows].astype(BF16)
        dct_s[head] = d_scaled_t[rows].astype(BF16)
    dq_s[...] = jnp.zeros_like(dq_s)
    dkt[...] = jnp.zeros_like(dkt)
    dvt[...] = jnp.zeros_like(dvt)
    dtab[...] = jnp.zeros_like(dtab)

    @pl.loop(0, SH)
    def _(head):
        diag[...] = jnp.zeros_like(diag)
        mine = head_of == head
        both_mine = jnp.concatenate([mine, mine], axis=1)
        tiles = []
        for block, rows in enumerate(blocks):
            lhs = jnp.where(both_mine, dcx[rows], jnp.zeros((TILE, 2 * W), BF16))
            d_scores = probs[head, rows].astype(F32) * dot_nt(lhs, v_s[...])
            start = (L // TILE - 1 - block) * TILE
            diag[:, start : start + L] += d_scores
            d16 = d_scores.astype(BF16)
            tiles.append(d16)
            dq_s[rows] = jnp.where(mine, dot(d16, k_s[...]), dq_s[rows])
        d_all = jnp.concatenate(tiles, axis=0)
        rows8 = pl.ds(pl.multiple_of(head * SHD, SHD), SHD)
        dkt[rows8] = dot(qt_s[head], d_all)
        dvt[rows8] = dot(dct_s[head], probs[head])
        cur = diag[...]
        half = TILE // 2
        while half >= 8:
            cur = pltpu.roll(cur[:half], half, 1) + cur[half:]
            half //= 2
        for shift in (4, 2, 1):
            cur = pltpu.roll(cur, shift, 1) + pltpu.roll(cur, 8 - shift, 0)
        dtab[pl.ds(head, 1)] = cur[:1]

    dq = dq_s[...].astype(BF16)
    dk = dkt[...].T.astype(BF16)
    dv = dvt[...].T.astype(BF16)
    for n, grad in enumerate((dq, dk, dv)):
        pack[QKV0 + n * DS : QKV0 + (n + 1) * DS] = dot_tn(normed1, grad)
    d_normed = dot_nt(dq, wpad[0]) + dot_nt(dk, wpad[1]) + dot_nt(dv, wpad[2])
    dyg = d_normed * gain1
    d_mixed = d_resid + scale1 * (dyg - unit1 * jnp.mean(dyg * unit1, axis=1, keepdims=True))
    gstate_ref[...] = ((1.0 - gate) * d_mixed).T.astype(BF16)
    d_tap = (gate * d_mixed).astype(BF16)
    copies[11].wait()
    down_t = dot_tn(d_tap, hidden[...])
    for n in range(D // W):
        pack[DOWN0 + n * DS : DOWN0 + (n + 1) * DS] = down_t[:, n * W : (n + 1) * W]
    rows = lax.broadcasted_iota(jnp.int32, (NB, 2 * L), 0)
    onehot = (rows == buckets[...]).astype(F32)
    totals = dot(dtab[...], onehot, ((1,), (1,)), lax.Precision.HIGHEST)
    pack[SMALL0 : SMALL0 + NB] = jnp.zeros((NB, W), F32)
    pack[SMALL0 : SMALL0 + 16, :NB] = totals
    g_gate = gate * (1.0 - gate) * jnp.sum(d_mixed * (tap - old), axis=0, keepdims=True)
    g_gain1 = jnp.sum(d_normed * unit1, axis=0, keepdims=True)
    pack[SMALL0 + 16 : SMALL0 + 17, :DS] = g_gate
    pack[SMALL0 + 17 : SMALL0 + 18, :DS] = g_gain1
    pack[SMALL0 + 18 : SMALL0 + 19, :DS] = g_gain2
    core = lax.rem(lax.axis_index("dp"), 2)
    keep_ref[...] = pack[pl.ds(pl.multiple_of(core * HALF, HALF), HALF)].astype(BF16)
    send_ref[...] = pack[pl.ds(pl.multiple_of((1 - core) * HALF, HALF), HALF)].astype(BF16)


def side_block(lengths, assign, taps, moved, *args):
    smem = pl.BlockSpec(memory_space=pltpu.SMEM)
    vmem = pl.BlockSpec(memory_space=pltpu.VMEM)
    hbm = pl.BlockSpec(memory_space=pl.ANY)
    count = len(moved)
    return pl.pallas_call(
        functools.partial(side_kernel, count),
        out_shape=(
            jax.ShapeDtypeStruct((DS, L), BF16),
            jax.ShapeDtypeStruct((DS, L), BF16),
            jax.ShapeDtypeStruct((HALF, W), BF16),
            jax.ShapeDtypeStruct((HALF, W), BF16),
        ),
        in_specs=[smem, smem, vmem] + [hbm] * (count + len(args)),
        out_specs=(vmem,) * 4,
        scratch_shapes=[
            pltpu.VMEM((1, 2 * L), jnp.int32),
            pltpu.VMEM((SH, NB), F32),
            pltpu.VMEM((1, DS), F32),
            pltpu.VMEM((1, DS), F32),
            pltpu.VMEM((1, DS), F32),
            pltpu.VMEM((DS, DS), BF16),
            pltpu.VMEM((DS, DS), BF16),
            pltpu.VMEM((DS, DS), BF16),
            pltpu.VMEM((DS, DS), BF16),
            pltpu.VMEM((DS, FS), BF16),
            pltpu.VMEM((DS, FS), BF16),
            pltpu.VMEM((L, D), BF16),
            pltpu.VMEM((2, DS, L), BF16),
            pltpu.SemaphoreType.DMA((13,)),
            pltpu.VMEM((4, DS, W), BF16),
            pltpu.VMEM((SH, TILE, 2 * L), F32),
            pltpu.VMEM((SH, L, L), BF16),
            pltpu.VMEM((L, W), BF16),
            pltpu.VMEM((L, W), BF16),
            pltpu.VMEM((L, 2 * W), BF16),
            pltpu.VMEM((L, W), F32),
            pltpu.VMEM((L, W), F32),
            pltpu.VMEM((L, 2 * W), BF16),
            pltpu.VMEM((SH, SHD, L), BF16),
            pltpu.VMEM((SH, SHD, L), BF16),
            pltpu.VMEM((L, W), F32),
            pltpu.VMEM((W, L), F32),
            pltpu.VMEM((W, L), F32),
            pltpu.VMEM((TILE, 2 * L), F32),
            pltpu.VMEM((16, 2 * L), F32),
            pltpu.VMEM((PACK, W), F32),
        ],
        compiler_params=pltpu.CompilerParams(vmem_limit_bytes=VMEM_BYTES),
        cost_estimate=pl.CostEstimate(
            flops=9_000_000_000, bytes_accessed=4_000_000, transcendentals=5_000_000
        ),
        name="side_block",
    )(lengths, assign, taps, *moved, *args)


def finish_kernel(count, assign_ref, mine_hbm, other_hbm, *rest):
    outs, gstates = rest[:count], rest[count : 2 * count]
    results = rest[2 * count : 2 * count + 13]
    half, out, gstate16, *parts, sems = rest[2 * count + 13 :]
    rank = lax.axis_index("side")
    core = lax.rem(lax.axis_index("dp"), 2)
    first = pltpu.make_async_copy(mine_hbm, half.at[core], sems.at[0])
    second = pltpu.make_async_copy(other_hbm, half.at[1 - core], sems.at[1])
    first.start()
    second.start()
    slot = jnp.int32(0)
    for n in range(count):
        slot = jnp.where(assign_ref[n] == rank, n, slot)
    for step in range(count):

        @pl.when(lax.rem(rank + count - slot, count) == step)
        def _():
            pltpu.make_async_copy(gstates[step], gstate16, sems.at[2]).start()
            pltpu.make_async_copy(outs[step], out, sems.at[3]).start()

    gstate, down, gate, gain1, gq, gk, gv, go, rel, gain2, g1, g2 = parts
    pltpu.make_async_copy(gstates[0], gstate16, sems.at[2]).wait()
    pltpu.make_async_copy(outs[0], out, sems.at[3]).wait()
    gstate[...] = gstate16[...].astype(F32)
    first.wait()
    second.wait()

    def take(start, stop):
        pieces = []
        for side in range(2):
            low, high = max(start, side * HALF), min(stop, (side + 1) * HALF)
            if low < high:
                pieces.append(half[side, low - side * HALF : high - side * HALF].astype(F32))
        return pieces[0] if len(pieces) == 1 else jnp.concatenate(pieces, axis=0)

    for n in range(D // W):
        down[:, n * W : (n + 1) * W] = take(DOWN0 + n * DS, DOWN0 + (n + 1) * DS)
    for n, ref in enumerate((gq, gk, gv)):
        ref[...] = take(QKV0 + n * DS, QKV0 + (n + 1) * DS)[:, :DS]
    small = take(SMALL0, SMALL0 + NB)
    rel[...] = small[:SH, :NB]
    gate[...] = small[16:17, :DS]
    gain1[...] = small[17:18, :DS]
    gain2[...] = small[18:19, :DS]
    go[...] = take(PROJ0, PROJ0 + DS)[:, :DS]
    for n in range(FS // W):
        g1[:, n * W : (n + 1) * W] = take(FFIN0 + n * DS, FFIN0 + (n + 1) * DS)
        g2[:, n * W : (n + 1) * W] = take(FFOUT0 + n * DS, FFOUT0 + (n + 1) * DS)
    pairs = [
        (ref.at[0] if ref.shape[0] == 1 else ref, result)
        for ref, result in zip([out, *parts], results, strict=True)
    ]
    for copy in start_all(pairs, sems):
        copy.wait()


def finish(assign, mine, other, outs, gstates):
    smem = pl.BlockSpec(memory_space=pltpu.SMEM)
    hbm = pl.BlockSpec(memory_space=pl.ANY)
    count = len(outs)
    parts = [
        (DS, L), (DS, D), (1, DS), (1, DS), (DS, DS), (DS, DS), (DS, DS), (DS, DS), (SH, NB), (1, DS), (DS, FS), (DS, FS),
    ]
    shapes = [jax.ShapeDtypeStruct(p[1:] if p[0] == 1 else p, F32) for p in parts]
    return pl.pallas_call(
        functools.partial(finish_kernel, count),
        out_shape=(jax.ShapeDtypeStruct((DS, L), BF16), *shapes),
        in_specs=[smem] + [hbm] * (2 + 2 * count),
        out_specs=(hbm,) * 13,
        scratch_shapes=[
            pltpu.VMEM((2, HALF, W), BF16),
            pltpu.VMEM((DS, L), BF16),
            pltpu.VMEM((DS, L), BF16),
            *[pltpu.VMEM(p, F32) for p in parts],
            pltpu.SemaphoreType.DMA((13,)),
        ],
        compiler_params=pltpu.CompilerParams(vmem_limit_bytes=16 * 1024 * 1024),
        name="finish",
    )(assign, mine, other, *outs, *gstates)


def swap(value, axis, bit):
    size = lax.axis_size(axis)
    return lax.ppermute(value, axis, [(i, i ^ bit) for i in range(size)])


def rotations(value):
    size = lax.axis_size("side")
    return [value] + [
        lax.ppermute(value, "side", [(i, (i + k) % size) for i in range(size)])
        for k in range(1, size)
    ]


def add(one, two):
    return (one.astype(F32) + two.astype(F32)).astype(BF16)


def total(keep, send):
    mine = add(keep, swap(send, "dp", 1))
    for axis, first in (("dp", 2), ("side", 1)):
        bit = first
        while bit < lax.axis_size(axis):
            mine = add(mine, swap(mine, axis, bit))
            bit *= 2
    return mine, swap(mine, "dp", 1)


def shards(
    hidden_in, side_state, lengths, assign, buckets,
    backbone_gain_attn, backbone_query, backbone_key, backbone_value, backbone_project, backbone_rel,
    backbone_gain_ff, backbone_ff_in, backbone_ff_out, down_weight, gate_logit,
    side_gain_attn, side_query, side_key, side_value, side_project, side_rel,
    side_gain_ff, side_ff_in, side_ff_out, cotangent,
):
    moved = rotations(jnp.stack([side_state[0].T, cotangent[0].T]))
    wide = jnp.pad(buckets, (0, 1))
    hidden, taps = backbone(
        lengths, assign, backbone_rel.T, wide, hidden_in[0], backbone_gain_attn,
        backbone_query, backbone_key, backbone_value, backbone_project, backbone_gain_ff,
        backbone_ff_in, backbone_ff_out, down_weight.T,
    )
    out, gstate, keep, send = side_block(
        lengths, assign, taps, moved, wide, side_rel.T, gate_logit, side_gain_attn, side_gain_ff,
        side_query, side_key, side_value, side_project, side_ff_in, side_ff_out.T, hidden,
    )
    outs, gstates = rotations(out), rotations(gstate)
    mine, other = total(keep, send)
    res = finish(assign, mine, other, outs, gstates)
    out, gstate, down, gate, gain1, gq, gk, gv, go, rel, gain2, g1, g2 = res
    return (
        out.T[None], gstate.T[None], down.T, gate, gain1, gq, gk, gv, go, rel.T, gain2, g1, g2.T,
    )


def solution(mesh):
    rows = P(("dp", "side"), None, None)
    return jax.shard_map(
        shards,
        mesh=mesh,
        in_specs=(rows, rows, P("dp"), P("dp")) + (P(),) * 21 + (rows,),
        out_specs=(rows, rows) + (P(),) * 11,
        check_vma=False,
    )
```

time: 1010 us -> 118 us (0.12); the launches traced: 994 us -> 118 us
  local copies, waits for them, and re-layouts: 421 us -> 3.38 us
  waiting for transfers between devices: 397 us -> 36.9 us
  matrix products: 97.9 us -> 0 us
  Pallas kernels: 0 us -> 54.8 us
  other arithmetic: 51.7 us -> 1.24 us
  between operations: 15 us -> 1.09 us
    psum x2 -> x0, waiting for transfers between devices: 392 us -> none  [shards(): lax.psum((grad_down, grad_gate, grad_gain_attn, grad_query, grad_key, gra...]
    unnamed x89 -> x30, local copies, waits for them, and re-layouts: 191 us -> 2.1 us
    reshape x5 -> x0, local copies, waits for them, and re-layouts: 119 us -> none  [the longest x2 83.2 us: skew_rows(): tiled[:, L - 1:L - 1 + L * (2 * L - 1)].reshape(head_count, L, 2 * L - 1)]
    dot_general x38 -> x0, matrix products: 97.9 us -> none  [the longest x12 36.7 us: project(): return jnp.dot(rows, weight, preferred_element_type=jnp.float32)]
    slice x7 -> x0, local copies, waits for them, and re-layouts: 73 us -> none  [the longest x2 51 us: skew_rows(): tiled[:, L - 1:L - 1 + L * (2 * L - 1)].reshape(head_count, L, 2 * L - 1)]
    pallas_call x0 -> x3, Pallas kernels: none -> 54.8 us  [the longest x1 30.2 us: side_block(): pl.pallas_call(functools.partial(side_kernel, count), out_shape=(jax.Shap...]
    ppermute x0 -> x15, waiting for transfers between devices: none -> 36.9 us  [the longest x6 23.6 us: swap(): return lax.ppermute(value, axis, [(i, i ^ bit) for i in range(size)])]
    broadcast_in_dim x2 -> x0, local copies, waits for them, and re-layouts: 23 us -> none  [skew_rows(): jnp.broadcast_to(padded[:, None, :], (head_count, L, 2 * L))]
  transfers between devices with their start and end apart: 4 -> 15, of which waited for: 3 -> 7; matrix products, arithmetic and copies ran while one was open for 17% -> 1% of each run, Pallas kernels for 0% -> 19%
where the time goes in v1:
time: 118 us
  Pallas kernels  54.8 us (46%)
  waiting for transfers between devices  36.9 us (31%)
  starting transfers between devices  20.4 us (17%)
  local copies, waits for them, and re-layouts  3.38 us (3%)
  other arithmetic  1.24 us (1%)
    pallas_call x1, Pallas kernels, side_block(): pl.pallas_call(functools.partial(side_kernel, count), out_shape=(jax.Shap...  30.2 us
    ppermute x6, waiting for transfers between devices, swap(): return lax.ppermute(value, axis, [(i, i ^ bit) for i in range(size)])  23.6 us
    pallas_call x1, Pallas kernels, backbone(): pl.pallas_call(backbone_kernel, out_shape=(jax.ShapeDtypeStruct((L, D), B...  22 us
    ppermute x9, waiting for transfers between devices, rotations(): lax.ppermute(value, 'side', [(i, (i + k) % size) for i in range(size)])  13.2 us
    ppermute x9, starting transfers between devices, rotations(): lax.ppermute(value, 'side', [(i, (i + k) % size) for i in range(size)])  13.2 us
    ppermute x6, starting transfers between devices, swap(): return lax.ppermute(value, axis, [(i, i ^ bit) for i in range(size)])  7.2 us
    pallas_call x1, Pallas kernels, finish(): pl.pallas_call(functools.partial(finish_kernel, count), out_shape=(jax.Sh...  2.6 us
  transfers between devices with their start and end apart: 15, of which 7 were waited for; matrix products, arithmetic and copies ran while one was open for 1% of the time, Pallas kernels for 19%

profile of v1, /device:TPU:0, one launch (start us, length us, event | category | flops | bytes accessed | tf_op | source)
XLA Modules:
  0.0 117.8 jit_solution(7348540199129828841)
XLA Ops:
  0.6 1.0 pad_maximum_fusion.rest_0_
  1.6 5.1 %collective-permute-start.2 = (bf16[2,96,512]{2,1,0:T(8,128)(2,1)S(1)}, bf16[2,96,512]{2,1,0:T(8,128)(2,1)S(1)}, u32[]{:S(2)}, u32[]{:S(2)}) collective-permute-start(bf16[2,96,512]{2,1,0:T(8,128)(2,1)S(1)} %pad_maximum_fusion.rest_0_), channel_id=1, source_target_pairs={{0,3},{1,0},{2,1},{3,2},{4,7},{5,4},{6,5},{7,6},{8,11},{9,8},{10,9... | collective-permute-start | bytes 589832 | tf_op jit(solution)/shard_map/ppermute | solution.py:575
  6.7 1.0 collective-permute-start
  7.7 1.3 %pad.4.bucket_hbm.rest_4_ = s32[1024]{0:T(1024)} pad(s32[1023]{0:T(1024)} %param.30, s32[]{:T(128)} %constant.0.clone.1), padding=0_1 | pad | bytes 8192 | tf_op jit(solution)/shard_map/jit(_pad)/pad | solution.py:602
  9.1 22.0 %backbone.1 = (bf16[512,768]{1,0:T(8,128)(2,1)}, bf16[512,96]{1,0:T(8,128)(2,1)}) custom-call(s32[4]{0:T(128)} %lengths_ref.3, s32[4]{0:T(128)} %assign_ref.5, f32[12,32]{1,0:T(8,128)} %bitcast.34, s32[1024]{0:T(1024)} %pad.4.bucket_hbm.rest_4_, bf16[512,768]{1,0:T(8,128)(2,1)} %bitcast.28, f32[768]{0:T(1024)} %gain1_hbm.1, bf16[768,768]{1,0:T(8,128)(2,1)} %wq_hbm.1, ...), custom_call_target="tpu_custom_call" | custom-call | flops 8999999488 | bytes 17000000 | tf_op jit(solution)/shard_map/backbone/pallas_call | solution.py:189
  31.3 1.1 copy-done.13
  32.4 0.9 copy-done.14
  33.3 30.2 %side_block.1 = (bf16[96,512]{1,0:T(8,128)(2,1)S(1)}, bf16[96,512]{1,0:T(8,128)(2,1)S(1)}, bf16[784,128]{1,0:T(8,128)(2,1)S(1)}, bf16[784,128]{1,0:T(8,128)(2,1)S(1)}) custom-call(s32[4]{0:T(128)S(1)} %copy-done.9, s32[4]{0:T(128)S(1)} %copy-done.1, bf16[512,96]{1,0:T(8,128)(2,1)S(1)} %copy-done.14, bf16[2,96,512]{2,1,0:T(8,128)(2,1)S(1)} %pad_maximum_fusion.rest_0_, ...), custom_call_target="tpu_custom_call" | custom-call | flops 8999999488 | bytes 4000000 | tf_op jit(solution)/shard_map/side_block/pallas_call | solution.py:435
  63.6 1.4 %collective-permute-done.3 = bf16[784,128]{1,0:T(8,128)(2,1)S(1)} collective-permute-done((bf16[784,128]{1,0:T(8,128)(2,1)S(1)}, bf16[784,128]{1,0:T(8,128)(2,1)S(1)}, u32[]{:S(2)}, u32[]{:S(2)}) %collective-permute-start.3) | collective-permute-done | bytes 200736 | tf_op jit(solution)/shard_map/ppermute | solution.py:569
  65.1 1.6 %collective-permute-start.4 = (bf16[784,128]{1,0:T(8,128)(2,1)S(1)}, bf16[784,128]{1,0:T(8,128)(2,1)S(1)}, u32[]{:S(2)}, u32[]{:S(2)}) collective-permute-start(bf16[784,128]{1,0:T(8,128)(2,1)S(1)} %add_convert_fusion.4), channel_id=1, source_target_pairs={{0,8},{4,12},{8,0},{12,4},{16,24},{20,28},{24,16},{28,20},{1,9},{5... | collective-permute-start | bytes 602120 | tf_op jit(solution)/shard_map/ppermute | solution.py:569
  66.6 5.5 %collective-permute-done.4 = bf16[784,128]{1,0:T(8,128)(2,1)S(1)} collective-permute-done((bf16[784,128]{1,0:T(8,128)(2,1)S(1)}, bf16[784,128]{1,0:T(8,128)(2,1)S(1)}, u32[]{:S(2)}, u32[]{:S(2)}) %collective-permute-start.4) | collective-permute-done | bytes 200736 | tf_op jit(solution)/shard_map/ppermute | solution.py:569
  72.2 1.5 %collective-permute-start.5 = (bf16[784,128]{1,0:T(8,128)(2,1)S(1)}, bf16[784,128]{1,0:T(8,128)(2,1)S(1)}, u32[]{:S(2)}, u32[]{:S(2)}) collective-permute-start(bf16[784,128]{1,0:T(8,128)(2,1)S(1)} %add_convert_fusion.3), channel_id=1, source_target_pairs={{0,16},{4,20},{8,24},{12,28},{16,0},{20,4},{24,8},{28,12},{1,17},{... | collective-permute-start | bytes 602120 | tf_op jit(solution)/shard_map/ppermute | solution.py:569
  73.8 4.7 %collective-permute-done.5 = bf16[784,128]{1,0:T(8,128)(2,1)S(1)} collective-permute-done((bf16[784,128]{1,0:T(8,128)(2,1)S(1)}, bf16[784,128]{1,0:T(8,128)(2,1)S(1)}, u32[]{:S(2)}, u32[]{:S(2)}) %collective-permute-start.5) | collective-permute-done | bytes 200736 | tf_op jit(solution)/shard_map/ppermute | solution.py:569
  78.6 2.5 %collective-permute-start.6 = (bf16[784,128]{1,0:T(8,128)(2,1)S(1)}, bf16[784,128]{1,0:T(8,128)(2,1)S(1)}, u32[]{:S(2)}, u32[]{:S(2)}) collective-permute-start(bf16[784,128]{1,0:T(8,128)(2,1)S(1)} %add_convert_fusion.2), channel_id=1, source_target_pairs={{0,1},{1,0},{2,3},{3,2},{4,5},{5,4},{6,7},{7,6},{8,9},{9,8},{10,11... | collective-permute-start | bytes 602120 | tf_op jit(solution)/shard_map/ppermute | solution.py:569
  81.1 3.8 %collective-permute-done.6 = bf16[784,128]{1,0:T(8,128)(2,1)S(1)} collective-permute-done((bf16[784,128]{1,0:T(8,128)(2,1)S(1)}, bf16[784,128]{1,0:T(8,128)(2,1)S(1)}, u32[]{:S(2)}, u32[]{:S(2)}) %collective-permute-start.6) | collective-permute-done | bytes 200736 | tf_op jit(solution)/shard_map/ppermute | solution.py:569
  84.9 1.4 %collective-permute-start.7 = (bf16[784,128]{1,0:T(8,128)(2,1)S(1)}, bf16[784,128]{1,0:T(8,128)(2,1)S(1)}, u32[]{:S(2)}, u32[]{:S(2)}) collective-permute-start(bf16[784,128]{1,0:T(8,128)(2,1)S(1)} %add_convert_fusion.1), channel_id=1, source_target_pairs={{0,2},{1,3},{2,0},{3,1},{4,6},{5,7},{6,4},{7,5},{8,10},{9,11},{10,... | collective-permute-start | bytes 602120 | tf_op jit(solution)/shard_map/ppermute | solution.py:569
  86.3 8.2 %collective-permute-done.7 = bf16[784,128]{1,0:T(8,128)(2,1)S(1)} collective-permute-done((bf16[784,128]{1,0:T(8,128)(2,1)S(1)}, bf16[784,128]{1,0:T(8,128)(2,1)S(1)}, u32[]{:S(2)}, u32[]{:S(2)}) %collective-permute-start.7) | collective-permute-done | bytes 200736 | tf_op jit(solution)/shard_map/ppermute | solution.py:569
  94.6 2.2 %collective-permute-start.11 = (bf16[96,512]{1,0:T(8,128)(2,1)S(1)}, bf16[96,512]{1,0:T(8,128)(2,1)S(1)}, u32[]{:S(2)}, u32[]{:S(2)}) collective-permute-start(bf16[96,512]{1,0:T(8,128)(2,1)S(1)} %get-tuple-element.36.rest_0_), channel_id=1, source_target_pairs={{0,3},{1,0},{2,1},{3,2},{4,7},{5,4},{6,5},{7,6},{8,11},{9,8},{10,9... | collective-permute-start | bytes 294920 | tf_op jit(solution)/shard_map/ppermute | solution.py:575
  96.8 0.7 collective-permute-start.9
  97.5 3.2 %collective-permute-start.14 = (bf16[96,512]{1,0:T(8,128)(2,1)S(1)}, bf16[96,512]{1,0:T(8,128)(2,1)S(1)}, u32[]{:S(2)}, u32[]{:S(2)}) collective-permute-start(bf16[96,512]{1,0:T(8,128)(2,1)S(1)} %get-tuple-element.37.rest_4_), channel_id=1, source_target_pairs={{0,3},{1,0},{2,1},{3,2},{4,7},{5,4},{6,5},{7,6},{8,11},{9,8},{10,9... | collective-permute-start | bytes 294920 | tf_op jit(solution)/shard_map/ppermute | solution.py:575
  100.6 1.1 collective-permute-start.13
  101.8 5.4 %collective-permute-done.10.rest_2_ = bf16[96,512]{1,0:T(8,128)(2,1)S(1)} collective-permute-done((bf16[96,512]{1,0:T(8,128)(2,1)S(1)}, bf16[96,512]{1,0:T(8,128)(2,1)S(1)}, u32[]{:S(2)}, u32[]{:S(2)}) %collective-permute-start.10) | collective-permute-done | bytes 98336 | tf_op jit(solution)/shard_map/ppermute | solution.py:575
  107.1 7.9 %collective-permute-done.13.rest_6_ = bf16[96,512]{1,0:T(8,128)(2,1)S(1)} collective-permute-done((bf16[96,512]{1,0:T(8,128)(2,1)S(1)}, bf16[96,512]{1,0:T(8,128)(2,1)S(1)}, u32[]{:S(2)}, u32[]{:S(2)}) %collective-permute-start.13) | collective-permute-done | bytes 98336 | tf_op jit(solution)/shard_map/ppermute | solution.py:575
  115.0 2.6 %finish.1 = (bf16[96,512]{1,0:T(8,128)(2,1)}, f32[96,512]{1,0:T(8,128)}, f32[96,768]{1,0:T(8,128)}, f32[96]{0:T(128)}, f32[96]{0:T(128)}, /*index=5*/f32[96,96]{...) custom-call(s32[4]{0:T(128)S(1)} %copy-done.1, ...), custom_call_target="tpu_custom_call" | custom-call | tf_op jit(solution)/shard_map/finish/pallas_call | solution.py:550
  (46 shorter events, 0.5 us)
Async XLA Ops:
  1.6 29.5 %collective-permute-start.2 = (bf16[2,96,512]{2,1,0:T(8,128)(2,1)S(1)}, bf16[2,96,512]{2,1,0:T(8,128)(2,1)S(1)}, u32[]{:S(2)}, u32[]{:S(2)}) collective-permute-start(bf16[2,96,512]{2,1,0:T(8,128)(2,1)S(1)} %pad_maximum_fusion.rest_0_), channel_id=1, source_target_pairs={{0,3},{1,0},{2,1},{3,2},{4,7},{5,4},{6,5},{7,6},{8,11},{9,8},{10,9... | collective-permute-start | bytes 589832 | tf_op jit(solution)/shard_map/ppermute | solution.py:575
  6.7 24.4 %collective-permute-start.1 = (bf16[2,96,512]{2,1,0:T(8,128)(2,1)S(1)}, bf16[2,96,512]{2,1,0:T(8,128)(2,1)S(1)}, u32[]{:S(2)}, u32[]{:S(2)}) collective-permute-start(bf16[2,96,512]{2,1,0:T(8,128)(2,1)S(1)} %pad_maximum_fusion.rest_0_), channel_id=1, source_target_pairs={{0,2},{1,3},{2,0},{3,1},{4,6},{5,7},{6,4},{7,5},{8,10},{9,11},{10,... | collective-permute-start | bytes 589832 | tf_op jit(solution)/shard_map/ppermute | solution.py:575
  6.7 24.4 %collective-permute-start = (bf16[2,96,512]{2,1,0:T(8,128)(2,1)S(1)}, bf16[2,96,512]{2,1,0:T(8,128)(2,1)S(1)}, u32[]{:S(2)}, u32[]{:S(2)}) collective-permute-start(bf16[2,96,512]{2,1,0:T(8,128)(2,1)S(1)} %pad_maximum_fusion.rest_0_), channel_id=1, source_target_pairs={{0,1},{1,2},{2,3},{3,0},{4,5},{5,6},{6,7},{7,4},{8,9},{9,10},{10,1... | collective-permute-start | bytes 589832 | tf_op jit(solution)/shard_map/ppermute | solution.py:575
  9.0 22.2 %copy-start.2 = (bf16[96,384]{1,0:T(8,128)(2,1)S(1)}, bf16[96,384]{1,0:T(8,128)(2,1)}, u32[]{:S(2)}) copy-start(bf16[96,384]{1,0:T(8,128)(2,1)} %rest_13_.1) | copy-start | bytes 221188
  9.0 22.2 %copy-start.3 = (bf16[384,96]{0,1:T(8,128)(2,1)S(1)}, bf16[384,96]{0,1:T(8,128)(2,1)}, u32[]{:S(2)}) copy-start(bf16[384,96]{0,1:T(8,128)(2,1)} %param.50) | copy-start | bytes 221188
  9.0 22.2 %copy-start.4 = (bf16[96,96]{1,0:T(8,128)(2,1)S(1)}, bf16[96,96]{1,0:T(8,128)(2,1)}, u32[]{:S(2)}) copy-start(bf16[96,96]{1,0:T(8,128)(2,1)} %rest_9_.1) | copy-start | bytes 55300
  9.0 22.2 %copy-start.5 = (bf16[96,96]{1,0:T(8,128)(2,1)S(1)}, bf16[96,96]{1,0:T(8,128)(2,1)}, u32[]{:S(2)}) copy-start(bf16[96,96]{1,0:T(8,128)(2,1)} %rest_10_.1) | copy-start | bytes 55300
  9.0 22.2 %copy-start.6 = (bf16[96,96]{1,0:T(8,128)(2,1)S(1)}, bf16[96,96]{1,0:T(8,128)(2,1)}, u32[]{:S(2)}) copy-start(bf16[96,96]{1,0:T(8,128)(2,1)} %rest_11_.1) | copy-start | bytes 55300
  9.1 22.2 %copy-start.7 = (bf16[96,96]{1,0:T(8,128)(2,1)S(1)}, bf16[96,96]{1,0:T(8,128)(2,1)}, u32[]{:S(2)}) copy-start(bf16[96,96]{1,0:T(8,128)(2,1)} %rest_12_.1) | copy-start | bytes 55300
  9.1 22.2 %copy-start.8 = (f32[32,12]{0,1:T(8,128)S(1)}, f32[32,12]{0,1:T(8,128)}, u32[]{:S(2)}) copy-start(f32[32,12]{0,1:T(8,128)} %param.47) | copy-start | bytes 4612
  9.1 22.2 %copy-start.9 = (s32[4]{0:T(128)S(1)}, s32[4]{0:T(128)}, u32[]{:S(2)}) copy-start(s32[4]{0:T(128)} %lengths_ref.3) | copy-start | bytes 52
  9.1 22.2 %copy-start.10 = (f32[96]{0:T(128)S(1)}, f32[96]{0:T(128)}, u32[]{:S(2)}) copy-start(f32[96]{0:T(128)} %rest_6_.1) | copy-start | bytes 1156
  63.5 1.5 %collective-permute-start.3 = (bf16[784,128]{1,0:T(8,128)(2,1)S(1)}, bf16[784,128]{1,0:T(8,128)(2,1)S(1)}, u32[]{:S(2)}, u32[]{:S(2)}) collective-permute-start(bf16[784,128]{1,0:T(8,128)(2,1)S(1)} %get-tuple-element.35), channel_id=1, source_target_pairs={{0,4},{4,0},{8,12},{12,8},{16,20},{20,16},{24,28},{28,24},{1,5},{5... | collective-permute-start | bytes 602120 | tf_op jit(solution)/shard_map/ppermute | solution.py:569
  65.1 7.1 %collective-permute-start.4 = (bf16[784,128]{1,0:T(8,128)(2,1)S(1)}, bf16[784,128]{1,0:T(8,128)(2,1)S(1)}, u32[]{:S(2)}, u32[]{:S(2)}) collective-permute-start(bf16[784,128]{1,0:T(8,128)(2,1)S(1)} %add_convert_fusion.4), channel_id=1, source_target_pairs={{0,8},{4,12},{8,0},{12,4},{16,24},{20,28},{24,16},{28,20},{1,9},{5... | collective-permute-start | bytes 602120 | tf_op jit(solution)/shard_map/ppermute | solution.py:569
  72.2 6.3 %collective-permute-start.5 = (bf16[784,128]{1,0:T(8,128)(2,1)S(1)}, bf16[784,128]{1,0:T(8,128)(2,1)S(1)}, u32[]{:S(2)}, u32[]{:S(2)}) collective-permute-start(bf16[784,128]{1,0:T(8,128)(2,1)S(1)} %add_convert_fusion.3), channel_id=1, source_target_pairs={{0,16},{4,20},{8,24},{12,28},{16,0},{20,4},{24,8},{28,12},{1,17},{... | collective-permute-start | bytes 602120 | tf_op jit(solution)/shard_map/ppermute | solution.py:569
  78.6 6.3 %collective-permute-start.6 = (bf16[784,128]{1,0:T(8,128)(2,1)S(1)}, bf16[784,128]{1,0:T(8,128)(2,1)S(1)}, u32[]{:S(2)}, u32[]{:S(2)}) collective-permute-start(bf16[784,128]{1,0:T(8,128)(2,1)S(1)} %add_convert_fusion.2), channel_id=1, source_target_pairs={{0,1},{1,0},{2,3},{3,2},{4,5},{5,4},{6,7},{7,6},{8,9},{9,8},{10,11... | collective-permute-start | bytes 602120 | tf_op jit(solution)/shard_map/ppermute | solution.py:569
  84.9 9.6 %collective-permute-start.7 = (bf16[784,128]{1,0:T(8,128)(2,1)S(1)}, bf16[784,128]{1,0:T(8,128)(2,1)S(1)}, u32[]{:S(2)}, u32[]{:S(2)}) collective-permute-start(bf16[784,128]{1,0:T(8,128)(2,1)S(1)} %add_convert_fusion.1), channel_id=1, source_target_pairs={{0,2},{1,3},{2,0},{3,1},{4,6},{5,7},{6,4},{7,5},{8,10},{9,11},{10,... | collective-permute-start | bytes 602120 | tf_op jit(solution)/shard_map/ppermute | solution.py:569
  94.6 20.4 %collective-permute-start.8 = (bf16[784,128]{1,0:T(8,128)(2,1)S(1)}, bf16[784,128]{1,0:T(8,128)(2,1)S(1)}, u32[]{:S(2)}, u32[]{:S(2)}) collective-permute-start(bf16[784,128]{1,0:T(8,128)(2,1)S(1)} %add_convert_fusion.mine_hbm), channel_id=1, source_target_pairs={{0,4},{4,0},{8,12},{12,8},{16,20},{20,16},{24,28},{28,24},{1,5},{5... | collective-permute-start | bytes 602120 | tf_op jit(solution)/shard_map/ppermute | solution.py:569
  94.6 6.0 %collective-permute-start.11 = (bf16[96,512]{1,0:T(8,128)(2,1)S(1)}, bf16[96,512]{1,0:T(8,128)(2,1)S(1)}, u32[]{:S(2)}, u32[]{:S(2)}) collective-permute-start(bf16[96,512]{1,0:T(8,128)(2,1)S(1)} %get-tuple-element.36.rest_0_), channel_id=1, source_target_pairs={{0,3},{1,0},{2,1},{3,2},{4,7},{5,4},{6,5},{7,6},{8,11},{9,8},{10,9... | collective-permute-start | bytes 294920 | tf_op jit(solution)/shard_map/ppermute | solution.py:575
  96.8 10.3 %collective-permute-start.10 = (bf16[96,512]{1,0:T(8,128)(2,1)S(1)}, bf16[96,512]{1,0:T(8,128)(2,1)S(1)}, u32[]{:S(2)}, u32[]{:S(2)}) collective-permute-start(bf16[96,512]{1,0:T(8,128)(2,1)S(1)} %get-tuple-element.36.rest_0_), channel_id=1, source_target_pairs={{0,2},{1,3},{2,0},{3,1},{4,6},{5,7},{6,4},{7,5},{8,10},{9,11},{10,... | collective-permute-start | bytes 294920 | tf_op jit(solution)/shard_map/ppermute | solution.py:575
  96.8 10.3 %collective-permute-start.9 = (bf16[96,512]{1,0:T(8,128)(2,1)S(1)}, bf16[96,512]{1,0:T(8,128)(2,1)S(1)}, u32[]{:S(2)}, u32[]{:S(2)}) collective-permute-start(bf16[96,512]{1,0:T(8,128)(2,1)S(1)} %get-tuple-element.36.rest_0_), channel_id=1, source_target_pairs={{0,1},{1,2},{2,3},{3,0},{4,5},{5,6},{6,7},{7,4},{8,9},{9,10},{10,1... | collective-permute-start | bytes 294920 | tf_op jit(solution)/shard_map/ppermute | solution.py:575
  97.5 9.7 %collective-permute-start.14 = (bf16[96,512]{1,0:T(8,128)(2,1)S(1)}, bf16[96,512]{1,0:T(8,128)(2,1)S(1)}, u32[]{:S(2)}, u32[]{:S(2)}) collective-permute-start(bf16[96,512]{1,0:T(8,128)(2,1)S(1)} %get-tuple-element.37.rest_4_), channel_id=1, source_target_pairs={{0,3},{1,0},{2,1},{3,2},{4,7},{5,4},{6,5},{7,6},{8,11},{9,8},{10,9... | collective-permute-start | bytes 294920 | tf_op jit(solution)/shard_map/ppermute | solution.py:575
  100.6 14.4 %collective-permute-start.13 = (bf16[96,512]{1,0:T(8,128)(2,1)S(1)}, bf16[96,512]{1,0:T(8,128)(2,1)S(1)}, u32[]{:S(2)}, u32[]{:S(2)}) collective-permute-start(bf16[96,512]{1,0:T(8,128)(2,1)S(1)} %get-tuple-element.37.rest_4_), channel_id=1, source_target_pairs={{0,2},{1,3},{2,0},{3,1},{4,6},{5,7},{6,4},{7,5},{8,10},{9,11},{10,... | collective-permute-start | bytes 294920 | tf_op jit(solution)/shard_map/ppermute | solution.py:575
  107.1 7.9 %collective-permute-start.12 = (bf16[96,512]{1,0:T(8,128)(2,1)S(1)}, bf16[96,512]{1,0:T(8,128)(2,1)S(1)}, u32[]{:S(2)}, u32[]{:S(2)}) collective-permute-start(bf16[96,512]{1,0:T(8,128)(2,1)S(1)} %get-tuple-element.37.rest_4_), channel_id=1, source_target_pairs={{0,1},{1,2},{2,3},{3,0},{4,5},{5,6},{6,7},{7,4},{8,9},{9,10},{10,1... | collective-permute-start | bytes 294920 | tf_op jit(solution)/shard_map/ppermute | solution.py:575
  (6 other events, 90.7 us)

commit v2 on v1

v2 whole, which is shorter than its diff:
```python
import functools
import math

import jax
import jax.numpy as jnp
from jax import lax
from jax.experimental import pallas as pl
from jax.experimental.pallas import tpu as pltpu
from jax.sharding import PartitionSpec as P

D = 768
H = 12
HD = 64
FF = 3072
NB = 32
DS = 96
SH = 12
SHD = 8
FS = 384
L = 512
W = 128
OFFSETS = 2 * L - 1
TILE = 128

EPS = 1e-06
MASKED = -1e9
LIMIT = 60.0
F32 = jnp.float32
BF16 = jnp.bfloat16
VMEM_BYTES = 44 * 1024 * 1024
UNROLL = 6
UNROLL_BACK = 6
PAIRS = 6


def dot(a, b, dims=((1,), (0,)), precision=None):
    return lax.dot_general(
        a, b, (dims, ((), ())), precision=precision, preferred_element_type=F32
    )


def dot_nt(a, b):
    return dot(a, b, ((1,), (1,)))


def dot_tn(a, b):
    return dot(a, b, ((0,), (0,)))


def normal_cdf(v):
    return 0.5 * (1.0 + lax.erf(v * (1.0 / math.sqrt(2.0))))


def offset_table(buckets, rel):
    rows = lax.broadcasted_iota(jnp.int32, (NB, OFFSETS), 0)
    onehot = (rows == buckets).astype(F32)
    table = dot(rel, onehot, precision=lax.Precision.HIGHEST)
    return jnp.concatenate([table, jnp.zeros((rel.shape[0], 1), F32)], axis=1)


def toeplitz(row):
    wide = jnp.broadcast_to(row, (TILE, 2 * L))
    return pltpu.roll(wide, 2 * L - (TILE - 1), 1, stride=1, stride_axis=0)


def bounded(q, k, table, size, heads):
    rows = lax.broadcasted_iota(jnp.int32, (q.shape[1], W), 0) // size
    cols = lax.broadcasted_iota(jnp.int32, (q.shape[1], W), 1)
    pick = ((rows == cols) & (rows < heads)).astype(BF16)
    qf, kf = q.astype(F32), k.astype(F32)
    qn = jnp.max(dot((qf * qf).astype(BF16), pick), axis=0, keepdims=True)
    kn = jnp.max(dot((kf * kf).astype(BF16), pick), axis=0, keepdims=True)
    top = jnp.max(jnp.sqrt(qn) * jnp.sqrt(kn)) * 1.02
    return top + jnp.max(jnp.abs(table)) < LIMIT


def start_all(pairs, sems):
    copies = [pltpu.make_async_copy(src, dst, sems.at[n]) for n, (src, dst) in enumerate(pairs)]
    for copy in copies:
        copy.start()
    return copies


def backbone_kernel(
    lengths_ref, assign_ref, rel_hbm, bucket_hbm, x_hbm, gain1_hbm, wq_hbm, wk_hbm, wv_hbm, wo_hbm, gain2_hbm, w1_hbm,
    w2_hbm, wd_hbm,
    hidden_ref, taps_ref,
    rel, buckets, x_ref, gain1_ref, wq, wk, wv, wo, gain2_ref, w1, w2, wd, sems,
    normed, q_s, k_s, vx, ctx, table, stream, inner,
):
    pairs = (
        (x_hbm, x_ref), (gain1_hbm, gain1_ref.at[0]), (rel_hbm, rel), (bucket_hbm, buckets.at[0]),
        (wq_hbm, wq), (wk_hbm, wk), (wv_hbm, wv), (wo_hbm, wo), (gain2_hbm, gain2_ref.at[0]),
        (w1_hbm, w1), (w2_hbm, w2), (wd_hbm, wd),
    )
    copies = [pltpu.make_async_copy(src, dst, sems.at[n]) for n, (src, dst) in enumerate(pairs)]
    for n in (0, 1, 4):
        copies[n].start()
    length = lengths_ref[assign_ref[lax.axis_index("side")]]
    copies[0].wait()
    copies[1].wait()
    for n in (5, 6, 2, 3):
        copies[n].start()
    x = x_ref[...].astype(F32)
    scale = lax.rsqrt(jnp.mean(x * x, axis=1, keepdims=True) + EPS)
    normed[...] = (x * scale * gain1_ref[...]).astype(BF16)
    copies[4].wait()
    copies[7].start()
    q_s[...] = dot(normed[...], wq[...]).astype(BF16)
    copies[5].wait()
    k_s[...] = dot(normed[...], wk[...]).astype(BF16)
    copies[6].wait()
    for n in (8, 9, 10, 11):
        copies[n].start()
    live_row = lax.broadcasted_iota(jnp.int32, (L, 1), 0) < length
    value = dot(normed[...], wv[...])
    value = jnp.where(live_row, value, 0.0).astype(BF16)
    ones = jnp.where(live_row, 1.0, 0.0).astype(BF16)
    for pair in range(H // 2):
        vx[pair, :, :W] = value[:, pair * W : (pair + 1) * W]
        vx[pair, :, W:] = jnp.broadcast_to(ones, (L, W))
    low_half = lax.broadcasted_iota(jnp.int32, (L, W), 1) < HD
    low_row = lax.broadcasted_iota(jnp.int32, (TILE, W), 1) < HD
    live = lax.broadcasted_iota(jnp.int32, (1, L), 1) < length

    def attend(pair, stable):
        lanes = pl.ds(pl.multiple_of(pair * W, W), W)
        keys = k_s[:, lanes]
        tiles = [toeplitz(table[pl.ds(pair * 2 + half, 1)]) for half in range(2)]
        for block in range(L // TILE):
            rows = slice(block * TILE, (block + 1) * TILE)
            start = (L // TILE - 1 - block) * TILE
            query = q_s[rows, lanes]
            results = []
            for half in range(2):
                mine = low_row if half == 0 else jnp.logical_not(low_row)
                scores = dot_nt(jnp.where(mine, query, jnp.zeros_like(query)), keys)
                scores = scores + tiles[half][:, start : start + L]
                if stable:
                    scores = jnp.where(live, scores, MASKED)
                    scores = scores - jnp.max(scores, axis=1, keepdims=True)
                results.append(dot(jnp.exp(scores).astype(BF16), vx[pair]))
            top = jnp.where(low_row, results[0][:, :W], results[1][:, :W])
            total = jnp.where(low_row, results[0][:, W:], results[1][:, W:])
            ctx[rows, lanes] = (top / total).astype(BF16)

    copies[2].wait()
    copies[3].wait()
    table[...] = jnp.zeros_like(table)
    table[:H] = offset_table(buckets[...], rel[...])
    safe = bounded(q_s[...], k_s[...], table[...], HD, H)

    @pl.when(safe)
    def _():
        @pl.loop(0, H // 2, step=PAIRS)
        def _(first):
            for n in range(PAIRS):
                attend(first + n, False)

    @pl.when(jnp.logical_not(safe))
    def _():
        @pl.loop(0, H // 2)
        def _(pair):
            attend(pair, True)

    copies[7].wait()
    copies[8].wait()
    flow = x_ref[...].astype(F32) + dot(ctx[...], wo[...])
    stream[...] = flow
    scale = lax.rsqrt(jnp.mean(flow * flow, axis=1, keepdims=True) + EPS)
    normed[...] = (flow * scale * gain2_ref[...]).astype(BF16)
    copies[9].wait()
    copies[10].wait()
    for r in range(L // 256):
        part = slice(r * 256, (r + 1) * 256)
        for n in range(FF // 3072):
            cols = slice(n * 3072, (n + 1) * 3072)
            pre = dot(normed[part], w1[:, cols])
            inner[part, cols] = (pre * normal_cdf(pre)).astype(BF16)
        hidden_ref[part] = (stream[part] + dot(inner[part], w2[...])).astype(BF16)
    copies[11].wait()
    taps_ref[...] = dot_nt(wd[...], hidden_ref[...]).astype(BF16)


def backbone(*args):
    smem = pl.BlockSpec(memory_space=pltpu.SMEM)
    vmem = pl.BlockSpec(memory_space=pltpu.VMEM)
    hbm = pl.BlockSpec(memory_space=pl.ANY)
    fixed = pl.BlockSpec(memory_space=pltpu.HBM)
    return pl.pallas_call(
        backbone_kernel,
        out_shape=(
            jax.ShapeDtypeStruct((L, D), BF16),
            jax.ShapeDtypeStruct((DS, L), BF16),
        ),
        in_specs=[smem, smem] + [fixed] * 12,
        out_specs=(vmem, vmem),
        scratch_shapes=[
            pltpu.VMEM((H, NB), F32),
            pltpu.VMEM((1, OFFSETS), jnp.int32),
            pltpu.VMEM((L, D), BF16),
            pltpu.VMEM((1, D), F32),
            pltpu.VMEM((D, D), BF16),
            pltpu.VMEM((D, D), BF16),
            pltpu.VMEM((D, D), BF16),
            pltpu.VMEM((D, D), BF16),
            pltpu.VMEM((1, D), F32),
            pltpu.VMEM((D, FF), BF16),
            pltpu.VMEM((FF, D), BF16),
            pltpu.VMEM((DS, D), BF16),
            pltpu.SemaphoreType.DMA((12,)),
            pltpu.VMEM((L, D), BF16),
            pltpu.VMEM((L, D), BF16),
            pltpu.VMEM((L, D), BF16),
            pltpu.VMEM((H // 2, L, 2 * W), BF16),
            pltpu.VMEM((L, D), BF16),
            pltpu.VMEM((16, 2 * L), F32),
            pltpu.VMEM((L, D), F32),
            pltpu.VMEM((L, FF), BF16),
        ],
        compiler_params=pltpu.CompilerParams(vmem_limit_bytes=60 * 1024 * 1024),
        cost_estimate=pl.CostEstimate(
            flops=9_000_000_000, bytes_accessed=17_000_000, transcendentals=5_000_000
        ),
        name="backbone",
    )(*args)


DOWN0, QKV0, PROJ0, FFIN0, FFOUT0 = 0, 576, 864, 960, 1248
PACK = 1536
PART = PACK // 4


def place():
    index = lax.axis_index("dp")
    return lax.rem(index, 2), lax.rem(lax.div(index, 2), 2)


def column_norm(rows):
    return lax.rsqrt(jnp.mean(rows * rows, axis=0, keepdims=True) + EPS)


def norm_back(grad, unit, scale):
    return scale * (grad - unit * jnp.mean(grad * unit, axis=0, keepdims=True))


def head_sums(rows):
    return jnp.sum(rows.reshape(SH, SHD, L), axis=1)


def fill_heads(ref, rows, extra):
    for head in range(SH):
        mine = rows[head * SHD : (head + 1) * SHD]
        other = extra[head] if isinstance(extra, list) else extra
        ref[head] = jnp.concatenate([mine, other], axis=0).astype(BF16)


def side_kernel(count, lengths_ref, assign_ref, *rest):
    moved_hbm, rest = rest[:count], rest[count:]
    (
        taps_hbm, gate_hbm, gain1_hbm, gain2_hbm, wq_hbm, wk_hbm, wv_hbm, bucket_hbm, rel_hbm, wo_hbm, w1_hbm, w2_hbm,
        back_ref, tap_ref, rest_ref,
        taps, vectors, wq, wk, wv, buckets, rel, wo, w1, w2,
        moved, sems, table, probs, qt, kt, vt, dt, ctx, sums, dq, dk, dv, dall, diag, dtab,
    ) = rest
    rank = lax.axis_index("side")
    seq = assign_ref[rank]
    for step in range(count):

        @pl.when(lax.rem(rank + count - seq, count) == step)
        def _():
            pltpu.make_async_copy(moved_hbm[step], moved, sems.at[12]).start()

    pairs = (
        (taps_hbm, taps), (gate_hbm, vectors.at[0]), (gain1_hbm, vectors.at[1]), (gain2_hbm, vectors.at[2]),
        (wq_hbm, wq), (wk_hbm, wk), (wv_hbm, wv), (bucket_hbm, buckets.at[0]), (rel_hbm, rel), (wo_hbm, wo),
        (w1_hbm, w1), (w2_hbm, w2),
    )
    vectors[...] = jnp.zeros_like(vectors)
    copies = start_all(pairs, sems)
    length = lengths_ref[seq]
    row8 = lax.broadcasted_iota(jnp.int32, (SHD, L), 0)
    lane8 = lax.broadcasted_iota(jnp.int32, (SHD, L), 1)
    for copy in copies[:9]:
        copy.wait()
    table[...] = jnp.zeros_like(table)
    table[:SH] = offset_table(buckets[...], rel[...])
    eye = lax.broadcasted_iota(jnp.int32, (DS, DS), 0) == lax.broadcasted_iota(
        jnp.int32, (DS, DS), 1
    )
    columns = dot(eye.astype(F32), vectors[...], ((1,), (1,)), lax.Precision.HIGHEST)
    gate = jax.nn.sigmoid(columns[:, 0:1])
    gain1, gain2 = columns[:, 1:2], columns[:, 2:3]
    pltpu.make_async_copy(moved_hbm[0], moved, sems.at[12]).wait()
    tap = taps[...].astype(F32)
    old = moved[0].astype(F32)
    mixed = gate * tap + (1.0 - gate) * old
    scale1 = column_norm(mixed)
    unit1 = mixed * scale1
    normed1 = (unit1 * gain1).astype(BF16)
    query = dot_tn(wq[...], normed1).astype(BF16).astype(F32)
    key = dot_tn(wk[...], normed1).astype(BF16).astype(F32)
    value = dot_tn(wv[...], normed1)
    fill_heads(qt, query, jnp.where(row8 == 0, 1.0, 0.0))
    fill_heads(kt, key, jnp.where((row8 == 0) & (lane8 >= length), MASKED, 0.0))
    fill_heads(vt, value, jnp.where(row8 < 2, 1.0, 0.0))
    top = jnp.max(head_sums(query * query), axis=1) * jnp.max(head_sums(key * key), axis=1)
    safe = jnp.sqrt(jnp.max(top)) + jnp.max(jnp.abs(table[...])) < LIMIT
    blocks = [slice(b * TILE, (b + 1) * TILE) for b in range(L // TILE)]

    def rows8(head):
        return pl.ds(pl.multiple_of(head * SHD, SHD), SHD)

    def attend(head, stable):
        tile = toeplitz(table[pl.ds(head, 1)])
        for block, rows in enumerate(blocks):
            start = (L // TILE - 1 - block) * TILE
            scores = dot_tn(qt[head, :, rows], kt[head]) + tile[:, start : start + L]
            if stable:
                scores = scores - jnp.max(scores, axis=1, keepdims=True)
            probs[head, rows] = jnp.exp(scores).astype(BF16)
        both = dot_nt(vt[head], probs[head])
        ctx[rows8(head)] = both[:SHD]
        sums[rows8(head)] = jnp.broadcast_to(both[SHD : SHD + 1], (SHD, L))

    @pl.when(safe)
    def _():
        @pl.loop(0, SH, step=UNROLL)
        def _(first):
            for n in range(UNROLL):
                attend(first + n, False)

    @pl.when(jnp.logical_not(safe))
    def _():
        @pl.loop(0, SH)
        def _(head):
            attend(head, True)

    for copy in copies[9:12]:
        copy.wait()
    inverse = 1.0 / sums[...]
    context = ctx[...] * inverse
    context16 = context.astype(BF16)
    residual = mixed + dot_tn(wo[...], context16)
    scale2 = column_norm(residual)
    unit2 = residual * scale2
    normed2 = (unit2 * gain2).astype(BF16)
    pre = dot_tn(w1[...], normed2)
    cdf = normal_cdf(pre)
    inner = (pre * cdf).astype(BF16)
    back_ref[0] = (residual + dot(w2[...], inner)).astype(BF16)

    cotangent = moved[1]
    slope = cdf + pre * (jnp.exp(-0.5 * pre * pre) * (1.0 / math.sqrt(2.0 * math.pi)))
    d_pre = (dot_tn(w2[...], cotangent) * slope).astype(BF16)
    g_ffout = dot_nt(cotangent, inner)
    g_ffin = dot_nt(normed2, d_pre)
    for n in range(FS // W):
        for first, grad in ((FFIN0, g_ffin), (FFOUT0, g_ffout)):
            start = first - QKV0 + n * DS
            rest_ref[start : start + DS] = grad[:, n * W : (n + 1) * W].astype(BF16)
    dy = dot(w1[...], d_pre)
    g_gain2 = jnp.sum(dy * unit2, axis=1, keepdims=True)
    d_resid = cotangent.astype(F32) + norm_back(dy * gain2, unit2, scale2)
    d_attn = d_resid.astype(BF16)
    pad = jnp.zeros((W - DS, L), BF16)
    g_project = dot_nt(context16, jnp.concatenate([d_attn, pad], axis=0))
    d_context = dot(wo[...], d_attn).astype(BF16)
    d_scaled = (d_context.astype(F32) * inverse).astype(BF16).astype(F32)
    delta = head_sums(d_scaled * context)
    delta_hi = delta.astype(BF16).astype(F32)
    extra = []
    for head in range(SH):
        high, low = delta_hi[head : head + 1], (delta - delta_hi)[head : head + 1]
        extra.append(jnp.where(row8 == 0, -high, jnp.where(row8 == 1, -low, 0.0)))
    fill_heads(dt, d_scaled, extra)
    dtab[...] = jnp.zeros_like(dtab)

    def attend_back(head, spot):
        for block, rows in enumerate(blocks):
            grads = dot_tn(dt[head, :, rows], vt[head])
            dall[spot, rows] = (probs[head, rows].astype(F32) * grads).astype(BF16)
        dk[rows8(head)] = dot(qt[head], dall[spot])[:SHD]
        dv[rows8(head)] = dot(dt[head], probs[head])[:SHD]
        dq[rows8(head)] = dot_nt(kt[head], dall[spot])[:SHD]
        tiles = []
        for offset in range(2 * (L // TILE) - 1):
            total_tile = None
            for block, rows in enumerate(blocks):
                n = offset + block - (L // TILE - 1)
                if 0 <= n < L // TILE:
                    piece = dall[spot, rows, n * TILE : (n + 1) * TILE].astype(F32)
                    total_tile = piece if total_tile is None else total_tile + piece
            diag[spot, :, offset * TILE : (offset + 1) * TILE] = total_tile
        diag[spot, :, 2 * L - TILE :] = jnp.zeros((TILE, TILE), F32)
        back = 7 - lax.broadcasted_iota(jnp.int32, (8, 2 * L), 0)
        groups = [
            jnp.take_along_axis(diag[spot, g * 8 : g * 8 + 8], back, axis=0)
            for g in reversed(range(TILE // 8))
        ]
        rolled = pltpu.roll(jnp.concatenate(groups, axis=0), 0, 1, stride=1, stride_axis=0)
        dtab[pl.ds(head, 1)] = jnp.sum(rolled, axis=0, keepdims=True)

    @pl.loop(0, SH, step=UNROLL_BACK)
    def _(first):
        for n in range(UNROLL_BACK):
            attend_back(first + n, n)


    spots = lax.broadcasted_iota(jnp.int32, (W, OFFSETS), 0) - DS
    onehot = (spots == buckets[...]).astype(F32)
    g_rel = dot(dtab[:, :OFFSETS], onehot, ((1,), (1,)), lax.Precision.HIGHEST)
    grads = [ref[...].astype(BF16) for ref in (dq, dk, dv)]
    for n, grad in enumerate(grads):
        full = dot_nt(normed1, jnp.concatenate([grad, pad], axis=0))
        if n == 0:
            full = full + jnp.concatenate([g_rel, jnp.zeros((DS - 16, W), F32)], axis=0)
        rest_ref[n * DS : (n + 1) * DS] = full.astype(BF16)
    d_normed = dot(wq[...], grads[0]) + dot(wk[...], grads[1]) + dot(wv[...], grads[2])
    d_mixed = d_resid + norm_back(d_normed * gain1, unit1, scale1)
    back_ref[1] = ((1.0 - gate) * d_mixed).astype(BF16)
    tap_ref[...] = (gate * d_mixed).astype(BF16)
    g_gate = gate * (1.0 - gate) * jnp.sum(d_mixed * (tap - old), axis=1, keepdims=True)
    g_gain1 = jnp.sum(d_normed * unit1, axis=1, keepdims=True)
    lane = lax.broadcasted_iota(jnp.int32, (DS, W), 1)
    for n, grad in enumerate((g_gate, g_gain1, g_gain2)):
        g_project = jnp.where(lane == DS + n, grad, g_project)
    rest_ref[PROJ0 - QKV0 : PROJ0 - QKV0 + DS] = g_project.astype(BF16)


def pack_kernel(tap_ref, rest_ref, hidden_ref, keep_ref, send_ref, pack):
    down = dot(tap_ref[...], hidden_ref[...])
    for n in range(D // W):
        pack[n * DS : (n + 1) * DS] = down[:, n * W : (n + 1) * W].astype(BF16)
    pack[QKV0:] = rest_ref[...]
    core, across = place()
    for n in range(2):
        for ref, half in ((keep_ref, core), (send_ref, 1 - core)):
            start = (half * 2 + (across if n == 0 else 1 - across)) * PART
            ref[n] = pack[pl.ds(pl.multiple_of(start, PART), PART)]


def pack_grads(tap, rest, hidden):
    vmem = pl.BlockSpec(memory_space=pltpu.VMEM)
    return pl.pallas_call(
        pack_kernel,
        out_shape=(jax.ShapeDtypeStruct((2, PART, W), BF16),) * 2,
        in_specs=[vmem] * 3,
        out_specs=(vmem,) * 2,
        scratch_shapes=[pltpu.VMEM((PACK, W), BF16)],
        compiler_params=pltpu.CompilerParams(vmem_limit_bytes=8 * 1024 * 1024),
        cost_estimate=pl.CostEstimate(
            flops=80_000_000, bytes_accessed=2_000_000, transcendentals=0
        ),
        name="pack_grads",
    )(tap, rest, hidden)


def side_block(lengths, assign, moved, *args):
    smem = pl.BlockSpec(memory_space=pltpu.SMEM)
    vmem = pl.BlockSpec(memory_space=pltpu.VMEM)
    hbm = pl.BlockSpec(memory_space=pl.ANY)
    count = len(moved)
    return pl.pallas_call(
        functools.partial(side_kernel, count),
        out_shape=(
            jax.ShapeDtypeStruct((2, DS, L), BF16),
            jax.ShapeDtypeStruct((DS, L), BF16),
            jax.ShapeDtypeStruct((PACK - QKV0, W), BF16),
        ),
        in_specs=[smem, smem] + [hbm] * (count + len(args)),
        out_specs=(vmem,) * 3,
        scratch_shapes=[
            pltpu.VMEM((DS, L), BF16),
            pltpu.VMEM((8, DS), F32),
            pltpu.VMEM((DS, DS), BF16),
            pltpu.VMEM((DS, DS), BF16),
            pltpu.VMEM((DS, DS), BF16),
            pltpu.VMEM((1, OFFSETS), jnp.int32),
            pltpu.VMEM((SH, NB), F32),
            pltpu.VMEM((DS, DS), BF16),
            pltpu.VMEM((DS, FS), BF16),
            pltpu.VMEM((DS, FS), BF16),
            pltpu.VMEM((2, DS, L), BF16),
            pltpu.SemaphoreType.DMA((13,)),
            pltpu.VMEM((16, 2 * L), F32),
            pltpu.VMEM((SH, L, L), BF16),
            pltpu.VMEM((SH, 2 * SHD, L), BF16),
            pltpu.VMEM((SH, 2 * SHD, L), BF16),
            pltpu.VMEM((SH, 2 * SHD, L), BF16),
            pltpu.VMEM((SH, 2 * SHD, L), BF16),
            pltpu.VMEM((DS, L), F32),
            pltpu.VMEM((DS, L), F32),
            pltpu.VMEM((DS, L), F32),
            pltpu.VMEM((DS, L), F32),
            pltpu.VMEM((DS, L), F32),
            pltpu.VMEM((UNROLL_BACK, L, L), BF16),
            pltpu.VMEM((UNROLL_BACK, TILE, 2 * L), F32),
            pltpu.VMEM((16, 2 * L), F32),
        ],
        compiler_params=pltpu.CompilerParams(vmem_limit_bytes=VMEM_BYTES),
        cost_estimate=pl.CostEstimate(
            flops=9_000_000_000, bytes_accessed=4_000_000, transcendentals=5_000_000
        ),
        name="side_block",
    )(lengths, assign, *moved, *args)


def finish_kernel(count, assign_ref, *rest):
    quarters, rest = rest[:4], rest[4:]
    backs, results = rest[:count], rest[count : count + 13]
    part, out, *parts, sems = rest[count + 13 :]
    rank = lax.axis_index("side")
    core, across = place()
    spots = [
        2 * half + quarter for half in (core, 1 - core) for quarter in (across, 1 - across)
    ]
    masks = [0]
    for n in reversed(range(16)):
        if 1 << n < count:
            masks += [mask ^ (1 << n) for mask in masks]
    slot = jnp.int32(0)
    for n in range(count):
        slot = jnp.where(assign_ref[n] == rank, n, slot)
    gstate, down, gate, gain1, gq, gk, gv, go, rel, gain2, g1, g2 = parts
    for step in range(count):

        @pl.when((rank ^ slot) == masks[step])
        def _():
            out[...] = backs[step][0]
            gstate[...] = backs[step][1].astype(F32)

    targets = [out, *parts]
    pairs = [
        (ref.at[0] if ref.shape[0] == 1 else ref, result)
        for ref, result in zip(targets, results, strict=True)
    ]
    copies = [pltpu.make_async_copy(src, dst, sems.at[n]) for n, (src, dst) in enumerate(pairs)]
    copies[0].start()
    copies[1].start()
    for ref, spot in zip(quarters, spots, strict=True):
        part[spot] = ref[...]

    def take(start, stop):
        pieces = []
        for n in range(4):
            low, high = max(start, n * PART), min(stop, (n + 1) * PART)
            if low < high:
                pieces.append(part[n, low - n * PART : high - n * PART].astype(F32))
        return pieces[0] if len(pieces) == 1 else jnp.concatenate(pieces, axis=0)

    for n in range(D // W):
        down[:, n * W : (n + 1) * W] = take(DOWN0 + n * DS, DOWN0 + (n + 1) * DS)
    for n, ref in enumerate((gq, gk, gv)):
        ref[...] = take(QKV0 + n * DS, QKV0 + (n + 1) * DS)[:, :DS]
    rel[...] = take(QKV0, QKV0 + 16)[:SH, DS : DS + NB]
    project = take(PROJ0, PROJ0 + DS)
    go[...] = project[:, :DS]
    turned = project.T
    gate[...] = turned[DS : DS + 1]
    gain1[...] = turned[DS + 1 : DS + 2]
    gain2[...] = turned[DS + 2 : DS + 3]
    for n in range(FS // W):
        g1[:, n * W : (n + 1) * W] = take(FFIN0 + n * DS, FFIN0 + (n + 1) * DS)
        g2[:, n * W : (n + 1) * W] = take(FFOUT0 + n * DS, FFOUT0 + (n + 1) * DS)
    for copy in copies[2:]:
        copy.start()
    for copy in copies:
        copy.wait()


def finish(assign, quarters, backs):
    smem = pl.BlockSpec(memory_space=pltpu.SMEM)
    vmem = pl.BlockSpec(memory_space=pltpu.VMEM)
    hbm = pl.BlockSpec(memory_space=pl.ANY)
    fixed = pl.BlockSpec(memory_space=pltpu.HBM)
    count = len(backs)
    parts = [
        (DS, L), (DS, D), (1, DS), (1, DS), (DS, DS), (DS, DS), (DS, DS), (DS, DS), (SH, NB), (1, DS), (DS, FS), (DS, FS),
    ]
    shapes = [jax.ShapeDtypeStruct(p[1:] if p[0] == 1 else p, F32) for p in parts]
    return pl.pallas_call(
        functools.partial(finish_kernel, count),
        out_shape=(jax.ShapeDtypeStruct((DS, L), BF16), *shapes),
        in_specs=[smem] + [vmem] * (4 + count),
        out_specs=(hbm,) * 13,
        scratch_shapes=[
            pltpu.VMEM((4, PART, W), BF16),
            pltpu.VMEM((DS, L), BF16),
            *[pltpu.VMEM(p, F32) for p in parts],
            pltpu.SemaphoreType.DMA((13,)),
        ],
        compiler_params=pltpu.CompilerParams(vmem_limit_bytes=16 * 1024 * 1024),
        name="finish",
    )(assign, *quarters, *backs)


def swap(value, axis, bit):
    size = lax.axis_size(axis)
    return lax.ppermute(value, axis, [(i, i ^ bit) for i in range(size)])


def rotations(value):
    size = lax.axis_size("side")
    return [value] + [
        lax.ppermute(value, "side", [(i, (i + k) % size) for i in range(size)])
        for k in range(1, size)
    ]


def add(one, two):
    return (one.astype(F32) + two.astype(F32)).astype(BF16)


def bits(axis, first=0):
    return [1 << n for n in range(first, 16) if 1 << n < lax.axis_size(axis)]


def spread(blocks, bit):
    return blocks + [swap(block, "side", bit) for block in blocks]


def total(keep, send, back):
    levels = bits("side")[::-1]
    backs = spread([back], levels[0])
    got = swap(send, "dp", 1)
    mine = add(keep[0], got[0])
    across = swap(add(keep[1], got[1]), "dp", 2)
    mine = add(mine, across)
    mine = add(mine, swap(mine, "side", 1))
    mine, *backs = lax.optimization_barrier((mine, *backs))
    for bit in levels[1:]:
        backs = spread(backs, bit)
    for bit in bits("dp", 2):
        mine = add(mine, swap(mine, "dp", bit))
    for bit in bits("side", 1):
        mine = add(mine, swap(mine, "side", bit))
    across = swap(mine, "dp", 2)
    return (mine, across, swap(mine, "dp", 1), swap(across, "dp", 1)), backs


def shards(
    hidden_in, side_state, lengths, assign, buckets,
    backbone_gain_attn, backbone_query, backbone_key, backbone_value, backbone_project, backbone_rel,
    backbone_gain_ff, backbone_ff_in, backbone_ff_out, down_weight, gate_logit,
    side_gain_attn, side_query, side_key, side_value, side_project, side_rel,
    side_gain_ff, side_ff_in, side_ff_out, cotangent,
):
    moved = rotations(jnp.stack([side_state[0].T, cotangent[0].T]))
    hidden, taps = backbone(
        lengths, assign, backbone_rel.T, buckets, hidden_in[0], backbone_gain_attn,
        backbone_query, backbone_key, backbone_value, backbone_project, backbone_gain_ff,
        backbone_ff_in, backbone_ff_out, down_weight.T,
    )
    back, tap, rest = side_block(
        lengths, assign, moved, taps, gate_logit, side_gain_attn, side_gain_ff,
        side_query, side_key, side_value, buckets, side_rel.T, side_project, side_ff_in, side_ff_out.T,
    )
    keep, send = pack_grads(tap, rest, hidden)
    quarters, backs = total(keep, send, back)
    res = finish(assign, quarters, backs)
    out, gstate, down, gate, gain1, gq, gk, gv, go, rel, gain2, g1, g2 = res
    return (
        out.T[None], gstate.T[None], down.T, gate, gain1, gq, gk, gv, go, rel.T, gain2, g1, g2.T,
    )


def solution(mesh):
    rows = P(("dp", "side"), None, None)
    return jax.shard_map(
        shards,
        mesh=mesh,
        in_specs=(rows, rows, P("dp"), P("dp")) + (P(),) * 21 + (rows,),
        out_specs=(rows, rows) + (P(),) * 11,
        check_vma=False,
    )
```

time: 118 us -> 81 us (0.69)
  Pallas kernels: 54.8 us -> 35.3 us
  waiting for transfers between devices: 36.9 us -> 25.8 us
  starting transfers between devices: 20.4 us -> 16.4 us
  local copies, waits for them, and re-layouts: 3.38 us -> 0.96 us
    pallas_call x1, Pallas kernels: 30.2 us -> 15.9 us  [side_block(): pl.pallas_call(functools.partial(side_kernel, count), out_shape=(jax.Shap...]
    ppermute x9 -> x3, waiting for transfers between devices: 13.2 us -> 0.01 us  [rotations(): lax.ppermute(value, 'side', [(i, (i + k) % size) for i in range(size)])]
    ppermute x9 -> x3, starting transfers between devices: 13.2 us -> 6.11 us  [rotations(): lax.ppermute(value, 'side', [(i, (i + k) % size) for i in range(size)])]
    pallas_call x1, Pallas kernels: 22 us -> 17.5 us  [backbone(): pl.pallas_call(backbone_kernel, out_shape=(jax.ShapeDtypeStruct((L, D), B...]
    ppermute x6 -> x11, starting transfers between devices: 7.2 us -> 10.3 us  [swap(): return lax.ppermute(value, axis, [(i, i ^ bit) for i in range(size)])]
    ppermute x6 -> x11, waiting for transfers between devices: 23.6 us -> 25.8 us  [swap(): return lax.ppermute(value, axis, [(i, i ^ bit) for i in range(size)])]
    pad x1 -> x0, local copies, waits for them, and re-layouts: 1.28 us -> none  [shards(): wide = jnp.pad(buckets, (0, 1))]
  transfers between devices with their start and end apart: 15 -> 14, of which waited for: 7 -> 9; matrix products, arithmetic and copies ran while one was open for 1% -> 0% of each run, Pallas kernels for 19% -> 22%
where the time goes in v2:
time: 81 us; the launch traced here: 80.7 us
  Pallas kernels  35.3 us (44%)
  waiting for transfers between devices  25.8 us (32%)
  starting transfers between devices  16.4 us (20%)
  other arithmetic  1.12 us (1%)
  between operations  1.11 us (1%)
  local copies, waits for them, and re-layouts  0.96 us (1%)
    ppermute x11, waiting for transfers between devices, swap(): return lax.ppermute(value, axis, [(i, i ^ bit) for i in range(size)])  25.8 us
    pallas_call x1, Pallas kernels, backbone(): pl.pallas_call(backbone_kernel, out_shape=(jax.ShapeDtypeStruct((L, D), B...  17.5 us
    pallas_call x1, Pallas kernels, side_block(): pl.pallas_call(functools.partial(side_kernel, count), out_shape=(jax.Shap...  15.9 us
    ppermute x11, starting transfers between devices, swap(): return lax.ppermute(value, axis, [(i, i ^ bit) for i in range(size)])  10.3 us
    ppermute x3, starting transfers between devices, rotations(): lax.ppermute(value, 'side', [(i, (i + k) % size) for i in range(size)])  6.11 us
    pallas_call x1, Pallas kernels, finish(): pl.pallas_call(functools.partial(finish_kernel, count), out_shape=(jax.Sh...  1.69 us
  transfers between devices with their start and end apart: 14, of which 9 were waited for; matrix products, arithmetic and copies ran while one was open for 0% of the time, Pallas kernels for 22%

profile of v2, /device:TPU:0, one launch (start us, length us, event | category | flops | bytes accessed | tf_op | source)
XLA Modules:
  0.0 80.7 jit_solution(15510185376492278762)
XLA Ops:
  0.6 1.0 %pad_maximum_fusion.rest_0_ = bf16[2,96,512]{2,1,0:T(8,128)(2,1)S(1)} fusion(bf16[1,96,512]{2,1,0:T(8,128)(2,1)} %bitcast.33, bf16[1,96,512]{2,1,0:T(8,128)(2,1)} %bitcast.34), kind=kLoop, calls=%fused_computation | loop fusion | flops 98304 | bytes 393216 | tf_op jit(solution)/shard_map/stack | solution.py:649
  1.6 5.1 %collective-permute-start.2 = (bf16[2,96,512]{2,1,0:T(8,128)(2,1)S(1)}, bf16[2,96,512]{2,1,0:T(8,128)(2,1)S(1)}, u32[]{:S(2)}, u32[]{:S(2)}) collective-permute-start(bf16[2,96,512]{2,1,0:T(8,128)(2,1)S(1)} %pad_maximum_fusion.rest_0_), channel_id=1, source_target_pairs={{0,3},{1,0},{2,1},{3,2},{4,7},{5,4},{6,5},{7,6},{8,11},{9,8},{10,9... | collective-permute-start | bytes 589832 | tf_op jit(solution)/shard_map/ppermute | solution.py:606
  6.7 1.0 %collective-permute-start = (bf16[2,96,512]{2,1,0:T(8,128)(2,1)S(1)}, bf16[2,96,512]{2,1,0:T(8,128)(2,1)S(1)}, u32[]{:S(2)}, u32[]{:S(2)}) collective-permute-start(bf16[2,96,512]{2,1,0:T(8,128)(2,1)S(1)} %pad_maximum_fusion.rest_0_), channel_id=1, source_target_pairs={{0,1},{1,2},{2,3},{3,0},{4,5},{5,6},{6,7},{7,4},{8,9},{9,10},{10,1... | collective-permute-start | bytes 589832 | tf_op jit(solution)/shard_map/ppermute | solution.py:606
  7.8 17.5 %backbone.1 = (bf16[512,768]{1,0:T(8,128)(2,1)}, bf16[96,512]{1,0:T(8,128)(2,1)}) custom-call(s32[4]{0:T(128)} %lengths_ref.3, s32[4]{0:T(128)} %assign_ref.5, f32[12,32]{1,0:T(8,128)} %bitcast.41, s32[1023]{0:T(1024)} %rest_11_.1, bf16[512,768]{1,0:T(8,128)(2,1)} %bitcast.35, f32[768]{0:T(1024)} %gain1_hbm.1, bf16[768,768]{1,0:T(8,128)(2,1)} %wq_hbm.1, ...), custom_call_target="tpu_custom_call" | custom-call | flops 8999999488 | bytes 17000000 | tf_op jit(solution)/shard_map/backbone/pallas_call | solution.py:190
  25.5 0.9 %copy-done.14 = bf16[96,512]{1,0:T(8,128)(2,1)S(1)} copy-done((bf16[96,512]{1,0:T(8,128)(2,1)S(1)}, bf16[96,512]{1,0:T(8,128)(2,1)}, u32[]{:S(2)}) %copy-start.14) | copy-done | bytes 98328
  26.4 15.9 %side_block.1 = (bf16[2,96,512]{2,1,0:T(8,128)(2,1)S(1)}, bf16[96,512]{1,0:T(8,128)(2,1)S(1)}, bf16[960,128]{1,0:T(8,128)(2,1)S(1)}) custom-call(s32[4]{0:T(128)S(1)} %copy-done.10, s32[4]{0:T(128)S(1)} %copy-done.1, bf16[2,96,512]{2,1,0:T(8,128)(2,1)S(1)} %pad_maximum_fusion.rest_0_, bf16[2,96,512]{2,1,0:T(8,128)(2,1)S(1)} %collective-permute-done.rest_1_, ...), custom_call_target="tpu_custom_call" | custom-call | flops 8999999488 | bytes 4000000 | tf_op jit(solution)/shard_map/side_block/pallas_call | solution.py:464
  42.3 0.3 pack_grads.1
  42.7 1.4 %collective-permute-done.3 = bf16[2,384,128]{2,1,0:T(8,128)(2,1)S(1)} collective-permute-done((bf16[2,384,128]{2,1,0:T(8,128)(2,1)S(1)}, bf16[2,384,128]{2,1,0:T(8,128)(2,1)S(1)}, u32[]{:S(2)}, u32[]{:S(2)}) %collective-permute-start.3) | collective-permute-done | bytes 196640 | tf_op jit(solution)/shard_map/ppermute | solution.py:600
  44.1 1.6 %collective-permute-start.4 = (bf16[384,128]{1,0:T(8,128)(2,1)S(1)}, bf16[384,128]{1,0:T(8,128)(2,1)S(1)}, u32[]{:S(2)}, u32[]{:S(2)}) collective-permute-start(bf16[384,128]{1,0:T(8,128)(2,1)S(1)} %fusion.2), channel_id=1, source_target_pairs={{0,8},{4,12},{8,0},{12,4},{16,24},{20,28},{24,16},{28,20},{1,9},{5... | collective-permute-start | bytes 294920 | tf_op jit(solution)/shard_map/ppermute | solution.py:600
  45.7 3.3 %collective-permute-done.4 = bf16[384,128]{1,0:T(8,128)(2,1)S(1)} collective-permute-done((bf16[384,128]{1,0:T(8,128)(2,1)S(1)}, bf16[384,128]{1,0:T(8,128)(2,1)S(1)}, u32[]{:S(2)}, u32[]{:S(2)}) %collective-permute-start.4) | collective-permute-done | bytes 98336 | tf_op jit(solution)/shard_map/ppermute | solution.py:600
  49.1 2.5 %collective-permute-start.5 = (bf16[384,128]{1,0:T(8,128)(2,1)S(1)}, bf16[384,128]{1,0:T(8,128)(2,1)S(1)}, u32[]{:S(2)}, u32[]{:S(2)}) collective-permute-start(bf16[384,128]{1,0:T(8,128)(2,1)S(1)} %fusion), channel_id=1, source_target_pairs={{0,1},{1,0},{2,3},{3,2},{4,5},{5,4},{6,7},{7,6},{8,9},{9,8},{10,11... | collective-permute-start | bytes 294920 | tf_op jit(solution)/shard_map/ppermute | solution.py:600
  51.6 0.9 %collective-permute-start.6 = (bf16[2,96,512]{2,1,0:T(8,128)(2,1)S(1)}, bf16[2,96,512]{2,1,0:T(8,128)(2,1)S(1)}, u32[]{:S(2)}, u32[]{:S(2)}) collective-permute-start(bf16[2,96,512]{2,1,0:T(8,128)(2,1)S(1)} %get-tuple-element.44.rest_4_), channel_id=1, source_target_pairs={{0,2},{1,3},{2,0},{3,1},{4,6},{5,7},{6,4},{7,5},{8,10},{9,11},{10,... | collective-permute-start | bytes 589832 | tf_op jit(solution)/shard_map/ppermute | solution.py:600
  52.5 2.4 %collective-permute-done.5 = bf16[384,128]{1,0:T(8,128)(2,1)S(1)} collective-permute-done((bf16[384,128]{1,0:T(8,128)(2,1)S(1)}, bf16[384,128]{1,0:T(8,128)(2,1)S(1)}, u32[]{:S(2)}, u32[]{:S(2)}) %collective-permute-start.5) | collective-permute-done | bytes 98336 | tf_op jit(solution)/shard_map/ppermute | solution.py:600
  54.9 7.5 %collective-permute-done.6.rest_5_ = bf16[2,96,512]{2,1,0:T(8,128)(2,1)S(1)} collective-permute-done((bf16[2,96,512]{2,1,0:T(8,128)(2,1)S(1)}, bf16[2,96,512]{2,1,0:T(8,128)(2,1)S(1)}, u32[]{:S(2)}, u32[]{:S(2)}) %collective-permute-start.6) | collective-permute-done | bytes 196640 | tf_op jit(solution)/shard_map/ppermute | solution.py:600
  62.4 1.5 %collective-permute-start.7 = (bf16[384,128]{1,0:T(8,128)(2,1)S(1)}, bf16[384,128]{1,0:T(8,128)(2,1)S(1)}, u32[]{:S(2)}, u32[]{:S(2)}) collective-permute-start(bf16[384,128]{1,0:T(8,128)(2,1)S(1)} %add_convert_fusion.2), channel_id=1, source_target_pairs={{0,16},{4,20},{8,24},{12,28},{16,0},{20,4},{24,8},{28,12},{1,17},{... | collective-permute-start | bytes 294920 | tf_op jit(solution)/shard_map/ppermute | solution.py:600
  63.9 3.1 %collective-permute-done.7 = bf16[384,128]{1,0:T(8,128)(2,1)S(1)} collective-permute-done((bf16[384,128]{1,0:T(8,128)(2,1)S(1)}, bf16[384,128]{1,0:T(8,128)(2,1)S(1)}, u32[]{:S(2)}, u32[]{:S(2)}) %collective-permute-start.7) | collective-permute-done | bytes 98336 | tf_op jit(solution)/shard_map/ppermute | solution.py:600
  67.1 1.6 %collective-permute-start.12 = (bf16[2,96,512]{2,1,0:T(8,128)(2,1)S(1)}, bf16[2,96,512]{2,1,0:T(8,128)(2,1)S(1)}, u32[]{:S(2)}, u32[]{:S(2)}) collective-permute-start(bf16[2,96,512]{2,1,0:T(8,128)(2,1)S(1)} %get-tuple-element.44.rest_4_), channel_id=1, source_target_pairs={{0,1},{1,0},{2,3},{3,2},{4,5},{5,4},{6,7},{7,6},{8,9},{9,8},{10,11... | collective-permute-start | bytes 589832 | tf_op jit(solution)/shard_map/ppermute | solution.py:600
  68.7 0.5 collective-permute-start.13
  69.2 3.6 %collective-permute-done.8 = bf16[384,128]{1,0:T(8,128)(2,1)S(1)} collective-permute-done((bf16[384,128]{1,0:T(8,128)(2,1)S(1)}, bf16[384,128]{1,0:T(8,128)(2,1)S(1)}, u32[]{:S(2)}, u32[]{:S(2)}) %collective-permute-start.8) | collective-permute-done | bytes 98336 | tf_op jit(solution)/shard_map/ppermute | solution.py:600
  72.9 1.6 %collective-permute-start.9 = (bf16[384,128]{1,0:T(8,128)(2,1)S(1)}, bf16[384,128]{1,0:T(8,128)(2,1)S(1)}, u32[]{:S(2)}, u32[]{:S(2)}) collective-permute-start(bf16[384,128]{1,0:T(8,128)(2,1)S(1)} %add_convert_fusion.rest_0_), channel_id=1, source_target_pairs={{0,8},{4,12},{8,0},{12,4},{16,24},{20,28},{24,16},{28,20},{1,9},{5... | collective-permute-start | bytes 294920 | tf_op jit(solution)/shard_map/ppermute | solution.py:600
  74.5 3.1 %collective-permute-done.9.rest_1_ = bf16[384,128]{1,0:T(8,128)(2,1)S(1)} collective-permute-done((bf16[384,128]{1,0:T(8,128)(2,1)S(1)}, bf16[384,128]{1,0:T(8,128)(2,1)S(1)}, u32[]{:S(2)}, u32[]{:S(2)}) %collective-permute-start.9) | collective-permute-done | bytes 98336 | tf_op jit(solution)/shard_map/ppermute | solution.py:600
  77.6 0.7 collective-permute-done.13.rest_7_
  78.2 0.6 collective-permute-done.11.rest_3_
  78.9 1.7 %finish.1 = (bf16[96,512]{1,0:T(8,128)(2,1)}, f32[96,512]{1,0:T(8,128)}, f32[96,768]{1,0:T(8,128)}, f32[96]{0:T(128)}, f32[96]{0:T(128)}, /*index=5*/f32[96,96]{...) custom-call(s32[4]{0:T(128)S(1)} %copy-done.1, ...), custom_call_target="tpu_custom_call" | custom-call | tf_op jit(solution)/shard_map/finish/pallas_call | solution.py:582
  (44 shorter events, 0.4 us)
Async XLA Ops:
  1.6 23.7 %collective-permute-start.2 = (bf16[2,96,512]{2,1,0:T(8,128)(2,1)S(1)}, bf16[2,96,512]{2,1,0:T(8,128)(2,1)S(1)}, u32[]{:S(2)}, u32[]{:S(2)}) collective-permute-start(bf16[2,96,512]{2,1,0:T(8,128)(2,1)S(1)} %pad_maximum_fusion.rest_0_), channel_id=1, source_target_pairs={{0,3},{1,0},{2,1},{3,2},{4,7},{5,4},{6,5},{7,6},{8,11},{9,8},{10,9... | collective-permute-start | bytes 589832 | tf_op jit(solution)/shard_map/ppermute | solution.py:606
  6.7 18.6 %collective-permute-start.1 = (bf16[2,96,512]{2,1,0:T(8,128)(2,1)S(1)}, bf16[2,96,512]{2,1,0:T(8,128)(2,1)S(1)}, u32[]{:S(2)}, u32[]{:S(2)}) collective-permute-start(bf16[2,96,512]{2,1,0:T(8,128)(2,1)S(1)} %pad_maximum_fusion.rest_0_), channel_id=1, source_target_pairs={{0,2},{1,3},{2,0},{3,1},{4,6},{5,7},{6,4},{7,5},{8,10},{9,11},{10,... | collective-permute-start | bytes 589832 | tf_op jit(solution)/shard_map/ppermute | solution.py:606
  6.7 18.6 %collective-permute-start = (bf16[2,96,512]{2,1,0:T(8,128)(2,1)S(1)}, bf16[2,96,512]{2,1,0:T(8,128)(2,1)S(1)}, u32[]{:S(2)}, u32[]{:S(2)}) collective-permute-start(bf16[2,96,512]{2,1,0:T(8,128)(2,1)S(1)} %pad_maximum_fusion.rest_0_), channel_id=1, source_target_pairs={{0,1},{1,2},{2,3},{3,0},{4,5},{5,6},{6,7},{7,4},{8,9},{9,10},{10,1... | collective-permute-start | bytes 589832 | tf_op jit(solution)/shard_map/ppermute | solution.py:606
  7.7 17.6 %copy-start.3 = (bf16[384,96]{0,1:T(8,128)(2,1)S(1)}, bf16[384,96]{0,1:T(8,128)(2,1)}, u32[]{:S(2)}) copy-start(bf16[384,96]{0,1:T(8,128)(2,1)} %param.50) | copy-start | bytes 221188
  7.7 17.6 %copy-start.4 = (bf16[96,96]{1,0:T(8,128)(2,1)S(1)}, bf16[96,96]{1,0:T(8,128)(2,1)}, u32[]{:S(2)}) copy-start(bf16[96,96]{1,0:T(8,128)(2,1)} %rest_8_.1) | copy-start | bytes 55300
  7.7 17.6 %copy-start.5 = (bf16[96,96]{1,0:T(8,128)(2,1)S(1)}, bf16[96,96]{1,0:T(8,128)(2,1)}, u32[]{:S(2)}) copy-start(bf16[96,96]{1,0:T(8,128)(2,1)} %rest_9_.1) | copy-start | bytes 55300
  7.7 17.6 %copy-start.6 = (bf16[96,96]{1,0:T(8,128)(2,1)S(1)}, bf16[96,96]{1,0:T(8,128)(2,1)}, u32[]{:S(2)}) copy-start(bf16[96,96]{1,0:T(8,128)(2,1)} %rest_10_.1) | copy-start | bytes 55300
  7.8 17.6 %copy-start.7 = (bf16[96,96]{1,0:T(8,128)(2,1)S(1)}, bf16[96,96]{1,0:T(8,128)(2,1)}, u32[]{:S(2)}) copy-start(bf16[96,96]{1,0:T(8,128)(2,1)} %rest_13_.1) | copy-start | bytes 55300
  7.8 17.6 %copy-start.8 = (f32[32,12]{0,1:T(8,128)S(1)}, f32[32,12]{0,1:T(8,128)}, u32[]{:S(2)}) copy-start(f32[32,12]{0,1:T(8,128)} %param.47) | copy-start | bytes 4612
  7.8 17.6 %copy-start.9 = (s32[1023]{0:T(1024)S(1)}, s32[1023]{0:T(1024)}, u32[]{:S(2)}) copy-start(s32[1023]{0:T(1024)} %rest_11_.1) | copy-start | bytes 12280
  7.8 17.6 %copy-start.10 = (s32[4]{0:T(128)S(1)}, s32[4]{0:T(128)}, u32[]{:S(2)}) copy-start(s32[4]{0:T(128)} %lengths_ref.3) | copy-start | bytes 52
  7.8 17.6 %copy-start.11 = (f32[96]{0:T(128)S(1)}, f32[96]{0:T(128)}, u32[]{:S(2)}) copy-start(f32[96]{0:T(128)} %rest_5_.1) | copy-start | bytes 1156
  7.8 17.6 %copy-start.12 = (f32[96]{0:T(128)S(1)}, f32[96]{0:T(128)}, u32[]{:S(2)}) copy-start(f32[96]{0:T(128)} %rest_6_.1) | copy-start | bytes 1156
  42.6 1.5 %collective-permute-start.3 = (bf16[2,384,128]{2,1,0:T(8,128)(2,1)S(1)}, bf16[2,384,128]{2,1,0:T(8,128)(2,1)S(1)}, u32[]{:S(2)}, u32[]{:S(2)}) collective-permute-start(bf16[2,384,128]{2,1,0:T(8,128)(2,1)S(1)} %get-tuple-element.41), channel_id=1, source_target_pairs={{0,4},{4,0},{8,12},{12,8},{16,20},{20,16},{24,28},{28,24},{1,5},{5... | collective-permute-start | bytes 589832 | tf_op jit(solution)/shard_map/ppermute | solution.py:600
  44.1 4.9 %collective-permute-start.4 = (bf16[384,128]{1,0:T(8,128)(2,1)S(1)}, bf16[384,128]{1,0:T(8,128)(2,1)S(1)}, u32[]{:S(2)}, u32[]{:S(2)}) collective-permute-start(bf16[384,128]{1,0:T(8,128)(2,1)S(1)} %fusion.2), channel_id=1, source_target_pairs={{0,8},{4,12},{8,0},{12,4},{16,24},{20,28},{24,16},{28,20},{1,9},{5... | collective-permute-start | bytes 294920 | tf_op jit(solution)/shard_map/ppermute | solution.py:600
  49.1 5.8 %collective-permute-start.5 = (bf16[384,128]{1,0:T(8,128)(2,1)S(1)}, bf16[384,128]{1,0:T(8,128)(2,1)S(1)}, u32[]{:S(2)}, u32[]{:S(2)}) collective-permute-start(bf16[384,128]{1,0:T(8,128)(2,1)S(1)} %fusion), channel_id=1, source_target_pairs={{0,1},{1,0},{2,3},{3,2},{4,5},{5,4},{6,7},{7,6},{8,9},{9,8},{10,11... | collective-permute-start | bytes 294920 | tf_op jit(solution)/shard_map/ppermute | solution.py:600
  51.6 10.8 %collective-permute-start.6 = (bf16[2,96,512]{2,1,0:T(8,128)(2,1)S(1)}, bf16[2,96,512]{2,1,0:T(8,128)(2,1)S(1)}, u32[]{:S(2)}, u32[]{:S(2)}) collective-permute-start(bf16[2,96,512]{2,1,0:T(8,128)(2,1)S(1)} %get-tuple-element.44.rest_4_), channel_id=1, source_target_pairs={{0,2},{1,3},{2,0},{3,1},{4,6},{5,7},{6,4},{7,5},{8,10},{9,11},{10,... | collective-permute-start | bytes 589832 | tf_op jit(solution)/shard_map/ppermute | solution.py:600
  62.4 4.6 %collective-permute-start.7 = (bf16[384,128]{1,0:T(8,128)(2,1)S(1)}, bf16[384,128]{1,0:T(8,128)(2,1)S(1)}, u32[]{:S(2)}, u32[]{:S(2)}) collective-permute-start(bf16[384,128]{1,0:T(8,128)(2,1)S(1)} %add_convert_fusion.2), channel_id=1, source_target_pairs={{0,16},{4,20},{8,24},{12,28},{16,0},{20,4},{24,8},{28,12},{1,17},{... | collective-permute-start | bytes 294920 | tf_op jit(solution)/shard_map/ppermute | solution.py:600
  67.0 5.8 %collective-permute-start.8 = (bf16[384,128]{1,0:T(8,128)(2,1)S(1)}, bf16[384,128]{1,0:T(8,128)(2,1)S(1)}, u32[]{:S(2)}, u32[]{:S(2)}) collective-permute-start(bf16[384,128]{1,0:T(8,128)(2,1)S(1)} %add_convert_fusion.1), channel_id=1, source_target_pairs={{0,2},{1,3},{2,0},{3,1},{4,6},{5,7},{6,4},{7,5},{8,10},{9,11},{10,... | collective-permute-start | bytes 294920 | tf_op jit(solution)/shard_map/ppermute | solution.py:600
  67.1 10.5 %collective-permute-start.12 = (bf16[2,96,512]{2,1,0:T(8,128)(2,1)S(1)}, bf16[2,96,512]{2,1,0:T(8,128)(2,1)S(1)}, u32[]{:S(2)}, u32[]{:S(2)}) collective-permute-start(bf16[2,96,512]{2,1,0:T(8,128)(2,1)S(1)} %get-tuple-element.44.rest_4_), channel_id=1, source_target_pairs={{0,1},{1,0},{2,3},{3,2},{4,5},{5,4},{6,7},{7,6},{8,9},{9,8},{10,11... | collective-permute-start | bytes 589832 | tf_op jit(solution)/shard_map/ppermute | solution.py:600
  68.7 9.5 %collective-permute-start.13 = (bf16[2,96,512]{2,1,0:T(8,128)(2,1)S(1)}, bf16[2,96,512]{2,1,0:T(8,128)(2,1)S(1)}, u32[]{:S(2)}, u32[]{:S(2)}) collective-permute-start(bf16[2,96,512]{2,1,0:T(8,128)(2,1)S(1)} %collective-permute-done.6.rest_5_), channel_id=1, source_target_pairs={{0,1},{1,0},{2,3},{3,2},{4,5},{5,4},{6,7},{7,6},{8,9},{9,8},{10,11... | collective-permute-start | bytes 589832 | tf_op jit(solution)/shard_map/ppermute | solution.py:600
  72.9 4.7 %collective-permute-start.9 = (bf16[384,128]{1,0:T(8,128)(2,1)S(1)}, bf16[384,128]{1,0:T(8,128)(2,1)S(1)}, u32[]{:S(2)}, u32[]{:S(2)}) collective-permute-start(bf16[384,128]{1,0:T(8,128)(2,1)S(1)} %add_convert_fusion.rest_0_), channel_id=1, source_target_pairs={{0,8},{4,12},{8,0},{12,4},{16,24},{20,28},{24,16},{28,20},{1,9},{5... | collective-permute-start | bytes 294920 | tf_op jit(solution)/shard_map/ppermute | solution.py:600
  74.4 3.8 %collective-permute-start.10 = (bf16[384,128]{1,0:T(8,128)(2,1)S(1)}, bf16[384,128]{1,0:T(8,128)(2,1)S(1)}, u32[]{:S(2)}, u32[]{:S(2)}) collective-permute-start(bf16[384,128]{1,0:T(8,128)(2,1)S(1)} %add_convert_fusion.rest_0_), channel_id=1, source_target_pairs={{0,4},{4,0},{8,12},{12,8},{16,20},{20,16},{24,28},{28,24},{1,5},{5... | collective-permute-start | bytes 294920 | tf_op jit(solution)/shard_map/ppermute | solution.py:600
  77.6 1.3 %collective-permute-start.11 = (bf16[384,128]{1,0:T(8,128)(2,1)S(1)}, bf16[384,128]{1,0:T(8,128)(2,1)S(1)}, u32[]{:S(2)}, u32[]{:S(2)}) collective-permute-start(bf16[384,128]{1,0:T(8,128)(2,1)S(1)} %collective-permute-done.9.rest_1_), channel_id=1, source_target_pairs={{0,4},{4,0},{8,12},{12,8},{16,20},{20,16},{24,28},{28,24},{1,5},{5... | collective-permute-start | bytes 294920 | tf_op jit(solution)/shard_map/ppermute | solution.py:600
  (5 other events, 69.7 us)

commit v3 on v2

--- a/solution.py
+++ b/solution.py
@@ -190,8 +190,8 @@
     return pl.pallas_call(
         backbone_kernel,
         out_shape=(
-            jax.ShapeDtypeStruct((L, D), BF16),
-            jax.ShapeDtypeStruct((DS, L), BF16),
+            pltpu.VMEM((L, D), BF16),
+            pltpu.VMEM((DS, L), BF16),
         ),
         in_specs=[smem, smem] + [fixed] * 12,
         out_specs=(vmem, vmem),
@@ -620,6 +620,24 @@
     return blocks + [swap(block, "side", bit) for block in blocks]
 
 
+def settle_kernel(_, out_ref):
+    del out_ref
+
+
+def settle(block):
+    hbm = pl.BlockSpec(memory_space=pl.ANY)
+    return pl.pallas_call(
+        settle_kernel,
+        out_shape=jax.ShapeDtypeStruct(block.shape, block.dtype),
+        in_specs=[hbm],
+        out_specs=hbm,
+        input_output_aliases={0: 0},
+        cost_estimate=pl.CostEstimate(flops=1000000000, bytes_accessed=0, transcendentals=0),
+        compiler_params=pltpu.CompilerParams(vmem_limit_bytes=1024 * 1024),
+        name="settle",
+    )(block)
+
+
 def total(keep, send, back):
     levels = bits("side")[::-1]
     backs = spread([back], levels[0])
@@ -628,7 +646,7 @@
     across = swap(add(keep[1], got[1]), "dp", 2)
     mine = add(mine, across)
     mine = add(mine, swap(mine, "side", 1))
-    mine, *backs = lax.optimization_barrier((mine, *backs))
+    mine, backs[1] = lax.optimization_barrier((mine, settle(backs[1])))
     for bit in levels[1:]:
         backs = spread(backs, bit)
     for bit in bits("dp", 2):

time: 81 us -> 75.1 us (0.927)
  waiting for transfers between devices: 25.8 us -> 20.2 us
  starting transfers between devices: 16.4 us -> 17.8 us
  local copies, waits for them, and re-layouts: 0.96 us -> 0.07 us
    ppermute x11, waiting for transfers between devices: 25.8 us -> 20.2 us  [swap(): return lax.ppermute(value, axis, [(i, i ^ bit) for i in range(size)])]
    ppermute x11, starting transfers between devices: 10.3 us -> 11.7 us  [swap(): return lax.ppermute(value, axis, [(i, i ^ bit) for i in range(size)])]
    unnamed x30 -> x26, local copies, waits for them, and re-layouts: 0.96 us -> 0.07 us
    pallas_call x1 -> x2, Pallas kernels: 17.5 us -> 16.8 us  [the longest x1 16.8 us: backbone(): pl.pallas_call(backbone_kernel, out_shape=(pltpu.VMEM((L, D), BF16), pltp...]
  transfers between devices with their start and end apart: 14 -> 14, of which waited for: 9 -> 7; matrix products, arithmetic and copies ran while one was open for 0% -> 0% of each run, Pallas kernels for 22% -> 22%
where the time goes in v3:
time: 75.1 us; the launch traced here: 74.9 us
  Pallas kernels  34.7 us (46%)
  waiting for transfers between devices  20.2 us (27%)
  starting transfers between devices  17.8 us (24%)
  other arithmetic  1.12 us (1%)
  between operations  1.11 us (1%)
    ppermute x11, waiting for transfers between devices, swap(): return lax.ppermute(value, axis, [(i, i ^ bit) for i in range(size)])  20.2 us
    pallas_call x1, Pallas kernels, backbone(): pl.pallas_call(backbone_kernel, out_shape=(pltpu.VMEM((L, D), BF16), pltp...  16.8 us
    pallas_call x1, Pallas kernels, side_block(): pl.pallas_call(functools.partial(side_kernel, count), out_shape=(jax.Shap...  15.9 us
    ppermute x11, starting transfers between devices, swap(): return lax.ppermute(value, axis, [(i, i ^ bit) for i in range(size)])  11.7 us
    ppermute x3, starting transfers between devices, rotations(): lax.ppermute(value, 'side', [(i, (i + k) % size) for i in range(size)])  6.11 us
    pallas_call x1, Pallas kernels, finish(): pl.pallas_call(functools.partial(finish_kernel, count), out_shape=(jax.Sh...  1.69 us
  transfers between devices with their start and end apart: 14, of which 7 were waited for; matrix products, arithmetic and copies ran while one was open for 0% of the time, Pallas kernels for 22%

profile of v3, /device:TPU:0, one launch (start us, length us, event | category | flops | bytes accessed | tf_op | source)
XLA Modules:
  0.0 74.9 jit_solution(1440820539636913610)
XLA Ops:
  0.6 1.0 %pad_maximum_fusion.rest_0_ = bf16[2,96,512]{2,1,0:T(8,128)(2,1)S(1)} fusion(bf16[1,96,512]{2,1,0:T(8,128)(2,1)} %bitcast.33, bf16[1,96,512]{2,1,0:T(8,128)(2,1)} %bitcast.34), kind=kLoop, calls=%fused_computation | loop fusion | flops 98304 | bytes 393216 | tf_op jit(solution)/shard_map/stack | solution.py:667
  1.6 5.1 %collective-permute-start.2 = (bf16[2,96,512]{2,1,0:T(8,128)(2,1)S(1)}, bf16[2,96,512]{2,1,0:T(8,128)(2,1)S(1)}, u32[]{:S(2)}, u32[]{:S(2)}) collective-permute-start(bf16[2,96,512]{2,1,0:T(8,128)(2,1)S(1)} %pad_maximum_fusion.rest_0_), channel_id=1, source_target_pairs={{0,3},{1,0},{2,1},{3,2},{4,7},{5,4},{6,5},{7,6},{8,11},{9,8},{10,9... | collective-permute-start | bytes 589832 | tf_op jit(solution)/shard_map/ppermute | solution.py:606
  6.7 1.0 %collective-permute-start = (bf16[2,96,512]{2,1,0:T(8,128)(2,1)S(1)}, bf16[2,96,512]{2,1,0:T(8,128)(2,1)S(1)}, u32[]{:S(2)}, u32[]{:S(2)}) collective-permute-start(bf16[2,96,512]{2,1,0:T(8,128)(2,1)S(1)} %pad_maximum_fusion.rest_0_), channel_id=1, source_target_pairs={{0,1},{1,2},{2,3},{3,0},{4,5},{5,6},{6,7},{7,4},{8,9},{9,10},{10,1... | collective-permute-start | bytes 589832 | tf_op jit(solution)/shard_map/ppermute | solution.py:606
  7.8 16.8 %backbone.1 = (bf16[512,768]{1,0:T(8,128)(2,1)S(1)}, bf16[96,512]{1,0:T(8,128)(2,1)S(1)}) custom-call(s32[4]{0:T(128)} %lengths_ref.3, s32[4]{0:T(128)} %assign_ref.5, f32[12,32]{1,0:T(8,128)} %bitcast.41, s32[1023]{0:T(1024)} %rest_11_.1, bf16[512,768]{1,0:T(8,128)(2,1)} %bitcast.35, f32[768]{0:T(1024)} %gain1_hbm.1, bf16[768,768]{1,0:T(8,128)(2,1)} %wq_hbm.1, ...), custom_call_target="tpu_custom_call" | custom-call | flops 8999999488 | bytes 17000000 | tf_op jit(solution)/shard_map/backbone/pallas_call | solution.py:190
  24.8 15.9 %side_block.1 = (bf16[2,96,512]{2,1,0:T(8,128)(2,1)S(1)}, bf16[96,512]{1,0:T(8,128)(2,1)S(1)}, bf16[960,128]{1,0:T(8,128)(2,1)S(1)}) custom-call(s32[4]{0:T(128)S(1)} %copy-done.9, s32[4]{0:T(128)S(1)} %copy-done, bf16[2,96,512]{2,1,0:T(8,128)(2,1)S(1)} %pad_maximum_fusion.rest_0_, bf16[2,96,512]{2,1,0:T(8,128)(2,1)S(1)} %collective-permute-done.rest_1_, ...), custom_call_target="tpu_custom_call" | custom-call | flops 8999999488 | bytes 4000000 | tf_op jit(solution)/shard_map/side_block/pallas_call | solution.py:464
  40.7 0.3 pack_grads.1
  41.0 0.1 collective-permute-start.3
  41.1 1.4 %collective-permute-done.3 = bf16[2,384,128]{2,1,0:T(8,128)(2,1)S(1)} collective-permute-done((bf16[2,384,128]{2,1,0:T(8,128)(2,1)S(1)}, bf16[2,384,128]{2,1,0:T(8,128)(2,1)S(1)}, u32[]{:S(2)}, u32[]{:S(2)}) %collective-permute-start.3) | collective-permute-done | bytes 196640 | tf_op jit(solution)/shard_map/ppermute | solution.py:600
  42.6 1.6 %collective-permute-start.4 = (bf16[384,128]{1,0:T(8,128)(2,1)S(1)}, bf16[384,128]{1,0:T(8,128)(2,1)S(1)}, u32[]{:S(2)}, u32[]{:S(2)}) collective-permute-start(bf16[384,128]{1,0:T(8,128)(2,1)S(1)} %fusion.2), channel_id=1, source_target_pairs={{0,8},{4,12},{8,0},{12,4},{16,24},{20,28},{24,16},{28,20},{1,9},{5... | collective-permute-start | bytes 294920 | tf_op jit(solution)/shard_map/ppermute | solution.py:600
  44.1 1.9 %collective-permute-start.6 = (bf16[2,96,512]{2,1,0:T(8,128)(2,1)S(1)}, bf16[2,96,512]{2,1,0:T(8,128)(2,1)S(1)}, u32[]{:S(2)}, u32[]{:S(2)}) collective-permute-start(bf16[2,96,512]{2,1,0:T(8,128)(2,1)S(1)} %get-tuple-element.41.rest_4_), channel_id=1, source_target_pairs={{0,2},{1,3},{2,0},{3,1},{4,6},{5,7},{6,4},{7,5},{8,10},{9,11},{10,... | collective-permute-start | bytes 589832 | tf_op jit(solution)/shard_map/ppermute | solution.py:600
  46.1 1.4 %collective-permute-done.4 = bf16[384,128]{1,0:T(8,128)(2,1)S(1)} collective-permute-done((bf16[384,128]{1,0:T(8,128)(2,1)S(1)}, bf16[384,128]{1,0:T(8,128)(2,1)S(1)}, u32[]{:S(2)}, u32[]{:S(2)}) %collective-permute-start.4) | collective-permute-done | bytes 98336 | tf_op jit(solution)/shard_map/ppermute | solution.py:600
  47.5 2.6 %collective-permute-start.5 = (bf16[384,128]{1,0:T(8,128)(2,1)S(1)}, bf16[384,128]{1,0:T(8,128)(2,1)S(1)}, u32[]{:S(2)}, u32[]{:S(2)}) collective-permute-start(bf16[384,128]{1,0:T(8,128)(2,1)S(1)} %fusion), channel_id=1, source_target_pairs={{0,1},{1,0},{2,3},{3,2},{4,5},{5,4},{6,7},{7,6},{8,9},{9,8},{10,11... | collective-permute-start | bytes 294920 | tf_op jit(solution)/shard_map/ppermute | solution.py:600
  50.1 5.8 %collective-permute-done.6._ = bf16[2,96,512]{2,1,0:T(8,128)(2,1)S(1)} collective-permute-done((bf16[2,96,512]{2,1,0:T(8,128)(2,1)S(1)}, bf16[2,96,512]{2,1,0:T(8,128)(2,1)S(1)}, u32[]{:S(2)}, u32[]{:S(2)}) %collective-permute-start.6) | collective-permute-done | bytes 196640 | tf_op jit(solution)/shard_map/ppermute | solution.py:600
  56.0 1.5 %collective-permute-start.7 = (bf16[384,128]{1,0:T(8,128)(2,1)S(1)}, bf16[384,128]{1,0:T(8,128)(2,1)S(1)}, u32[]{:S(2)}, u32[]{:S(2)}) collective-permute-start(bf16[384,128]{1,0:T(8,128)(2,1)S(1)} %add_convert_fusion.2), channel_id=1, source_target_pairs={{0,16},{4,20},{8,24},{12,28},{16,0},{20,4},{24,8},{28,12},{1,17},{... | collective-permute-start | bytes 294920 | tf_op jit(solution)/shard_map/ppermute | solution.py:600
  57.5 3.1 %collective-permute-done.7 = bf16[384,128]{1,0:T(8,128)(2,1)S(1)} collective-permute-done((bf16[384,128]{1,0:T(8,128)(2,1)S(1)}, bf16[384,128]{1,0:T(8,128)(2,1)S(1)}, u32[]{:S(2)}, u32[]{:S(2)}) %collective-permute-start.7) | collective-permute-done | bytes 98336 | tf_op jit(solution)/shard_map/ppermute | solution.py:600
  60.7 1.4 %collective-permute-start.8 = (bf16[384,128]{1,0:T(8,128)(2,1)S(1)}, bf16[384,128]{1,0:T(8,128)(2,1)S(1)}, u32[]{:S(2)}, u32[]{:S(2)}) collective-permute-start(bf16[384,128]{1,0:T(8,128)(2,1)S(1)} %add_convert_fusion.1), channel_id=1, source_target_pairs={{0,2},{1,3},{2,0},{3,1},{4,6},{5,7},{6,4},{7,5},{8,10},{9,11},{10,... | collective-permute-start | bytes 294920 | tf_op jit(solution)/shard_map/ppermute | solution.py:600
  62.0 2.4 %collective-permute-start.12 = (bf16[2,96,512]{2,1,0:T(8,128)(2,1)S(1)}, bf16[2,96,512]{2,1,0:T(8,128)(2,1)S(1)}, u32[]{:S(2)}, u32[]{:S(2)}) collective-permute-start(bf16[2,96,512]{2,1,0:T(8,128)(2,1)S(1)} %get-tuple-element.41.rest_4_), channel_id=1, source_target_pairs={{0,1},{1,0},{2,3},{3,2},{4,5},{5,4},{6,7},{7,6},{8,9},{9,8},{10,11... | collective-permute-start | bytes 589832 | tf_op jit(solution)/shard_map/ppermute | solution.py:600
  64.5 0.0 collective-permute-start.13
  64.5 2.4 %collective-permute-done.8 = bf16[384,128]{1,0:T(8,128)(2,1)S(1)} collective-permute-done((bf16[384,128]{1,0:T(8,128)(2,1)S(1)}, bf16[384,128]{1,0:T(8,128)(2,1)S(1)}, u32[]{:S(2)}, u32[]{:S(2)}) %collective-permute-start.8) | collective-permute-done | bytes 98336 | tf_op jit(solution)/shard_map/ppermute | solution.py:600
  67.0 0.1 collective-permute-start.9
  67.1 0.1 collective-permute-start.10
  67.1 4.5 %collective-permute-done.9.rest_1_ = bf16[384,128]{1,0:T(8,128)(2,1)S(1)} collective-permute-done((bf16[384,128]{1,0:T(8,128)(2,1)S(1)}, bf16[384,128]{1,0:T(8,128)(2,1)S(1)}, u32[]{:S(2)}, u32[]{:S(2)}) %collective-permute-start.9) | collective-permute-done | bytes 98336 | tf_op jit(solution)/shard_map/ppermute | solution.py:600
  71.7 1.4 %collective-permute-done.13.rest_7_ = bf16[2,96,512]{2,1,0:T(8,128)(2,1)S(1)} collective-permute-done((bf16[2,96,512]{2,1,0:T(8,128)(2,1)S(1)}, bf16[2,96,512]{2,1,0:T(8,128)(2,1)S(1)}, u32[]{:S(2)}, u32[]{:S(2)}) %collective-permute-start.13) | collective-permute-done | bytes 196640 | tf_op jit(solution)/shard_map/ppermute | solution.py:600
  73.1 1.7 %finish.1 = (bf16[96,512]{1,0:T(8,128)(2,1)}, f32[96,512]{1,0:T(8,128)}, f32[96,768]{1,0:T(8,128)}, f32[96]{0:T(128)}, f32[96]{0:T(128)}, /*index=5*/f32[96,96]{...) custom-call(s32[4]{0:T(128)S(1)} %copy-done, ...), custom_call_target="tpu_custom_call" | custom-call | tf_op jit(solution)/shard_map/finish/pallas_call | solution.py:582
  (41 shorter events, 0.3 us)
Async XLA Ops:
  1.6 23.1 %collective-permute-start.2 = (bf16[2,96,512]{2,1,0:T(8,128)(2,1)S(1)}, bf16[2,96,512]{2,1,0:T(8,128)(2,1)S(1)}, u32[]{:S(2)}, u32[]{:S(2)}) collective-permute-start(bf16[2,96,512]{2,1,0:T(8,128)(2,1)S(1)} %pad_maximum_fusion.rest_0_), channel_id=1, source_target_pairs={{0,3},{1,0},{2,1},{3,2},{4,7},{5,4},{6,5},{7,6},{8,11},{9,8},{10,9... | collective-permute-start | bytes 589832 | tf_op jit(solution)/shard_map/ppermute | solution.py:606
  6.7 18.0 %collective-permute-start.1 = (bf16[2,96,512]{2,1,0:T(8,128)(2,1)S(1)}, bf16[2,96,512]{2,1,0:T(8,128)(2,1)S(1)}, u32[]{:S(2)}, u32[]{:S(2)}) collective-permute-start(bf16[2,96,512]{2,1,0:T(8,128)(2,1)S(1)} %pad_maximum_fusion.rest_0_), channel_id=1, source_target_pairs={{0,2},{1,3},{2,0},{3,1},{4,6},{5,7},{6,4},{7,5},{8,10},{9,11},{10,... | collective-permute-start | bytes 589832 | tf_op jit(solution)/shard_map/ppermute | solution.py:606
  6.7 18.0 %collective-permute-start = (bf16[2,96,512]{2,1,0:T(8,128)(2,1)S(1)}, bf16[2,96,512]{2,1,0:T(8,128)(2,1)S(1)}, u32[]{:S(2)}, u32[]{:S(2)}) collective-permute-start(bf16[2,96,512]{2,1,0:T(8,128)(2,1)S(1)} %pad_maximum_fusion.rest_0_), channel_id=1, source_target_pairs={{0,1},{1,2},{2,3},{3,0},{4,5},{5,6},{6,7},{7,4},{8,9},{9,10},{10,1... | collective-permute-start | bytes 589832 | tf_op jit(solution)/shard_map/ppermute | solution.py:606
  7.7 17.0 %copy-start.2 = (bf16[384,96]{0,1:T(8,128)(2,1)S(1)}, bf16[384,96]{0,1:T(8,128)(2,1)}, u32[]{:S(2)}) copy-start(bf16[384,96]{0,1:T(8,128)(2,1)} %param.50) | copy-start | bytes 221188
  7.7 17.0 %copy-start.3 = (bf16[96,96]{1,0:T(8,128)(2,1)S(1)}, bf16[96,96]{1,0:T(8,128)(2,1)}, u32[]{:S(2)}) copy-start(bf16[96,96]{1,0:T(8,128)(2,1)} %rest_8_.1) | copy-start | bytes 55300
  7.7 17.0 %copy-start.4 = (bf16[96,96]{1,0:T(8,128)(2,1)S(1)}, bf16[96,96]{1,0:T(8,128)(2,1)}, u32[]{:S(2)}) copy-start(bf16[96,96]{1,0:T(8,128)(2,1)} %rest_9_.1) | copy-start | bytes 55300
  7.7 17.0 %copy-start.5 = (bf16[96,96]{1,0:T(8,128)(2,1)S(1)}, bf16[96,96]{1,0:T(8,128)(2,1)}, u32[]{:S(2)}) copy-start(bf16[96,96]{1,0:T(8,128)(2,1)} %rest_10_.1) | copy-start | bytes 55300
  7.8 17.0 %copy-start.6 = (bf16[96,96]{1,0:T(8,128)(2,1)S(1)}, bf16[96,96]{1,0:T(8,128)(2,1)}, u32[]{:S(2)}) copy-start(bf16[96,96]{1,0:T(8,128)(2,1)} %rest_13_.1) | copy-start | bytes 55300
  7.8 17.0 %copy-start.7 = (f32[32,12]{0,1:T(8,128)S(1)}, f32[32,12]{0,1:T(8,128)}, u32[]{:S(2)}) copy-start(f32[32,12]{0,1:T(8,128)} %param.47) | copy-start | bytes 4612
  7.8 17.0 %copy-start.8 = (s32[1023]{0:T(1024)S(1)}, s32[1023]{0:T(1024)}, u32[]{:S(2)}) copy-start(s32[1023]{0:T(1024)} %rest_11_.1) | copy-start | bytes 12280
  7.8 17.0 %copy-start.9 = (s32[4]{0:T(128)S(1)}, s32[4]{0:T(128)}, u32[]{:S(2)}) copy-start(s32[4]{0:T(128)} %lengths_ref.3) | copy-start | bytes 52
  7.8 17.0 %copy-start.10 = (f32[96]{0:T(128)S(1)}, f32[96]{0:T(128)}, u32[]{:S(2)}) copy-start(f32[96]{0:T(128)} %rest_5_.1) | copy-start | bytes 1156
  7.8 17.0 %copy-start.11 = (f32[96]{0:T(128)S(1)}, f32[96]{0:T(128)}, u32[]{:S(2)}) copy-start(f32[96]{0:T(128)} %rest_6_.1) | copy-start | bytes 1156
  41.0 1.5 %collective-permute-start.3 = (bf16[2,384,128]{2,1,0:T(8,128)(2,1)S(1)}, bf16[2,384,128]{2,1,0:T(8,128)(2,1)S(1)}, u32[]{:S(2)}, u32[]{:S(2)}) collective-permute-start(bf16[2,384,128]{2,1,0:T(8,128)(2,1)S(1)} %get-tuple-element.40), channel_id=1, source_target_pairs={{0,4},{4,0},{8,12},{12,8},{16,20},{20,16},{24,28},{28,24},{1,5},{5... | collective-permute-start | bytes 589832 | tf_op jit(solution)/shard_map/ppermute | solution.py:600
  42.6 4.9 %collective-permute-start.4 = (bf16[384,128]{1,0:T(8,128)(2,1)S(1)}, bf16[384,128]{1,0:T(8,128)(2,1)S(1)}, u32[]{:S(2)}, u32[]{:S(2)}) collective-permute-start(bf16[384,128]{1,0:T(8,128)(2,1)S(1)} %fusion.2), channel_id=1, source_target_pairs={{0,8},{4,12},{8,0},{12,4},{16,24},{20,28},{24,16},{28,20},{1,9},{5... | collective-permute-start | bytes 294920 | tf_op jit(solution)/shard_map/ppermute | solution.py:600
  44.1 11.8 %collective-permute-start.6 = (bf16[2,96,512]{2,1,0:T(8,128)(2,1)S(1)}, bf16[2,96,512]{2,1,0:T(8,128)(2,1)S(1)}, u32[]{:S(2)}, u32[]{:S(2)}) collective-permute-start(bf16[2,96,512]{2,1,0:T(8,128)(2,1)S(1)} %get-tuple-element.41.rest_4_), channel_id=1, source_target_pairs={{0,2},{1,3},{2,0},{3,1},{4,6},{5,7},{6,4},{7,5},{8,10},{9,11},{10,... | collective-permute-start | bytes 589832 | tf_op jit(solution)/shard_map/ppermute | solution.py:600
  47.5 8.4 %collective-permute-start.5 = (bf16[384,128]{1,0:T(8,128)(2,1)S(1)}, bf16[384,128]{1,0:T(8,128)(2,1)S(1)}, u32[]{:S(2)}, u32[]{:S(2)}) collective-permute-start(bf16[384,128]{1,0:T(8,128)(2,1)S(1)} %fusion), channel_id=1, source_target_pairs={{0,1},{1,0},{2,3},{3,2},{4,5},{5,4},{6,7},{7,6},{8,9},{9,8},{10,11... | collective-permute-start | bytes 294920 | tf_op jit(solution)/shard_map/ppermute | solution.py:600
  56.0 4.7 %collective-permute-start.7 = (bf16[384,128]{1,0:T(8,128)(2,1)S(1)}, bf16[384,128]{1,0:T(8,128)(2,1)S(1)}, u32[]{:S(2)}, u32[]{:S(2)}) collective-permute-start(bf16[384,128]{1,0:T(8,128)(2,1)S(1)} %add_convert_fusion.2), channel_id=1, source_target_pairs={{0,16},{4,20},{8,24},{12,28},{16,0},{20,4},{24,8},{28,12},{1,17},{... | collective-permute-start | bytes 294920 | tf_op jit(solution)/shard_map/ppermute | solution.py:600
  60.7 6.3 %collective-permute-start.8 = (bf16[384,128]{1,0:T(8,128)(2,1)S(1)}, bf16[384,128]{1,0:T(8,128)(2,1)S(1)}, u32[]{:S(2)}, u32[]{:S(2)}) collective-permute-start(bf16[384,128]{1,0:T(8,128)(2,1)S(1)} %add_convert_fusion.1), channel_id=1, source_target_pairs={{0,2},{1,3},{2,0},{3,1},{4,6},{5,7},{6,4},{7,5},{8,10},{9,11},{10,... | collective-permute-start | bytes 294920 | tf_op jit(solution)/shard_map/ppermute | solution.py:600
  62.0 9.6 %collective-permute-start.12 = (bf16[2,96,512]{2,1,0:T(8,128)(2,1)S(1)}, bf16[2,96,512]{2,1,0:T(8,128)(2,1)S(1)}, u32[]{:S(2)}, u32[]{:S(2)}) collective-permute-start(bf16[2,96,512]{2,1,0:T(8,128)(2,1)S(1)} %get-tuple-element.41.rest_4_), channel_id=1, source_target_pairs={{0,1},{1,0},{2,3},{3,2},{4,5},{5,4},{6,7},{7,6},{8,9},{9,8},{10,11... | collective-permute-start | bytes 589832 | tf_op jit(solution)/shard_map/ppermute | solution.py:600
  64.5 8.6 %collective-permute-start.13 = (bf16[2,96,512]{2,1,0:T(8,128)(2,1)S(1)}, bf16[2,96,512]{2,1,0:T(8,128)(2,1)S(1)}, u32[]{:S(2)}, u32[]{:S(2)}) collective-permute-start(bf16[2,96,512]{2,1,0:T(8,128)(2,1)S(1)} %settle.1.rest_5_), channel_id=1, source_target_pairs={{0,1},{1,0},{2,3},{3,2},{4,5},{5,4},{6,7},{7,6},{8,9},{9,8},{10,11... | collective-permute-start | bytes 589832 | tf_op jit(solution)/shard_map/ppermute | solution.py:600
  67.0 4.7 %collective-permute-start.9 = (bf16[384,128]{1,0:T(8,128)(2,1)S(1)}, bf16[384,128]{1,0:T(8,128)(2,1)S(1)}, u32[]{:S(2)}, u32[]{:S(2)}) collective-permute-start(bf16[384,128]{1,0:T(8,128)(2,1)S(1)} %add_convert_fusion.rest_0_), channel_id=1, source_target_pairs={{0,8},{4,12},{8,0},{12,4},{16,24},{20,28},{24,16},{28,20},{1,9},{5... | collective-permute-start | bytes 294920 | tf_op jit(solution)/shard_map/ppermute | solution.py:600
  67.1 6.0 %collective-permute-start.10 = (bf16[384,128]{1,0:T(8,128)(2,1)S(1)}, bf16[384,128]{1,0:T(8,128)(2,1)S(1)}, u32[]{:S(2)}, u32[]{:S(2)}) collective-permute-start(bf16[384,128]{1,0:T(8,128)(2,1)S(1)} %add_convert_fusion.rest_0_), channel_id=1, source_target_pairs={{0,4},{4,0},{8,12},{12,8},{16,20},{20,16},{24,28},{28,24},{1,5},{5... | collective-permute-start | bytes 294920 | tf_op jit(solution)/shard_map/ppermute | solution.py:600
  71.7 1.4 %collective-permute-start.11 = (bf16[384,128]{1,0:T(8,128)(2,1)S(1)}, bf16[384,128]{1,0:T(8,128)(2,1)S(1)}, u32[]{:S(2)}, u32[]{:S(2)}) collective-permute-start(bf16[384,128]{1,0:T(8,128)(2,1)S(1)} %collective-permute-done.9.rest_1_), channel_id=1, source_target_pairs={{0,4},{4,0},{8,12},{12,8},{16,20},{20,16},{24,28},{28,24},{1,5},{5... | collective-permute-start | bytes 294920 | tf_op jit(solution)/shard_map/ppermute | solution.py:600
  (3 other events, 50.9 us)

commit v4 on v3

--- a/solution.py
+++ b/solution.py
@@ -28,8 +28,8 @@
 F32 = jnp.float32
 BF16 = jnp.bfloat16
 VMEM_BYTES = 44 * 1024 * 1024
-UNROLL = 6
-UNROLL_BACK = 6
+UNROLL = 12
+UNROLL_BACK = 12
 PAIRS = 6
 
 
@@ -94,12 +94,16 @@
         (w1_hbm, w1), (w2_hbm, w2), (wd_hbm, wd),
     )
     copies = [pltpu.make_async_copy(src, dst, sems.at[n]) for n, (src, dst) in enumerate(pairs)]
-    for n in (0, 1, 4):
+    for n in (2, 3, 0, 1, 4):
         copies[n].start()
     length = lengths_ref[assign_ref[lax.axis_index("side")]]
+    copies[2].wait()
+    copies[3].wait()
+    table[...] = jnp.zeros_like(table)
+    table[:H] = offset_table(buckets[...], rel[...])
     copies[0].wait()
     copies[1].wait()
-    for n in (5, 6, 2, 3):
+    for n in (5, 6):
         copies[n].start()
     x = x_ref[...].astype(F32)
     scale = lax.rsqrt(jnp.mean(x * x, axis=1, keepdims=True) + EPS)
@@ -144,10 +148,6 @@
             total = jnp.where(low_row, results[0][:, W:], results[1][:, W:])
             ctx[rows, lanes] = (top / total).astype(BF16)
 
-    copies[2].wait()
-    copies[3].wait()
-    table[...] = jnp.zeros_like(table)
-    table[:H] = offset_table(buckets[...], rel[...])
     safe = bounded(q_s[...], k_s[...], table[...], HD, H)
 
     @pl.when(safe)
@@ -256,32 +256,30 @@
 
 
 def side_kernel(count, lengths_ref, assign_ref, *rest):
-    moved_hbm, rest = rest[:count], rest[count:]
+    moved_refs, rest = rest[:count], rest[count:]
     (
-        taps_hbm, gate_hbm, gain1_hbm, gain2_hbm, wq_hbm, wk_hbm, wv_hbm, bucket_hbm, rel_hbm, wo_hbm, w1_hbm, w2_hbm,
+        taps, gate_hbm, gain1_hbm, gain2_hbm, wq, wk, wv, bucket_hbm, rel, wo, w1, w2,
         back_ref, tap_ref, rest_ref,
-        taps, vectors, wq, wk, wv, buckets, rel, wo, w1, w2,
-        moved, sems, table, probs, qt, kt, vt, dt, ctx, sums, dq, dk, dv, dall, diag, dtab,
+        vectors, buckets, moved, sems, table, probs, qt, kt, vt, dt, ctx, sums, dq, dk, dv, dall, diag, dtab,
     ) = rest
     rank = lax.axis_index("side")
     seq = assign_ref[rank]
+    pairs = (
+        (bucket_hbm, buckets.at[0]), (gate_hbm, vectors.at[0]), (gain1_hbm, vectors.at[1]),
+        (gain2_hbm, vectors.at[2]),
+    )
+    vectors[...] = jnp.zeros_like(vectors)
+    copies = start_all(pairs, sems)
     for step in range(count):
 
         @pl.when(lax.rem(rank + count - seq, count) == step)
         def _():
-            pltpu.make_async_copy(moved_hbm[step], moved, sems.at[12]).start()
-
-    pairs = (
-        (taps_hbm, taps), (gate_hbm, vectors.at[0]), (gain1_hbm, vectors.at[1]), (gain2_hbm, vectors.at[2]),
-        (wq_hbm, wq), (wk_hbm, wk), (wv_hbm, wv), (bucket_hbm, buckets.at[0]), (rel_hbm, rel), (wo_hbm, wo),
-        (w1_hbm, w1), (w2_hbm, w2),
-    )
-    vectors[...] = jnp.zeros_like(vectors)
-    copies = start_all(pairs, sems)
+            moved[...] = moved_refs[step][...]
+
     length = lengths_ref[seq]
     row8 = lax.broadcasted_iota(jnp.int32, (SHD, L), 0)
     lane8 = lax.broadcasted_iota(jnp.int32, (SHD, L), 1)
-    for copy in copies[:9]:
+    for copy in copies:
         copy.wait()
     table[...] = jnp.zeros_like(table)
     table[:SH] = offset_table(buckets[...], rel[...])
@@ -291,7 +289,6 @@
     columns = dot(eye.astype(F32), vectors[...], ((1,), (1,)), lax.Precision.HIGHEST)
     gate = jax.nn.sigmoid(columns[:, 0:1])
     gain1, gain2 = columns[:, 1:2], columns[:, 2:3]
-    pltpu.make_async_copy(moved_hbm[0], moved, sems.at[12]).wait()
     tap = taps[...].astype(F32)
     old = moved[0].astype(F32)
     mixed = gate * tap + (1.0 - gate) * old
@@ -336,8 +333,6 @@
         def _(head):
             attend(head, True)
 
-    for copy in copies[9:12]:
-        copy.wait()
     inverse = 1.0 / sums[...]
     context = ctx[...] * inverse
     context16 = context.astype(BF16)
@@ -468,21 +463,13 @@
             jax.ShapeDtypeStruct((DS, L), BF16),
             jax.ShapeDtypeStruct((PACK - QKV0, W), BF16),
         ),
-        in_specs=[smem, smem] + [hbm] * (count + len(args)),
+        in_specs=[smem, smem] + [vmem] * count + [hbm if a.ndim == 1 else vmem for a in args],
         out_specs=(vmem,) * 3,
         scratch_shapes=[
-            pltpu.VMEM((DS, L), BF16),
             pltpu.VMEM((8, DS), F32),
-            pltpu.VMEM((DS, DS), BF16),
-            pltpu.VMEM((DS, DS), BF16),
-            pltpu.VMEM((DS, DS), BF16),
             pltpu.VMEM((1, OFFSETS), jnp.int32),
-            pltpu.VMEM((SH, NB), F32),
-            pltpu.VMEM((DS, DS), BF16),
-            pltpu.VMEM((DS, FS), BF16),
-            pltpu.VMEM((DS, FS), BF16),
             pltpu.VMEM((2, DS, L), BF16),
-            pltpu.SemaphoreType.DMA((13,)),
+            pltpu.SemaphoreType.DMA((4,)),
             pltpu.VMEM((16, 2 * L), F32),
             pltpu.VMEM((SH, L, L), BF16),
             pltpu.VMEM((SH, 2 * SHD, L), BF16),
@@ -653,6 +640,9 @@
         mine = add(mine, swap(mine, "dp", bit))
     for bit in bits("side", 1):
         mine = add(mine, swap(mine, "side", bit))
+    if len(levels) > 1:
+        own = len(backs) // 2
+        mine, backs[own] = lax.optimization_barrier((mine, settle(backs[own])))
     across = swap(mine, "dp", 2)
     return (mine, across, swap(mine, "dp", 1), swap(across, "dp", 1)), backs
 

time: 75.1 us -> 73.9 us (0.984)
  waiting for transfers between devices: 20.2 us -> 22.5 us
  starting transfers between devices: 17.8 us -> 15.8 us
  Pallas kernels: 34.7 us -> 33 us
    ppermute x11, waiting for transfers between devices: 20.2 us -> 22.5 us  [swap(): return lax.ppermute(value, axis, [(i, i ^ bit) for i in range(size)])]
    ppermute x11, starting transfers between devices: 11.7 us -> 9.64 us  [swap(): return lax.ppermute(value, axis, [(i, i ^ bit) for i in range(size)])]
    pallas_call x1, Pallas kernels: 15.9 us -> 14.5 us  [side_block(): pl.pallas_call(functools.partial(side_kernel, count), out_shape=(jax.Shap...]
  transfers between devices with their start and end apart: 14 -> 14, of which waited for: 7 -> 8; matrix products, arithmetic and copies ran while one was open for 0% -> 0% of each run, Pallas kernels for 22% -> 22%
where the time goes in v4:
time: 73.9 us; the launch traced here: 73.6 us
  Pallas kernels  33 us (45%)
  waiting for transfers between devices  22.5 us (30%)
  starting transfers between devices  15.8 us (21%)
  other arithmetic  1.12 us (2%)
  between operations  1.11 us (2%)
    ppermute x11, waiting for transfers between devices, swap(): return lax.ppermute(value, axis, [(i, i ^ bit) for i in range(size)])  22.5 us
    pallas_call x1, Pallas kernels, backbone(): pl.pallas_call(backbone_kernel, out_shape=(pltpu.VMEM((L, D), BF16), pltp...  16.6 us
    pallas_call x1, Pallas kernels, side_block(): pl.pallas_call(functools.partial(side_kernel, count), out_shape=(jax.Shap...  14.5 us
    ppermute x11, starting transfers between devices, swap(): return lax.ppermute(value, axis, [(i, i ^ bit) for i in range(size)])  9.64 us
    ppermute x3, starting transfers between devices, rotations(): lax.ppermute(value, 'side', [(i, (i + k) % size) for i in range(size)])  6.11 us
    pallas_call x1, Pallas kernels, finish(): pl.pallas_call(functools.partial(finish_kernel, count), out_shape=(jax.Sh...  1.69 us
  transfers between devices with their start and end apart: 14, of which 8 were waited for; matrix products, arithmetic and copies ran while one was open for 0% of the time, Pallas kernels for 22%

profile of v4, /device:TPU:0, one launch (start us, length us, event | category | flops | bytes accessed | tf_op | source)
XLA Modules:
  0.0 73.6 jit_solution(9271414061846061146)
XLA Ops:
  0.6 1.0 %pad_maximum_fusion.rest_0_ = bf16[2,96,512]{2,1,0:T(8,128)(2,1)S(1)} fusion(bf16[1,96,512]{2,1,0:T(8,128)(2,1)} %bitcast.33, bf16[1,96,512]{2,1,0:T(8,128)(2,1)} %bitcast.34), kind=kLoop, calls=%fused_computation | loop fusion | flops 98304 | bytes 393216 | tf_op jit(solution)/shard_map/stack | solution.py:657
  1.6 5.1 %collective-permute-start.2 = (bf16[2,96,512]{2,1,0:T(8,128)(2,1)S(1)}, bf16[2,96,512]{2,1,0:T(8,128)(2,1)S(1)}, u32[]{:S(2)}, u32[]{:S(2)}) collective-permute-start(bf16[2,96,512]{2,1,0:T(8,128)(2,1)S(1)} %pad_maximum_fusion.rest_0_), channel_id=1, source_target_pairs={{0,3},{1,0},{2,1},{3,2},{4,7},{5,4},{6,5},{7,6},{8,11},{9,8},{10,9... | collective-permute-start | bytes 589832 | tf_op jit(solution)/shard_map/ppermute | solution.py:593
  6.7 1.0 %collective-permute-start = (bf16[2,96,512]{2,1,0:T(8,128)(2,1)S(1)}, bf16[2,96,512]{2,1,0:T(8,128)(2,1)S(1)}, u32[]{:S(2)}, u32[]{:S(2)}) collective-permute-start(bf16[2,96,512]{2,1,0:T(8,128)(2,1)S(1)} %pad_maximum_fusion.rest_0_), channel_id=1, source_target_pairs={{0,1},{1,2},{2,3},{3,0},{4,5},{5,6},{6,7},{7,4},{8,9},{9,10},{10,1... | collective-permute-start | bytes 589832 | tf_op jit(solution)/shard_map/ppermute | solution.py:593
  7.8 16.6 %backbone.1 = (bf16[512,768]{1,0:T(8,128)(2,1)S(1)}, bf16[96,512]{1,0:T(8,128)(2,1)S(1)}) custom-call(s32[4]{0:T(128)} %lengths_ref.3, s32[4]{0:T(128)} %assign_ref.5, f32[12,32]{1,0:T(8,128)} %bitcast.41, s32[1023]{0:T(1024)} %rest_11_.1, bf16[512,768]{1,0:T(8,128)(2,1)} %bitcast.35, f32[768]{0:T(1024)} %gain1_hbm.1, bf16[768,768]{1,0:T(8,128)(2,1)} %wq_hbm.1, ...), custom_call_target="tpu_custom_call" | custom-call | flops 8999999488 | bytes 17000000 | tf_op jit(solution)/shard_map/backbone/pallas_call | solution.py:190
  24.6 14.5 %side_block.1 = (bf16[2,96,512]{2,1,0:T(8,128)(2,1)S(1)}, bf16[96,512]{1,0:T(8,128)(2,1)S(1)}, bf16[960,128]{1,0:T(8,128)(2,1)S(1)}) custom-call(s32[4]{0:T(128)S(1)} %copy-done.9, s32[4]{0:T(128)S(1)} %copy-done, bf16[2,96,512]{2,1,0:T(8,128)(2,1)S(1)} %pad_maximum_fusion.rest_0_, bf16[2,96,512]{2,1,0:T(8,128)(2,1)S(1)} %collective-permute-done.rest_1_, ...), custom_call_target="tpu_custom_call" | custom-call | flops 8999999488 | bytes 4000000 | tf_op jit(solution)/shard_map/side_block/pallas_call | solution.py:459
  39.1 0.3 pack_grads.1
  39.4 0.1 collective-permute-start.3
  39.5 1.4 %collective-permute-done.3 = bf16[2,384,128]{2,1,0:T(8,128)(2,1)S(1)} collective-permute-done((bf16[2,384,128]{2,1,0:T(8,128)(2,1)S(1)}, bf16[2,384,128]{2,1,0:T(8,128)(2,1)S(1)}, u32[]{:S(2)}, u32[]{:S(2)}) %collective-permute-start.3) | collective-permute-done | bytes 196640 | tf_op jit(solution)/shard_map/ppermute | solution.py:587
  40.9 1.6 %collective-permute-start.4 = (bf16[384,128]{1,0:T(8,128)(2,1)S(1)}, bf16[384,128]{1,0:T(8,128)(2,1)S(1)}, u32[]{:S(2)}, u32[]{:S(2)}) collective-permute-start(bf16[384,128]{1,0:T(8,128)(2,1)S(1)} %fusion.2), channel_id=1, source_target_pairs={{0,8},{4,12},{8,0},{12,4},{16,24},{20,28},{24,16},{28,20},{1,9},{5... | collective-permute-start | bytes 294920 | tf_op jit(solution)/shard_map/ppermute | solution.py:587
  42.5 1.9 %collective-permute-start.6 = (bf16[2,96,512]{2,1,0:T(8,128)(2,1)S(1)}, bf16[2,96,512]{2,1,0:T(8,128)(2,1)S(1)}, u32[]{:S(2)}, u32[]{:S(2)}) collective-permute-start(bf16[2,96,512]{2,1,0:T(8,128)(2,1)S(1)} %get-tuple-element.43.rest_4_), channel_id=1, source_target_pairs={{0,2},{1,3},{2,0},{3,1},{4,6},{5,7},{6,4},{7,5},{8,10},{9,11},{10,... | collective-permute-start | bytes 589832 | tf_op jit(solution)/shard_map/ppermute | solution.py:587
  44.4 1.4 %collective-permute-done.4 = bf16[384,128]{1,0:T(8,128)(2,1)S(1)} collective-permute-done((bf16[384,128]{1,0:T(8,128)(2,1)S(1)}, bf16[384,128]{1,0:T(8,128)(2,1)S(1)}, u32[]{:S(2)}, u32[]{:S(2)}) %collective-permute-start.4) | collective-permute-done | bytes 98336 | tf_op jit(solution)/shard_map/ppermute | solution.py:587
  45.9 2.6 %collective-permute-start.5 = (bf16[384,128]{1,0:T(8,128)(2,1)S(1)}, bf16[384,128]{1,0:T(8,128)(2,1)S(1)}, u32[]{:S(2)}, u32[]{:S(2)}) collective-permute-start(bf16[384,128]{1,0:T(8,128)(2,1)S(1)} %fusion), channel_id=1, source_target_pairs={{0,1},{1,0},{2,3},{3,2},{4,5},{5,4},{6,7},{7,6},{8,9},{9,8},{10,11... | collective-permute-start | bytes 294920 | tf_op jit(solution)/shard_map/ppermute | solution.py:587
  48.4 5.8 %collective-permute-done.6._ = bf16[2,96,512]{2,1,0:T(8,128)(2,1)S(1)} collective-permute-done((bf16[2,96,512]{2,1,0:T(8,128)(2,1)S(1)}, bf16[2,96,512]{2,1,0:T(8,128)(2,1)S(1)}, u32[]{:S(2)}, u32[]{:S(2)}) %collective-permute-start.6) | collective-permute-done | bytes 196640 | tf_op jit(solution)/shard_map/ppermute | solution.py:587
  54.3 1.6 %collective-permute-start.7 = (bf16[384,128]{1,0:T(8,128)(2,1)S(1)}, bf16[384,128]{1,0:T(8,128)(2,1)S(1)}, u32[]{:S(2)}, u32[]{:S(2)}) collective-permute-start(bf16[384,128]{1,0:T(8,128)(2,1)S(1)} %add_convert_fusion.2), channel_id=1, source_target_pairs={{0,16},{4,20},{8,24},{12,28},{16,0},{20,4},{24,8},{28,12},{1,17},{... | collective-permute-start | bytes 294920 | tf_op jit(solution)/shard_map/ppermute | solution.py:587
  55.9 3.1 %collective-permute-done.7 = bf16[384,128]{1,0:T(8,128)(2,1)S(1)} collective-permute-done((bf16[384,128]{1,0:T(8,128)(2,1)S(1)}, bf16[384,128]{1,0:T(8,128)(2,1)S(1)}, u32[]{:S(2)}, u32[]{:S(2)}) %collective-permute-start.7) | collective-permute-done | bytes 98336 | tf_op jit(solution)/shard_map/ppermute | solution.py:587
  59.0 1.4 %collective-permute-start.8 = (bf16[384,128]{1,0:T(8,128)(2,1)S(1)}, bf16[384,128]{1,0:T(8,128)(2,1)S(1)}, u32[]{:S(2)}, u32[]{:S(2)}) collective-permute-start(bf16[384,128]{1,0:T(8,128)(2,1)S(1)} %add_convert_fusion.1), channel_id=1, source_target_pairs={{0,2},{1,3},{2,0},{3,1},{4,6},{5,7},{6,4},{7,5},{8,10},{9,11},{10,... | collective-permute-start | bytes 294920 | tf_op jit(solution)/shard_map/ppermute | solution.py:587
  60.4 2.6 %collective-permute-done.9._ = bf16[2,96,512]{2,1,0:T(8,128)(2,1)S(1)} collective-permute-done((bf16[2,96,512]{2,1,0:T(8,128)(2,1)S(1)}, bf16[2,96,512]{2,1,0:T(8,128)(2,1)S(1)}, u32[]{:S(2)}, u32[]{:S(2)}) %collective-permute-start.9) | collective-permute-done | bytes 196640 | tf_op jit(solution)/shard_map/ppermute | solution.py:587
  63.0 0.4 collective-permute-start.13
  63.4 2.4 %collective-permute-done.8 = bf16[384,128]{1,0:T(8,128)(2,1)S(1)} collective-permute-done((bf16[384,128]{1,0:T(8,128)(2,1)S(1)}, bf16[384,128]{1,0:T(8,128)(2,1)S(1)}, u32[]{:S(2)}, u32[]{:S(2)}) %collective-permute-start.8) | collective-permute-done | bytes 98336 | tf_op jit(solution)/shard_map/ppermute | solution.py:587
  65.8 0.1 collective-permute-start.10
  65.9 0.1 collective-permute-start.11
  65.9 4.5 %collective-permute-done.10.rest_1_ = bf16[384,128]{1,0:T(8,128)(2,1)S(1)} collective-permute-done((bf16[384,128]{1,0:T(8,128)(2,1)S(1)}, bf16[384,128]{1,0:T(8,128)(2,1)S(1)}, u32[]{:S(2)}, u32[]{:S(2)}) %collective-permute-start.10) | collective-permute-done | bytes 98336 | tf_op jit(solution)/shard_map/ppermute | solution.py:587
  70.5 1.3 %collective-permute-done.12.rest_3_ = bf16[384,128]{1,0:T(8,128)(2,1)S(1)} collective-permute-done((bf16[384,128]{1,0:T(8,128)(2,1)S(1)}, bf16[384,128]{1,0:T(8,128)(2,1)S(1)}, u32[]{:S(2)}, u32[]{:S(2)}) %collective-permute-start.12) | collective-permute-done | bytes 98336 | tf_op jit(solution)/shard_map/ppermute | solution.py:587
  71.8 1.7 %finish.1 = (bf16[96,512]{1,0:T(8,128)(2,1)}, f32[96,512]{1,0:T(8,128)}, f32[96,768]{1,0:T(8,128)}, f32[96]{0:T(128)}, f32[96]{0:T(128)}, /*index=5*/f32[96,96]{...) custom-call(s32[4]{0:T(128)S(1)} %copy-done, ...), custom_call_target="tpu_custom_call" | custom-call | tf_op jit(solution)/shard_map/finish/pallas_call | solution.py:569
  (42 shorter events, 0.3 us)
Async XLA Ops:
  1.6 22.8 %collective-permute-start.2 = (bf16[2,96,512]{2,1,0:T(8,128)(2,1)S(1)}, bf16[2,96,512]{2,1,0:T(8,128)(2,1)S(1)}, u32[]{:S(2)}, u32[]{:S(2)}) collective-permute-start(bf16[2,96,512]{2,1,0:T(8,128)(2,1)S(1)} %pad_maximum_fusion.rest_0_), channel_id=1, source_target_pairs={{0,3},{1,0},{2,1},{3,2},{4,7},{5,4},{6,5},{7,6},{8,11},{9,8},{10,9... | collective-permute-start | bytes 589832 | tf_op jit(solution)/shard_map/ppermute | solution.py:593
  6.7 17.7 %collective-permute-start.1 = (bf16[2,96,512]{2,1,0:T(8,128)(2,1)S(1)}, bf16[2,96,512]{2,1,0:T(8,128)(2,1)S(1)}, u32[]{:S(2)}, u32[]{:S(2)}) collective-permute-start(bf16[2,96,512]{2,1,0:T(8,128)(2,1)S(1)} %pad_maximum_fusion.rest_0_), channel_id=1, source_target_pairs={{0,2},{1,3},{2,0},{3,1},{4,6},{5,7},{6,4},{7,5},{8,10},{9,11},{10,... | collective-permute-start | bytes 589832 | tf_op jit(solution)/shard_map/ppermute | solution.py:593
  6.7 17.7 %collective-permute-start = (bf16[2,96,512]{2,1,0:T(8,128)(2,1)S(1)}, bf16[2,96,512]{2,1,0:T(8,128)(2,1)S(1)}, u32[]{:S(2)}, u32[]{:S(2)}) collective-permute-start(bf16[2,96,512]{2,1,0:T(8,128)(2,1)S(1)} %pad_maximum_fusion.rest_0_), channel_id=1, source_target_pairs={{0,1},{1,2},{2,3},{3,0},{4,5},{5,6},{6,7},{7,4},{8,9},{9,10},{10,1... | collective-permute-start | bytes 589832 | tf_op jit(solution)/shard_map/ppermute | solution.py:593
  7.7 16.7 %copy-start.2 = (bf16[384,96]{0,1:T(8,128)(2,1)S(1)}, bf16[384,96]{0,1:T(8,128)(2,1)}, u32[]{:S(2)}) copy-start(bf16[384,96]{0,1:T(8,128)(2,1)} %param.50) | copy-start | bytes 221188
  7.7 16.7 %copy-start.3 = (bf16[96,96]{1,0:T(8,128)(2,1)S(1)}, bf16[96,96]{1,0:T(8,128)(2,1)}, u32[]{:S(2)}) copy-start(bf16[96,96]{1,0:T(8,128)(2,1)} %rest_8_.1) | copy-start | bytes 55300
  7.7 16.7 %copy-start.4 = (bf16[96,96]{1,0:T(8,128)(2,1)S(1)}, bf16[96,96]{1,0:T(8,128)(2,1)}, u32[]{:S(2)}) copy-start(bf16[96,96]{1,0:T(8,128)(2,1)} %rest_9_.1) | copy-start | bytes 55300
  7.7 16.7 %copy-start.5 = (bf16[96,96]{1,0:T(8,128)(2,1)S(1)}, bf16[96,96]{1,0:T(8,128)(2,1)}, u32[]{:S(2)}) copy-start(bf16[96,96]{1,0:T(8,128)(2,1)} %rest_10_.1) | copy-start | bytes 55300
  7.8 16.7 %copy-start.6 = (bf16[96,96]{1,0:T(8,128)(2,1)S(1)}, bf16[96,96]{1,0:T(8,128)(2,1)}, u32[]{:S(2)}) copy-start(bf16[96,96]{1,0:T(8,128)(2,1)} %rest_13_.1) | copy-start | bytes 55300
  7.8 16.7 %copy-start.7 = (f32[32,12]{0,1:T(8,128)S(1)}, f32[32,12]{0,1:T(8,128)}, u32[]{:S(2)}) copy-start(f32[32,12]{0,1:T(8,128)} %param.47) | copy-start | bytes 4612
  7.8 16.7 %copy-start.8 = (s32[1023]{0:T(1024)S(1)}, s32[1023]{0:T(1024)}, u32[]{:S(2)}) copy-start(s32[1023]{0:T(1024)} %rest_11_.1) | copy-start | bytes 12280
  7.8 16.7 %copy-start.9 = (s32[4]{0:T(128)S(1)}, s32[4]{0:T(128)}, u32[]{:S(2)}) copy-start(s32[4]{0:T(128)} %lengths_ref.3) | copy-start | bytes 52
  7.8 16.7 %copy-start.10 = (f32[96]{0:T(128)S(1)}, f32[96]{0:T(128)}, u32[]{:S(2)}) copy-start(f32[96]{0:T(128)} %rest_5_.1) | copy-start | bytes 1156
  7.8 16.7 %copy-start.11 = (f32[96]{0:T(128)S(1)}, f32[96]{0:T(128)}, u32[]{:S(2)}) copy-start(f32[96]{0:T(128)} %rest_6_.1) | copy-start | bytes 1156
  39.4 1.5 %collective-permute-start.3 = (bf16[2,384,128]{2,1,0:T(8,128)(2,1)S(1)}, bf16[2,384,128]{2,1,0:T(8,128)(2,1)S(1)}, u32[]{:S(2)}, u32[]{:S(2)}) collective-permute-start(bf16[2,384,128]{2,1,0:T(8,128)(2,1)S(1)} %get-tuple-element.42), channel_id=1, source_target_pairs={{0,4},{4,0},{8,12},{12,8},{16,20},{20,16},{24,28},{28,24},{1,5},{5... | collective-permute-start | bytes 589832 | tf_op jit(solution)/shard_map/ppermute | solution.py:587
  40.9 4.9 %collective-permute-start.4 = (bf16[384,128]{1,0:T(8,128)(2,1)S(1)}, bf16[384,128]{1,0:T(8,128)(2,1)S(1)}, u32[]{:S(2)}, u32[]{:S(2)}) collective-permute-start(bf16[384,128]{1,0:T(8,128)(2,1)S(1)} %fusion.2), channel_id=1, source_target_pairs={{0,8},{4,12},{8,0},{12,4},{16,24},{20,28},{24,16},{28,20},{1,9},{5... | collective-permute-start | bytes 294920 | tf_op jit(solution)/shard_map/ppermute | solution.py:587
  42.5 11.8 %collective-permute-start.6 = (bf16[2,96,512]{2,1,0:T(8,128)(2,1)S(1)}, bf16[2,96,512]{2,1,0:T(8,128)(2,1)S(1)}, u32[]{:S(2)}, u32[]{:S(2)}) collective-permute-start(bf16[2,96,512]{2,1,0:T(8,128)(2,1)S(1)} %get-tuple-element.43.rest_4_), channel_id=1, source_target_pairs={{0,2},{1,3},{2,0},{3,1},{4,6},{5,7},{6,4},{7,5},{8,10},{9,11},{10,... | collective-permute-start | bytes 589832 | tf_op jit(solution)/shard_map/ppermute | solution.py:587
  45.9 8.4 %collective-permute-start.5 = (bf16[384,128]{1,0:T(8,128)(2,1)S(1)}, bf16[384,128]{1,0:T(8,128)(2,1)S(1)}, u32[]{:S(2)}, u32[]{:S(2)}) collective-permute-start(bf16[384,128]{1,0:T(8,128)(2,1)S(1)} %fusion), channel_id=1, source_target_pairs={{0,1},{1,0},{2,3},{3,2},{4,5},{5,4},{6,7},{7,6},{8,9},{9,8},{10,11... | collective-permute-start | bytes 294920 | tf_op jit(solution)/shard_map/ppermute | solution.py:587
  54.3 4.7 %collective-permute-start.7 = (bf16[384,128]{1,0:T(8,128)(2,1)S(1)}, bf16[384,128]{1,0:T(8,128)(2,1)S(1)}, u32[]{:S(2)}, u32[]{:S(2)}) collective-permute-start(bf16[384,128]{1,0:T(8,128)(2,1)S(1)} %add_convert_fusion.2), channel_id=1, source_target_pairs={{0,16},{4,20},{8,24},{12,28},{16,0},{20,4},{24,8},{28,12},{1,17},{... | collective-permute-start | bytes 294920 | tf_op jit(solution)/shard_map/ppermute | solution.py:587
  55.9 7.1 %collective-permute-start.9 = (bf16[2,96,512]{2,1,0:T(8,128)(2,1)S(1)}, bf16[2,96,512]{2,1,0:T(8,128)(2,1)S(1)}, u32[]{:S(2)}, u32[]{:S(2)}) collective-permute-start(bf16[2,96,512]{2,1,0:T(8,128)(2,1)S(1)} %get-tuple-element.43.rest_4_), channel_id=1, source_target_pairs={{0,1},{1,0},{2,3},{3,2},{4,5},{5,4},{6,7},{7,6},{8,9},{9,8},{10,11... | collective-permute-start | bytes 589832 | tf_op jit(solution)/shard_map/ppermute | solution.py:587
  59.0 6.7 %collective-permute-start.8 = (bf16[384,128]{1,0:T(8,128)(2,1)S(1)}, bf16[384,128]{1,0:T(8,128)(2,1)S(1)}, u32[]{:S(2)}, u32[]{:S(2)}) collective-permute-start(bf16[384,128]{1,0:T(8,128)(2,1)S(1)} %add_convert_fusion.1), channel_id=1, source_target_pairs={{0,2},{1,3},{2,0},{3,1},{4,6},{5,7},{6,4},{7,5},{8,10},{9,11},{10,... | collective-permute-start | bytes 294920 | tf_op jit(solution)/shard_map/ppermute | solution.py:587
  63.0 7.5 %collective-permute-start.13 = (bf16[2,96,512]{2,1,0:T(8,128)(2,1)S(1)}, bf16[2,96,512]{2,1,0:T(8,128)(2,1)S(1)}, u32[]{:S(2)}, u32[]{:S(2)}) collective-permute-start(bf16[2,96,512]{2,1,0:T(8,128)(2,1)S(1)} %settle.2.rest_5_), channel_id=1, source_target_pairs={{0,1},{1,0},{2,3},{3,2},{4,5},{5,4},{6,7},{7,6},{8,9},{9,8},{10,11... | collective-permute-start | bytes 589832 | tf_op jit(solution)/shard_map/ppermute | solution.py:587
  65.8 4.7 %collective-permute-start.10 = (bf16[384,128]{1,0:T(8,128)(2,1)S(1)}, bf16[384,128]{1,0:T(8,128)(2,1)S(1)}, u32[]{:S(2)}, u32[]{:S(2)}) collective-permute-start(bf16[384,128]{1,0:T(8,128)(2,1)S(1)} %add_convert_fusion.rest_0_), channel_id=1, source_target_pairs={{0,8},{4,12},{8,0},{12,4},{16,24},{20,28},{24,16},{28,20},{1,9},{5... | collective-permute-start | bytes 294920 | tf_op jit(solution)/shard_map/ppermute | solution.py:587
  65.9 4.6 %collective-permute-start.11 = (bf16[384,128]{1,0:T(8,128)(2,1)S(1)}, bf16[384,128]{1,0:T(8,128)(2,1)S(1)}, u32[]{:S(2)}, u32[]{:S(2)}) collective-permute-start(bf16[384,128]{1,0:T(8,128)(2,1)S(1)} %add_convert_fusion.rest_0_), channel_id=1, source_target_pairs={{0,4},{4,0},{8,12},{12,8},{16,20},{20,16},{24,28},{28,24},{1,5},{5... | collective-permute-start | bytes 294920 | tf_op jit(solution)/shard_map/ppermute | solution.py:587
  70.5 1.3 %collective-permute-start.12 = (bf16[384,128]{1,0:T(8,128)(2,1)S(1)}, bf16[384,128]{1,0:T(8,128)(2,1)S(1)}, u32[]{:S(2)}, u32[]{:S(2)}) collective-permute-start(bf16[384,128]{1,0:T(8,128)(2,1)S(1)} %collective-permute-done.10.rest_1_), channel_id=1, source_target_pairs={{0,4},{4,0},{8,12},{12,8},{16,20},{20,16},{24,28},{28,24},{1,5},{5... | collective-permute-start | bytes 294920 | tf_op jit(solution)/shard_map/ppermute | solution.py:587
  (3 other events, 50.2 us)

commit v5 on v4

--- a/solution.py
+++ b/solution.py
@@ -67,9 +67,8 @@
     rows = lax.broadcasted_iota(jnp.int32, (q.shape[1], W), 0) // size
     cols = lax.broadcasted_iota(jnp.int32, (q.shape[1], W), 1)
     pick = ((rows == cols) & (rows < heads)).astype(BF16)
-    qf, kf = q.astype(F32), k.astype(F32)
-    qn = jnp.max(dot((qf * qf).astype(BF16), pick), axis=0, keepdims=True)
-    kn = jnp.max(dot((kf * kf).astype(BF16), pick), axis=0, keepdims=True)
+    qn = jnp.max(dot(q * q, pick), axis=0, keepdims=True)
+    kn = jnp.max(dot(k * k, pick), axis=0, keepdims=True)
     top = jnp.max(jnp.sqrt(qn) * jnp.sqrt(kn)) * 1.02
     return top + jnp.max(jnp.abs(table)) < LIMIT
 
@@ -259,7 +258,7 @@
     moved_refs, rest = rest[:count], rest[count:]
     (
         taps, gate_hbm, gain1_hbm, gain2_hbm, wq, wk, wv, bucket_hbm, rel, wo, w1, w2,
-        back_ref, tap_ref, rest_ref,
+        out_ref, gstate_ref, tap_ref, rest_ref,
         vectors, buckets, moved, sems, table, probs, qt, kt, vt, dt, ctx, sums, dq, dk, dv, dall, diag, dtab,
     ) = rest
     rank = lax.axis_index("side")
@@ -343,7 +342,7 @@
     pre = dot_tn(w1[...], normed2)
     cdf = normal_cdf(pre)
     inner = (pre * cdf).astype(BF16)
-    back_ref[0] = (residual + dot(w2[...], inner)).astype(BF16)
+    out_ref[...] = (residual + dot(w2[...], inner)).astype(BF16)
 
     cotangent = moved[1]
     slope = cdf + pre * (jnp.exp(-0.5 * pre * pre) * (1.0 / math.sqrt(2.0 * math.pi)))
@@ -413,7 +412,7 @@
         rest_ref[n * DS : (n + 1) * DS] = full.astype(BF16)
     d_normed = dot(wq[...], grads[0]) + dot(wk[...], grads[1]) + dot(wv[...], grads[2])
     d_mixed = d_resid + norm_back(d_normed * gain1, unit1, scale1)
-    back_ref[1] = ((1.0 - gate) * d_mixed).astype(BF16)
+    gstate_ref[...] = ((1.0 - gate) * d_mixed).astype(BF16)
     tap_ref[...] = (gate * d_mixed).astype(BF16)
     g_gate = gate * (1.0 - gate) * jnp.sum(d_mixed * (tap - old), axis=1, keepdims=True)
     g_gain1 = jnp.sum(d_normed * unit1, axis=1, keepdims=True)
@@ -459,12 +458,13 @@
     return pl.pallas_call(
         functools.partial(side_kernel, count),
         out_shape=(
-            jax.ShapeDtypeStruct((2, DS, L), BF16),
-            jax.ShapeDtypeStruct((DS, L), BF16),
-            jax.ShapeDtypeStruct((PACK - QKV0, W), BF16),
+            pltpu.VMEM((DS, L), BF16),
+            pltpu.VMEM((DS, L), BF16),
+            pltpu.VMEM((DS, L), BF16),
+            pltpu.VMEM((PACK - QKV0, W), BF16),
         ),
         in_specs=[smem, smem] + [vmem] * count + [hbm if a.ndim == 1 else vmem for a in args],
-        out_specs=(vmem,) * 3,
+        out_specs=(vmem,) * 4,
         scratch_shapes=[
             pltpu.VMEM((8, DS), F32),
             pltpu.VMEM((1, OFFSETS), jnp.int32),
@@ -495,8 +495,8 @@
 
 def finish_kernel(count, assign_ref, *rest):
     quarters, rest = rest[:4], rest[4:]
-    backs, results = rest[:count], rest[count : count + 13]
-    part, out, *parts, sems = rest[count + 13 :]
+    outs, gstates, results = rest[:count], rest[count : 2 * count], rest[2 * count : 2 * count + 13]
+    part, out, *parts, sems = rest[2 * count + 13 :]
     rank = lax.axis_index("side")
     core, across = place()
     spots = [
@@ -514,8 +514,8 @@
 
         @pl.when((rank ^ slot) == masks[step])
         def _():
-            out[...] = backs[step][0]
-            gstate[...] = backs[step][1].astype(F32)
+            out[...] = outs[step][...]
+            gstate[...] = gstates[step][...].astype(F32)
 
     targets = [out, *parts]
     pairs = [
@@ -538,30 +538,36 @@
 
     for n in range(D // W):
         down[:, n * W : (n + 1) * W] = take(DOWN0 + n * DS, DOWN0 + (n + 1) * DS)
+    copies[2].start()
+    for n in range(FS // W):
+        g1[:, n * W : (n + 1) * W] = take(FFIN0 + n * DS, FFIN0 + (n + 1) * DS)
+        g2[:, n * W : (n + 1) * W] = take(FFOUT0 + n * DS, FFOUT0 + (n + 1) * DS)
+    copies[11].start()
+    copies[12].start()
     for n, ref in enumerate((gq, gk, gv)):
         ref[...] = take(QKV0 + n * DS, QKV0 + (n + 1) * DS)[:, :DS]
+        copies[5 + n].start()
     rel[...] = take(QKV0, QKV0 + 16)[:SH, DS : DS + NB]
     project = take(PROJ0, PROJ0 + DS)
     go[...] = project[:, :DS]
+    copies[8].start()
+    copies[9].start()
     turned = project.T
     gate[...] = turned[DS : DS + 1]
     gain1[...] = turned[DS + 1 : DS + 2]
     gain2[...] = turned[DS + 2 : DS + 3]
-    for n in range(FS // W):
-        g1[:, n * W : (n + 1) * W] = take(FFIN0 + n * DS, FFIN0 + (n + 1) * DS)
-        g2[:, n * W : (n + 1) * W] = take(FFOUT0 + n * DS, FFOUT0 + (n + 1) * DS)
-    for copy in copies[2:]:
-        copy.start()
+    for n in (3, 4, 10):
+        copies[n].start()
     for copy in copies:
         copy.wait()
 
 
-def finish(assign, quarters, backs):
+def finish(assign, quarters, outs, gstates):
     smem = pl.BlockSpec(memory_space=pltpu.SMEM)
     vmem = pl.BlockSpec(memory_space=pltpu.VMEM)
     hbm = pl.BlockSpec(memory_space=pl.ANY)
     fixed = pl.BlockSpec(memory_space=pltpu.HBM)
-    count = len(backs)
+    count = len(outs)
     parts = [
         (DS, L), (DS, D), (1, DS), (1, DS), (DS, DS), (DS, DS), (DS, DS), (DS, DS), (SH, NB), (1, DS), (DS, FS), (DS, FS),
     ]
@@ -569,7 +575,7 @@
     return pl.pallas_call(
         functools.partial(finish_kernel, count),
         out_shape=(jax.ShapeDtypeStruct((DS, L), BF16), *shapes),
-        in_specs=[smem] + [vmem] * (4 + count),
+        in_specs=[smem] + [vmem] * (4 + 2 * count),
         out_specs=(hbm,) * 13,
         scratch_shapes=[
             pltpu.VMEM((4, PART, W), BF16),
@@ -579,7 +585,7 @@
         ],
         compiler_params=pltpu.CompilerParams(vmem_limit_bytes=16 * 1024 * 1024),
         name="finish",
-    )(assign, *quarters, *backs)
+    )(assign, *quarters, *outs, *gstates)
 
 
 def swap(value, axis, bit):
@@ -625,26 +631,31 @@
     )(block)
 
 
-def total(keep, send, back):
+def hold(value, blocks):
+    return lax.optimization_barrier((value, [settle(block) for block in blocks]))
+
+
+def total(keep, send, out, gstate):
     levels = bits("side")[::-1]
-    backs = spread([back], levels[0])
+    outs, gstates = spread([out], levels[0]), spread([gstate], levels[0])
     got = swap(send, "dp", 1)
     mine = add(keep[0], got[0])
     across = swap(add(keep[1], got[1]), "dp", 2)
     mine = add(mine, across)
     mine = add(mine, swap(mine, "side", 1))
-    mine, backs[1] = lax.optimization_barrier((mine, settle(backs[1])))
-    for bit in levels[1:]:
-        backs = spread(backs, bit)
+    mine, outs[1:] = hold(mine, outs[1:])
     for bit in bits("dp", 2):
         mine = add(mine, swap(mine, "dp", bit))
+    mine, gstates[1:] = hold(mine, gstates[1:])
+    for bit in levels[1:]:
+        outs, gstates = spread(outs, bit), spread(gstates, bit)
     for bit in bits("side", 1):
         mine = add(mine, swap(mine, "side", bit))
     if len(levels) > 1:
-        own = len(backs) // 2
-        mine, backs[own] = lax.optimization_barrier((mine, settle(backs[own])))
+        own = len(outs) // 2
+        mine, outs[own:] = hold(mine, outs[own:])
     across = swap(mine, "dp", 2)
-    return (mine, across, swap(mine, "dp", 1), swap(across, "dp", 1)), backs
+    return (mine, across, swap(mine, "dp", 1), swap(across, "dp", 1)), outs, gstates
 
 
 def shards(
@@ -660,13 +671,13 @@
         backbone_query, backbone_key, backbone_value, backbone_project, backbone_gain_ff,
         backbone_ff_in, backbone_ff_out, down_weight.T,
     )
-    back, tap, rest = side_block(
+    out, gstate, tap, rest = side_block(
         lengths, assign, moved, taps, gate_logit, side_gain_attn, side_gain_ff,
         side_query, side_key, side_value, buckets, side_rel.T, side_project, side_ff_in, side_ff_out.T,
     )
     keep, send = pack_grads(tap, rest, hidden)
-    quarters, backs = total(keep, send, back)
-    res = finish(assign, quarters, backs)
+    quarters, outs, gstates = total(keep, send, out, gstate)
+    res = finish(assign, quarters, outs, gstates)
     out, gstate, down, gate, gain1, gq, gk, gv, go, rel, gain2, g1, g2 = res
     return (
         out.T[None], gstate.T[None], down.T, gate, gain1, gq, gk, gv, go, rel.T, gain2, g1, g2.T,

time: 73.9 us -> 73.5 us (level)
  waiting for transfers between devices: 22.5 us -> 12.1 us
  starting transfers between devices: 15.8 us -> 25.9 us
    ppermute x11 -> x14, waiting for transfers between devices: 22.5 us -> 12.1 us  [swap(): return lax.ppermute(value, axis, [(i, i ^ bit) for i in range(size)])]
    ppermute x11 -> x14, starting transfers between devices: 9.64 us -> 19.8 us  [swap(): return lax.ppermute(value, axis, [(i, i ^ bit) for i in range(size)])]
  transfers between devices with their start and end apart: 14 -> 17, of which waited for: 8 -> 10; matrix products, arithmetic and copies ran while one was open for 0% -> 0% of each run, Pallas kernels for 22% -> 23%
where the time goes in v5:
time: 73.5 us; the launch traced here: 73.3 us
  Pallas kernels  33 us (45%)
  starting transfers between devices  25.9 us (35%)
  waiting for transfers between devices  12.1 us (16%)
  other arithmetic  1.12 us (2%)
  between operations  1.1 us (1%)
    ppermute x14, starting transfers between devices, swap(): return lax.ppermute(value, axis, [(i, i ^ bit) for i in range(size)])  19.8 us
    pallas_call x1, Pallas kernels, backbone(): pl.pallas_call(backbone_kernel, out_shape=(pltpu.VMEM((L, D), BF16), pltp...  16.6 us
    pallas_call x1, Pallas kernels, side_block(): pl.pallas_call(functools.partial(side_kernel, count), out_shape=(pltpu.VM...  14.5 us
    ppermute x14, waiting for transfers between devices, swap(): return lax.ppermute(value, axis, [(i, i ^ bit) for i in range(size)])  12.1 us
    ppermute x3, starting transfers between devices, rotations(): lax.ppermute(value, 'side', [(i, (i + k) % size) for i in range(size)])  6.11 us
    pallas_call x1, Pallas kernels, finish(): pl.pallas_call(functools.partial(finish_kernel, count), out_shape=(jax.Sh...  1.68 us
  transfers between devices with their start and end apart: 17, of which 10 were waited for; matrix products, arithmetic and copies ran while one was open for 0% of the time, Pallas kernels for 23%

profile of v5, /device:TPU:0, one launch (start us, length us, event | category | flops | bytes accessed | tf_op | source)
XLA Modules:
  0.0 73.3 jit_solution(2208632675234374248)
XLA Ops:
  0.6 1.0 %pad_maximum_fusion.rest_0_ = bf16[2,96,512]{2,1,0:T(8,128)(2,1)S(1)} fusion(bf16[1,96,512]{2,1,0:T(8,128)(2,1)} %bitcast.33, bf16[1,96,512]{2,1,0:T(8,128)(2,1)} %bitcast.34), kind=kLoop, calls=%fused_computation | loop fusion | flops 98304 | bytes 393216 | tf_op jit(solution)/shard_map/stack | solution.py:668
  1.6 5.1 %collective-permute-start.2 = (bf16[2,96,512]{2,1,0:T(8,128)(2,1)S(1)}, bf16[2,96,512]{2,1,0:T(8,128)(2,1)S(1)}, u32[]{:S(2)}, u32[]{:S(2)}) collective-permute-start(bf16[2,96,512]{2,1,0:T(8,128)(2,1)S(1)} %pad_maximum_fusion.rest_0_), channel_id=1, source_target_pairs={{0,3},{1,0},{2,1},{3,2},{4,7},{5,4},{6,5},{7,6},{8,11},{9,8},{10,9... | collective-permute-start | bytes 589832 | tf_op jit(solution)/shard_map/ppermute | solution.py:599
  6.7 1.0 %collective-permute-start = (bf16[2,96,512]{2,1,0:T(8,128)(2,1)S(1)}, bf16[2,96,512]{2,1,0:T(8,128)(2,1)S(1)}, u32[]{:S(2)}, u32[]{:S(2)}) collective-permute-start(bf16[2,96,512]{2,1,0:T(8,128)(2,1)S(1)} %pad_maximum_fusion.rest_0_), channel_id=1, source_target_pairs={{0,1},{1,2},{2,3},{3,0},{4,5},{5,6},{6,7},{7,4},{8,9},{9,10},{10,1... | collective-permute-start | bytes 589832 | tf_op jit(solution)/shard_map/ppermute | solution.py:599
  7.8 16.6 %backbone.1 = (bf16[512,768]{1,0:T(8,128)(2,1)S(1)}, bf16[96,512]{1,0:T(8,128)(2,1)S(1)}) custom-call(s32[4]{0:T(128)} %lengths_ref.3, s32[4]{0:T(128)} %assign_ref.5, f32[12,32]{1,0:T(8,128)} %bitcast.41, s32[1023]{0:T(1024)} %rest_11_.1, bf16[512,768]{1,0:T(8,128)(2,1)} %bitcast.35, f32[768]{0:T(1024)} %gain1_hbm.1, bf16[768,768]{1,0:T(8,128)(2,1)} %wq_hbm.1, ...), custom_call_target="tpu_custom_call" | custom-call | flops 8999999488 | bytes 17000000 | tf_op jit(solution)/shard_map/backbone/pallas_call | solution.py:189
  24.6 14.5 %side_block.1 = (bf16[96,512]{1,0:T(8,128)(2,1)S(1)}, bf16[96,512]{1,0:T(8,128)(2,1)S(1)}, bf16[96,512]{1,0:T(8,128)(2,1)S(1)}, bf16[960,128]{1,0:T(8,128)(2,1)S(1)}) custom-call(s32[4]{0:T(128)S(1)} %copy-done.9, s32[4]{0:T(128)S(1)} %copy-done, bf16[2,96,512]{2,1,0:T(8,128)(2,1)S(1)} %pad_maximum_fusion.rest_0_, ...), custom_call_target="tpu_custom_call" | custom-call | flops 8999999488 | bytes 4000000 | tf_op jit(solution)/shard_map/side_block/pallas_call | solution.py:458
  39.5 1.4 %collective-permute-done.3 = bf16[2,384,128]{2,1,0:T(8,128)(2,1)S(1)} collective-permute-done((bf16[2,384,128]{2,1,0:T(8,128)(2,1)S(1)}, bf16[2,384,128]{2,1,0:T(8,128)(2,1)S(1)}, u32[]{:S(2)}, u32[]{:S(2)}) %collective-permute-start.3) | collective-permute-done | bytes 196640 | tf_op jit(solution)/shard_map/ppermute | solution.py:593
  40.9 1.6 %collective-permute-start.4 = (bf16[384,128]{1,0:T(8,128)(2,1)S(1)}, bf16[384,128]{1,0:T(8,128)(2,1)S(1)}, u32[]{:S(2)}, u32[]{:S(2)}) collective-permute-start(bf16[384,128]{1,0:T(8,128)(2,1)S(1)} %fusion.2), channel_id=1, source_target_pairs={{0,8},{4,12},{8,0},{12,4},{16,24},{20,28},{24,16},{28,20},{1,9},{5... | collective-permute-start | bytes 294920 | tf_op jit(solution)/shard_map/ppermute | solution.py:593
  42.5 1.9 %collective-permute-start.6 = (bf16[96,512]{1,0:T(8,128)(2,1)S(1)}, bf16[96,512]{1,0:T(8,128)(2,1)S(1)}, u32[]{:S(2)}, u32[]{:S(2)}) collective-permute-start(bf16[96,512]{1,0:T(8,128)(2,1)S(1)} %get-tuple-element.47.rest_4_), channel_id=1, source_target_pairs={{0,2},{1,3},{2,0},{3,1},{4,6},{5,7},{6,4},{7,5},{8,10},{9,11},{10,... | collective-permute-start | bytes 294920 | tf_op jit(solution)/shard_map/ppermute | solution.py:593
  44.4 1.4 %collective-permute-done.4 = bf16[384,128]{1,0:T(8,128)(2,1)S(1)} collective-permute-done((bf16[384,128]{1,0:T(8,128)(2,1)S(1)}, bf16[384,128]{1,0:T(8,128)(2,1)S(1)}, u32[]{:S(2)}, u32[]{:S(2)}) %collective-permute-start.4) | collective-permute-done | bytes 98336 | tf_op jit(solution)/shard_map/ppermute | solution.py:593
  45.9 2.5 %collective-permute-start.5 = (bf16[384,128]{1,0:T(8,128)(2,1)S(1)}, bf16[384,128]{1,0:T(8,128)(2,1)S(1)}, u32[]{:S(2)}, u32[]{:S(2)}) collective-permute-start(bf16[384,128]{1,0:T(8,128)(2,1)S(1)} %fusion), channel_id=1, source_target_pairs={{0,1},{1,0},{2,3},{3,2},{4,5},{5,4},{6,7},{7,6},{8,9},{9,8},{10,11... | collective-permute-start | bytes 294920 | tf_op jit(solution)/shard_map/ppermute | solution.py:593
  48.4 0.9 %collective-permute-start.8 = (bf16[96,512]{1,0:T(8,128)(2,1)S(1)}, bf16[96,512]{1,0:T(8,128)(2,1)S(1)}, u32[]{:S(2)}, u32[]{:S(2)}) collective-permute-start(bf16[96,512]{1,0:T(8,128)(2,1)S(1)} %get-tuple-element.49.rest_8_), channel_id=1, source_target_pairs={{0,2},{1,3},{2,0},{3,1},{4,6},{5,7},{6,4},{7,5},{8,10},{9,11},{10,... | collective-permute-start | bytes 294920 | tf_op jit(solution)/shard_map/ppermute | solution.py:593
  49.6 1.5 %collective-permute-done.5 = bf16[384,128]{1,0:T(8,128)(2,1)S(1)} collective-permute-done((bf16[384,128]{1,0:T(8,128)(2,1)S(1)}, bf16[384,128]{1,0:T(8,128)(2,1)S(1)}, u32[]{:S(2)}, u32[]{:S(2)}) %collective-permute-start.5) | collective-permute-done | bytes 98336 | tf_op jit(solution)/shard_map/ppermute | solution.py:593
  51.1 1.6 %collective-permute-start.7 = (bf16[384,128]{1,0:T(8,128)(2,1)S(1)}, bf16[384,128]{1,0:T(8,128)(2,1)S(1)}, u32[]{:S(2)}, u32[]{:S(2)}) collective-permute-start(bf16[384,128]{1,0:T(8,128)(2,1)S(1)} %add_convert_fusion.2), channel_id=1, source_target_pairs={{0,16},{4,20},{8,24},{12,28},{16,0},{20,4},{24,8},{28,12},{1,17},{... | collective-permute-start | bytes 294920 | tf_op jit(solution)/shard_map/ppermute | solution.py:593
  52.6 2.5 %collective-permute-start.10 = (bf16[96,512]{1,0:T(8,128)(2,1)S(1)}, bf16[96,512]{1,0:T(8,128)(2,1)S(1)}, u32[]{:S(2)}, u32[]{:S(2)}) collective-permute-start(bf16[96,512]{1,0:T(8,128)(2,1)S(1)} %get-tuple-element.47.rest_4_), channel_id=1, source_target_pairs={{0,1},{1,0},{2,3},{3,2},{4,5},{5,4},{6,7},{7,6},{8,9},{9,8},{10,11... | collective-permute-start | bytes 294920 | tf_op jit(solution)/shard_map/ppermute | solution.py:593
  55.3 0.5 collective-permute-done.7
  55.8 3.3 %collective-permute-start.9 = (bf16[384,128]{1,0:T(8,128)(2,1)S(1)}, bf16[384,128]{1,0:T(8,128)(2,1)S(1)}, u32[]{:S(2)}, u32[]{:S(2)}) collective-permute-start(bf16[384,128]{1,0:T(8,128)(2,1)S(1)} %add_convert_fusion.1), channel_id=1, source_target_pairs={{0,2},{1,3},{2,0},{3,1},{4,6},{5,7},{6,4},{7,5},{8,10},{9,11},{10,... | collective-permute-start | bytes 294920 | tf_op jit(solution)/shard_map/ppermute | solution.py:593
  59.1 1.6 %collective-permute-done.11._ = bf16[96,512]{1,0:T(8,128)(2,1)S(1)} collective-permute-done((bf16[96,512]{1,0:T(8,128)(2,1)S(1)}, bf16[96,512]{1,0:T(8,128)(2,1)S(1)}, u32[]{:S(2)}, u32[]{:S(2)}) %collective-permute-start.11) | collective-permute-done | bytes 98336 | tf_op jit(solution)/shard_map/ppermute | solution.py:593
  60.7 1.2 %collective-permute-done.9 = bf16[384,128]{1,0:T(8,128)(2,1)S(1)} collective-permute-done((bf16[384,128]{1,0:T(8,128)(2,1)S(1)}, bf16[384,128]{1,0:T(8,128)(2,1)S(1)}, u32[]{:S(2)}, u32[]{:S(2)}) %collective-permute-start.9) | collective-permute-done | bytes 98336 | tf_op jit(solution)/shard_map/ppermute | solution.py:593
  61.9 1.5 %collective-permute-start.12 = (bf16[384,128]{1,0:T(8,128)(2,1)S(1)}, bf16[384,128]{1,0:T(8,128)(2,1)S(1)}, u32[]{:S(2)}, u32[]{:S(2)}) collective-permute-start(bf16[384,128]{1,0:T(8,128)(2,1)S(1)} %add_convert_fusion.rest_0_), channel_id=1, source_target_pairs={{0,8},{4,12},{8,0},{12,4},{16,24},{20,28},{24,16},{28,20},{1,9},{5... | collective-permute-start | bytes 294920 | tf_op jit(solution)/shard_map/ppermute | solution.py:593
  63.4 3.4 %collective-permute-start.15 = (bf16[96,512]{1,0:T(8,128)(2,1)S(1)}, bf16[96,512]{1,0:T(8,128)(2,1)S(1)}, u32[]{:S(2)}, u32[]{:S(2)}) collective-permute-start(bf16[96,512]{1,0:T(8,128)(2,1)S(1)} %get-tuple-element.49.rest_8_), channel_id=1, source_target_pairs={{0,1},{1,0},{2,3},{3,2},{4,5},{5,4},{6,7},{7,6},{8,9},{9,8},{10,11... | collective-permute-start | bytes 294920 | tf_op jit(solution)/shard_map/ppermute | solution.py:593
  66.8 0.5 collective-permute-start.14
  67.3 2.8 %collective-permute-done.15.rest_10_ = bf16[96,512]{1,0:T(8,128)(2,1)S(1)} collective-permute-done((bf16[96,512]{1,0:T(8,128)(2,1)S(1)}, bf16[96,512]{1,0:T(8,128)(2,1)S(1)}, u32[]{:S(2)}, u32[]{:S(2)}) %collective-permute-start.15) | collective-permute-done | bytes 98336 | tf_op jit(solution)/shard_map/ppermute | solution.py:593
  70.1 1.3 %collective-permute-done.16.rest_11_ = bf16[96,512]{1,0:T(8,128)(2,1)S(1)} collective-permute-done((bf16[96,512]{1,0:T(8,128)(2,1)S(1)}, bf16[96,512]{1,0:T(8,128)(2,1)S(1)}, u32[]{:S(2)}, u32[]{:S(2)}) %collective-permute-start.16) | collective-permute-done | bytes 98336 | tf_op jit(solution)/shard_map/ppermute | solution.py:593
  71.4 1.7 %finish.1 = (bf16[96,512]{1,0:T(8,128)(2,1)}, f32[96,512]{1,0:T(8,128)}, f32[96,768]{1,0:T(8,128)}, f32[96]{0:T(128)}, f32[96]{0:T(128)}, /*index=5*/f32[96,96]{...) custom-call(s32[4]{0:T(128)S(1)} %copy-done, ...), custom_call_target="tpu_custom_call" | custom-call | tf_op jit(solution)/shard_map/finish/pallas_call | solution.py:575
  (50 shorter events, 1.1 us)
Async XLA Ops:
  1.6 22.8 %collective-permute-start.2 = (bf16[2,96,512]{2,1,0:T(8,128)(2,1)S(1)}, bf16[2,96,512]{2,1,0:T(8,128)(2,1)S(1)}, u32[]{:S(2)}, u32[]{:S(2)}) collective-permute-start(bf16[2,96,512]{2,1,0:T(8,128)(2,1)S(1)} %pad_maximum_fusion.rest_0_), channel_id=1, source_target_pairs={{0,3},{1,0},{2,1},{3,2},{4,7},{5,4},{6,5},{7,6},{8,11},{9,8},{10,9... | collective-permute-start | bytes 589832 | tf_op jit(solution)/shard_map/ppermute | solution.py:599
  6.7 17.7 %collective-permute-start.1 = (bf16[2,96,512]{2,1,0:T(8,128)(2,1)S(1)}, bf16[2,96,512]{2,1,0:T(8,128)(2,1)S(1)}, u32[]{:S(2)}, u32[]{:S(2)}) collective-permute-start(bf16[2,96,512]{2,1,0:T(8,128)(2,1)S(1)} %pad_maximum_fusion.rest_0_), channel_id=1, source_target_pairs={{0,2},{1,3},{2,0},{3,1},{4,6},{5,7},{6,4},{7,5},{8,10},{9,11},{10,... | collective-permute-start | bytes 589832 | tf_op jit(solution)/shard_map/ppermute | solution.py:599
  6.7 17.7 %collective-permute-start = (bf16[2,96,512]{2,1,0:T(8,128)(2,1)S(1)}, bf16[2,96,512]{2,1,0:T(8,128)(2,1)S(1)}, u32[]{:S(2)}, u32[]{:S(2)}) collective-permute-start(bf16[2,96,512]{2,1,0:T(8,128)(2,1)S(1)} %pad_maximum_fusion.rest_0_), channel_id=1, source_target_pairs={{0,1},{1,2},{2,3},{3,0},{4,5},{5,6},{6,7},{7,4},{8,9},{9,10},{10,1... | collective-permute-start | bytes 589832 | tf_op jit(solution)/shard_map/ppermute | solution.py:599
  7.7 16.7 %copy-start.3 = (bf16[96,96]{1,0:T(8,128)(2,1)S(1)}, bf16[96,96]{1,0:T(8,128)(2,1)}, u32[]{:S(2)}) copy-start(bf16[96,96]{1,0:T(8,128)(2,1)} %rest_8_.1) | copy-start | bytes 55300
  7.7 16.7 %copy-start.4 = (bf16[96,96]{1,0:T(8,128)(2,1)S(1)}, bf16[96,96]{1,0:T(8,128)(2,1)}, u32[]{:S(2)}) copy-start(bf16[96,96]{1,0:T(8,128)(2,1)} %rest_9_.1) | copy-start | bytes 55300
  7.7 16.7 %copy-start.5 = (bf16[96,96]{1,0:T(8,128)(2,1)S(1)}, bf16[96,96]{1,0:T(8,128)(2,1)}, u32[]{:S(2)}) copy-start(bf16[96,96]{1,0:T(8,128)(2,1)} %rest_10_.1) | copy-start | bytes 55300
  7.8 16.7 %copy-start.6 = (bf16[96,96]{1,0:T(8,128)(2,1)S(1)}, bf16[96,96]{1,0:T(8,128)(2,1)}, u32[]{:S(2)}) copy-start(bf16[96,96]{1,0:T(8,128)(2,1)} %rest_13_.1) | copy-start | bytes 55300
  7.8 16.7 %copy-start.7 = (f32[32,12]{0,1:T(8,128)S(1)}, f32[32,12]{0,1:T(8,128)}, u32[]{:S(2)}) copy-start(f32[32,12]{0,1:T(8,128)} %param.47) | copy-start | bytes 4612
  7.8 16.7 %copy-start.8 = (s32[1023]{0:T(1024)S(1)}, s32[1023]{0:T(1024)}, u32[]{:S(2)}) copy-start(s32[1023]{0:T(1024)} %rest_11_.1) | copy-start | bytes 12280
  7.8 16.7 %copy-start.9 = (s32[4]{0:T(128)S(1)}, s32[4]{0:T(128)}, u32[]{:S(2)}) copy-start(s32[4]{0:T(128)} %lengths_ref.3) | copy-start | bytes 52
  39.4 1.5 %collective-permute-start.3 = (bf16[2,384,128]{2,1,0:T(8,128)(2,1)S(1)}, bf16[2,384,128]{2,1,0:T(8,128)(2,1)S(1)}, u32[]{:S(2)}, u32[]{:S(2)}) collective-permute-start(bf16[2,384,128]{2,1,0:T(8,128)(2,1)S(1)} %get-tuple-element.46), channel_id=1, source_target_pairs={{0,4},{4,0},{8,12},{12,8},{16,20},{20,16},{24,28},{28,24},{1,5},{5... | collective-permute-start | bytes 589832 | tf_op jit(solution)/shard_map/ppermute | solution.py:593
  40.9 4.9 %collective-permute-start.4 = (bf16[384,128]{1,0:T(8,128)(2,1)S(1)}, bf16[384,128]{1,0:T(8,128)(2,1)S(1)}, u32[]{:S(2)}, u32[]{:S(2)}) collective-permute-start(bf16[384,128]{1,0:T(8,128)(2,1)S(1)} %fusion.2), channel_id=1, source_target_pairs={{0,8},{4,12},{8,0},{12,4},{16,24},{20,28},{24,16},{28,20},{1,9},{5... | collective-permute-start | bytes 294920 | tf_op jit(solution)/shard_map/ppermute | solution.py:593
  42.5 7.1 %collective-permute-start.6 = (bf16[96,512]{1,0:T(8,128)(2,1)S(1)}, bf16[96,512]{1,0:T(8,128)(2,1)S(1)}, u32[]{:S(2)}, u32[]{:S(2)}) collective-permute-start(bf16[96,512]{1,0:T(8,128)(2,1)S(1)} %get-tuple-element.47.rest_4_), channel_id=1, source_target_pairs={{0,2},{1,3},{2,0},{3,1},{4,6},{5,7},{6,4},{7,5},{8,10},{9,11},{10,... | collective-permute-start | bytes 294920 | tf_op jit(solution)/shard_map/ppermute | solution.py:593
  45.9 5.2 %collective-permute-start.5 = (bf16[384,128]{1,0:T(8,128)(2,1)S(1)}, bf16[384,128]{1,0:T(8,128)(2,1)S(1)}, u32[]{:S(2)}, u32[]{:S(2)}) collective-permute-start(bf16[384,128]{1,0:T(8,128)(2,1)S(1)} %fusion), channel_id=1, source_target_pairs={{0,1},{1,0},{2,3},{3,2},{4,5},{5,4},{6,7},{7,6},{8,9},{9,8},{10,11... | collective-permute-start | bytes 294920 | tf_op jit(solution)/shard_map/ppermute | solution.py:593
  48.4 6.8 %collective-permute-start.8 = (bf16[96,512]{1,0:T(8,128)(2,1)S(1)}, bf16[96,512]{1,0:T(8,128)(2,1)S(1)}, u32[]{:S(2)}, u32[]{:S(2)}) collective-permute-start(bf16[96,512]{1,0:T(8,128)(2,1)S(1)} %get-tuple-element.49.rest_8_), channel_id=1, source_target_pairs={{0,2},{1,3},{2,0},{3,1},{4,6},{5,7},{6,4},{7,5},{8,10},{9,11},{10,... | collective-permute-start | bytes 294920 | tf_op jit(solution)/shard_map/ppermute | solution.py:593
  51.1 4.7 %collective-permute-start.7 = (bf16[384,128]{1,0:T(8,128)(2,1)S(1)}, bf16[384,128]{1,0:T(8,128)(2,1)S(1)}, u32[]{:S(2)}, u32[]{:S(2)}) collective-permute-start(bf16[384,128]{1,0:T(8,128)(2,1)S(1)} %add_convert_fusion.2), channel_id=1, source_target_pairs={{0,16},{4,20},{8,24},{12,28},{16,0},{20,4},{24,8},{28,12},{1,17},{... | collective-permute-start | bytes 294920 | tf_op jit(solution)/shard_map/ppermute | solution.py:593
  52.6 6.4 %collective-permute-start.10 = (bf16[96,512]{1,0:T(8,128)(2,1)S(1)}, bf16[96,512]{1,0:T(8,128)(2,1)S(1)}, u32[]{:S(2)}, u32[]{:S(2)}) collective-permute-start(bf16[96,512]{1,0:T(8,128)(2,1)S(1)} %get-tuple-element.47.rest_4_), channel_id=1, source_target_pairs={{0,1},{1,0},{2,3},{3,2},{4,5},{5,4},{6,7},{7,6},{8,9},{9,8},{10,11... | collective-permute-start | bytes 294920 | tf_op jit(solution)/shard_map/ppermute | solution.py:593
  55.3 5.4 %collective-permute-start.11 = (bf16[96,512]{1,0:T(8,128)(2,1)S(1)}, bf16[96,512]{1,0:T(8,128)(2,1)S(1)}, u32[]{:S(2)}, u32[]{:S(2)}) collective-permute-start(bf16[96,512]{1,0:T(8,128)(2,1)S(1)} %settle.4.rest_5_), channel_id=1, source_target_pairs={{0,1},{1,0},{2,3},{3,2},{4,5},{5,4},{6,7},{7,6},{8,9},{9,8},{10,11... | collective-permute-start | bytes 294920 | tf_op jit(solution)/shard_map/ppermute | solution.py:593
  55.8 6.1 %collective-permute-start.9 = (bf16[384,128]{1,0:T(8,128)(2,1)S(1)}, bf16[384,128]{1,0:T(8,128)(2,1)S(1)}, u32[]{:S(2)}, u32[]{:S(2)}) collective-permute-start(bf16[384,128]{1,0:T(8,128)(2,1)S(1)} %add_convert_fusion.1), channel_id=1, source_target_pairs={{0,2},{1,3},{2,0},{3,1},{4,6},{5,7},{6,4},{7,5},{8,10},{9,11},{10,... | collective-permute-start | bytes 294920 | tf_op jit(solution)/shard_map/ppermute | solution.py:593
  61.9 4.9 %collective-permute-start.12 = (bf16[384,128]{1,0:T(8,128)(2,1)S(1)}, bf16[384,128]{1,0:T(8,128)(2,1)S(1)}, u32[]{:S(2)}, u32[]{:S(2)}) collective-permute-start(bf16[384,128]{1,0:T(8,128)(2,1)S(1)} %add_convert_fusion.rest_0_), channel_id=1, source_target_pairs={{0,8},{4,12},{8,0},{12,4},{16,24},{20,28},{24,16},{28,20},{1,9},{5... | collective-permute-start | bytes 294920 | tf_op jit(solution)/shard_map/ppermute | solution.py:593
  63.4 6.7 %collective-permute-start.15 = (bf16[96,512]{1,0:T(8,128)(2,1)S(1)}, bf16[96,512]{1,0:T(8,128)(2,1)S(1)}, u32[]{:S(2)}, u32[]{:S(2)}) collective-permute-start(bf16[96,512]{1,0:T(8,128)(2,1)S(1)} %get-tuple-element.49.rest_8_), channel_id=1, source_target_pairs={{0,1},{1,0},{2,3},{3,2},{4,5},{5,4},{6,7},{7,6},{8,9},{9,8},{10,11... | collective-permute-start | bytes 294920 | tf_op jit(solution)/shard_map/ppermute | solution.py:593
  66.8 4.6 %collective-permute-start.16 = (bf16[96,512]{1,0:T(8,128)(2,1)S(1)}, bf16[96,512]{1,0:T(8,128)(2,1)S(1)}, u32[]{:S(2)}, u32[]{:S(2)}) collective-permute-start(bf16[96,512]{1,0:T(8,128)(2,1)S(1)} %settle.5.rest_9_), channel_id=1, source_target_pairs={{0,1},{1,0},{2,3},{3,2},{4,5},{5,4},{6,7},{7,6},{8,9},{9,8},{10,11... | collective-permute-start | bytes 294920 | tf_op jit(solution)/shard_map/ppermute | solution.py:593
  66.8 4.6 %collective-permute-start.13 = (bf16[384,128]{1,0:T(8,128)(2,1)S(1)}, bf16[384,128]{1,0:T(8,128)(2,1)S(1)}, u32[]{:S(2)}, u32[]{:S(2)}) collective-permute-start(bf16[384,128]{1,0:T(8,128)(2,1)S(1)} %add_convert_fusion.rest_0_), channel_id=1, source_target_pairs={{0,4},{4,0},{8,12},{12,8},{16,20},{20,16},{24,28},{28,24},{1,5},{5... | collective-permute-start | bytes 294920 | tf_op jit(solution)/shard_map/ppermute | solution.py:593
  66.8 4.6 %collective-permute-start.14 = (bf16[384,128]{1,0:T(8,128)(2,1)S(1)}, bf16[384,128]{1,0:T(8,128)(2,1)S(1)}, u32[]{:S(2)}, u32[]{:S(2)}) collective-permute-start(bf16[384,128]{1,0:T(8,128)(2,1)S(1)} %collective-permute-done.12.rest_1_), channel_id=1, source_target_pairs={{0,4},{4,0},{8,12},{12,8},{16,20},{20,16},{24,28},{28,24},{1,5},{5... | collective-permute-start | bytes 294920 | tf_op jit(solution)/shard_map/ppermute | solution.py:593
  (6 other events, 100.4 us)

commit v6 on v5

--- a/solution.py
+++ b/solution.py
@@ -653,7 +653,9 @@
         mine = add(mine, swap(mine, "side", bit))
     if len(levels) > 1:
         own = len(outs) // 2
-        mine, outs[own:] = hold(mine, outs[own:])
+        mine, outs[own:], gstates[own : own + 1] = lax.optimization_barrier(
+            (mine, [settle(b) for b in outs[own:]], [settle(gstates[own])])
+        )
     across = swap(mine, "dp", 2)
     return (mine, across, swap(mine, "dp", 1), swap(across, "dp", 1)), outs, gstates
 

time: 73.5 us -> 73.7 us (level)
  waiting for transfers between devices: 12.1 us -> 16.8 us
  starting transfers between devices: 25.9 us -> 21.3 us
    ppermute x14, waiting for transfers between devices: 12.1 us -> 16.8 us  [swap(): return lax.ppermute(value, axis, [(i, i ^ bit) for i in range(size)])]
    ppermute x14, starting transfers between devices: 19.8 us -> 15.2 us  [swap(): return lax.ppermute(value, axis, [(i, i ^ bit) for i in range(size)])]
where the time goes in v6:
time: 73.7 us; the launch traced here: 73.5 us
  Pallas kernels  33 us (45%)
  starting transfers between devices  21.3 us (29%)
  waiting for transfers between devices  16.8 us (23%)
  other arithmetic  1.12 us (2%)
  between operations  1.1 us (1%)
    ppermute x14, waiting for transfers between devices, swap(): return lax.ppermute(value, axis, [(i, i ^ bit) for i in range(size)])  16.8 us
    pallas_call x1, Pallas kernels, backbone(): pl.pallas_call(backbone_kernel, out_shape=(pltpu.VMEM((L, D), BF16), pltp...  16.6 us
    ppermute x14, starting transfers between devices, swap(): return lax.ppermute(value, axis, [(i, i ^ bit) for i in range(size)])  15.2 us
    pallas_call x1, Pallas kernels, side_block(): pl.pallas_call(functools.partial(side_kernel, count), out_shape=(pltpu.VM...  14.5 us
    ppermute x3, starting transfers between devices, rotations(): lax.ppermute(value, 'side', [(i, (i + k) % size) for i in range(size)])  6.11 us
    pallas_call x1, Pallas kernels, finish(): pl.pallas_call(functools.partial(finish_kernel, count), out_shape=(jax.Sh...  1.68 us
  transfers between devices with their start and end apart: 17, of which 10 were waited for; matrix products, arithmetic and copies ran while one was open for 0% of the time, Pallas kernels for 23%

profile of v6, /device:TPU:0, one launch (start us, length us, event | category | flops | bytes accessed | tf_op | source)
XLA Modules:
  0.0 73.5 jit_solution(47660123151750599)
XLA Ops:
  0.6 1.0 %pad_maximum_fusion.rest_0_ = bf16[2,96,512]{2,1,0:T(8,128)(2,1)S(1)} fusion(bf16[1,96,512]{2,1,0:T(8,128)(2,1)} %bitcast.33, bf16[1,96,512]{2,1,0:T(8,128)(2,1)} %bitcast.34), kind=kLoop, calls=%fused_computation | loop fusion | flops 98304 | bytes 393216 | tf_op jit(solution)/shard_map/stack | solution.py:670
  1.6 5.1 %collective-permute-start.2 = (bf16[2,96,512]{2,1,0:T(8,128)(2,1)S(1)}, bf16[2,96,512]{2,1,0:T(8,128)(2,1)S(1)}, u32[]{:S(2)}, u32[]{:S(2)}) collective-permute-start(bf16[2,96,512]{2,1,0:T(8,128)(2,1)S(1)} %pad_maximum_fusion.rest_0_), channel_id=1, source_target_pairs={{0,3},{1,0},{2,1},{3,2},{4,7},{5,4},{6,5},{7,6},{8,11},{9,8},{10,9... | collective-permute-start | bytes 589832 | tf_op jit(solution)/shard_map/ppermute | solution.py:599
  6.7 1.0 %collective-permute-start = (bf16[2,96,512]{2,1,0:T(8,128)(2,1)S(1)}, bf16[2,96,512]{2,1,0:T(8,128)(2,1)S(1)}, u32[]{:S(2)}, u32[]{:S(2)}) collective-permute-start(bf16[2,96,512]{2,1,0:T(8,128)(2,1)S(1)} %pad_maximum_fusion.rest_0_), channel_id=1, source_target_pairs={{0,1},{1,2},{2,3},{3,0},{4,5},{5,6},{6,7},{7,4},{8,9},{9,10},{10,1... | collective-permute-start | bytes 589832 | tf_op jit(solution)/shard_map/ppermute | solution.py:599
  7.8 16.6 %backbone.1 = (bf16[512,768]{1,0:T(8,128)(2,1)S(1)}, bf16[96,512]{1,0:T(8,128)(2,1)S(1)}) custom-call(s32[4]{0:T(128)} %lengths_ref.3, s32[4]{0:T(128)} %assign_ref.5, f32[12,32]{1,0:T(8,128)} %bitcast.41, s32[1023]{0:T(1024)} %rest_11_.1, bf16[512,768]{1,0:T(8,128)(2,1)} %bitcast.35, f32[768]{0:T(1024)} %gain1_hbm.1, bf16[768,768]{1,0:T(8,128)(2,1)} %wq_hbm.1, ...), custom_call_target="tpu_custom_call" | custom-call | flops 8999999488 | bytes 17000000 | tf_op jit(solution)/shard_map/backbone/pallas_call | solution.py:189
  24.6 14.5 %side_block.1 = (bf16[96,512]{1,0:T(8,128)(2,1)S(1)}, bf16[96,512]{1,0:T(8,128)(2,1)S(1)}, bf16[96,512]{1,0:T(8,128)(2,1)S(1)}, bf16[960,128]{1,0:T(8,128)(2,1)S(1)}) custom-call(s32[4]{0:T(128)S(1)} %copy-done.9, s32[4]{0:T(128)S(1)} %copy-done, bf16[2,96,512]{2,1,0:T(8,128)(2,1)S(1)} %pad_maximum_fusion.rest_0_, ...), custom_call_target="tpu_custom_call" | custom-call | flops 8999999488 | bytes 4000000 | tf_op jit(solution)/shard_map/side_block/pallas_call | solution.py:458
  39.5 1.4 %collective-permute-done.3 = bf16[2,384,128]{2,1,0:T(8,128)(2,1)S(1)} collective-permute-done((bf16[2,384,128]{2,1,0:T(8,128)(2,1)S(1)}, bf16[2,384,128]{2,1,0:T(8,128)(2,1)S(1)}, u32[]{:S(2)}, u32[]{:S(2)}) %collective-permute-start.3) | collective-permute-done | bytes 196640 | tf_op jit(solution)/shard_map/ppermute | solution.py:593
  40.9 1.6 %collective-permute-start.4 = (bf16[384,128]{1,0:T(8,128)(2,1)S(1)}, bf16[384,128]{1,0:T(8,128)(2,1)S(1)}, u32[]{:S(2)}, u32[]{:S(2)}) collective-permute-start(bf16[384,128]{1,0:T(8,128)(2,1)S(1)} %fusion.2), channel_id=1, source_target_pairs={{0,8},{4,12},{8,0},{12,4},{16,24},{20,28},{24,16},{28,20},{1,9},{5... | collective-permute-start | bytes 294920 | tf_op jit(solution)/shard_map/ppermute | solution.py:593
  42.5 1.9 %collective-permute-start.6 = (bf16[96,512]{1,0:T(8,128)(2,1)S(1)}, bf16[96,512]{1,0:T(8,128)(2,1)S(1)}, u32[]{:S(2)}, u32[]{:S(2)}) collective-permute-start(bf16[96,512]{1,0:T(8,128)(2,1)S(1)} %get-tuple-element.48.rest_4_), channel_id=1, source_target_pairs={{0,2},{1,3},{2,0},{3,1},{4,6},{5,7},{6,4},{7,5},{8,10},{9,11},{10,... | collective-permute-start | bytes 294920 | tf_op jit(solution)/shard_map/ppermute | solution.py:593
  44.4 1.4 %collective-permute-done.4 = bf16[384,128]{1,0:T(8,128)(2,1)S(1)} collective-permute-done((bf16[384,128]{1,0:T(8,128)(2,1)S(1)}, bf16[384,128]{1,0:T(8,128)(2,1)S(1)}, u32[]{:S(2)}, u32[]{:S(2)}) %collective-permute-start.4) | collective-permute-done | bytes 98336 | tf_op jit(solution)/shard_map/ppermute | solution.py:593
  45.9 2.5 %collective-permute-start.5 = (bf16[384,128]{1,0:T(8,128)(2,1)S(1)}, bf16[384,128]{1,0:T(8,128)(2,1)S(1)}, u32[]{:S(2)}, u32[]{:S(2)}) collective-permute-start(bf16[384,128]{1,0:T(8,128)(2,1)S(1)} %fusion), channel_id=1, source_target_pairs={{0,1},{1,0},{2,3},{3,2},{4,5},{5,4},{6,7},{7,6},{8,9},{9,8},{10,11... | collective-permute-start | bytes 294920 | tf_op jit(solution)/shard_map/ppermute | solution.py:593
  48.5 1.9 %collective-permute-start.12 = (bf16[96,512]{1,0:T(8,128)(2,1)S(1)}, bf16[96,512]{1,0:T(8,128)(2,1)S(1)}, u32[]{:S(2)}, u32[]{:S(2)}) collective-permute-start(bf16[96,512]{1,0:T(8,128)(2,1)S(1)} %get-tuple-element.50.rest_8_), channel_id=1, source_target_pairs={{0,1},{1,0},{2,3},{3,2},{4,5},{5,4},{6,7},{7,6},{8,9},{9,8},{10,11... | collective-permute-start | bytes 294920 | tf_op jit(solution)/shard_map/ppermute | solution.py:593
  50.5 0.9 %collective-permute-start.8 = (bf16[96,512]{1,0:T(8,128)(2,1)S(1)}, bf16[96,512]{1,0:T(8,128)(2,1)S(1)}, u32[]{:S(2)}, u32[]{:S(2)}) collective-permute-start(bf16[96,512]{1,0:T(8,128)(2,1)S(1)} %get-tuple-element.50.rest_8_), channel_id=1, source_target_pairs={{0,2},{1,3},{2,0},{3,1},{4,6},{5,7},{6,4},{7,5},{8,10},{9,11},{10,... | collective-permute-start | bytes 294920 | tf_op jit(solution)/shard_map/ppermute | solution.py:593
  51.4 0.6 collective-permute-done.5
  52.0 1.6 %collective-permute-start.7 = (bf16[384,128]{1,0:T(8,128)(2,1)S(1)}, bf16[384,128]{1,0:T(8,128)(2,1)S(1)}, u32[]{:S(2)}, u32[]{:S(2)}) collective-permute-start(bf16[384,128]{1,0:T(8,128)(2,1)S(1)} %add_convert_fusion.2), channel_id=1, source_target_pairs={{0,16},{4,20},{8,24},{12,28},{16,0},{20,4},{24,8},{28,12},{1,17},{... | collective-permute-start | bytes 294920 | tf_op jit(solution)/shard_map/ppermute | solution.py:593
  53.6 2.1 %collective-permute-done.10._ = bf16[96,512]{1,0:T(8,128)(2,1)S(1)} collective-permute-done((bf16[96,512]{1,0:T(8,128)(2,1)S(1)}, bf16[96,512]{1,0:T(8,128)(2,1)S(1)}, u32[]{:S(2)}, u32[]{:S(2)}) %collective-permute-start.10) | collective-permute-done | bytes 98336 | tf_op jit(solution)/shard_map/ppermute | solution.py:593
  55.7 1.0 %collective-permute-done.8._ = bf16[96,512]{1,0:T(8,128)(2,1)S(1)} collective-permute-done((bf16[96,512]{1,0:T(8,128)(2,1)S(1)}, bf16[96,512]{1,0:T(8,128)(2,1)S(1)}, u32[]{:S(2)}, u32[]{:S(2)}) %collective-permute-start.8) | collective-permute-done | bytes 98336 | tf_op jit(solution)/shard_map/ppermute | solution.py:593
  56.7 2.2 %collective-permute-start.11 = (bf16[96,512]{1,0:T(8,128)(2,1)S(1)}, bf16[96,512]{1,0:T(8,128)(2,1)S(1)}, u32[]{:S(2)}, u32[]{:S(2)}) collective-permute-start(bf16[96,512]{1,0:T(8,128)(2,1)S(1)} %settle.5.rest_5_), channel_id=1, source_target_pairs={{0,1},{1,0},{2,3},{3,2},{4,5},{5,4},{6,7},{7,6},{8,9},{9,8},{10,11... | collective-permute-start | bytes 294920 | tf_op jit(solution)/shard_map/ppermute | solution.py:593
  58.9 1.0 %collective-permute-start.9 = (bf16[384,128]{1,0:T(8,128)(2,1)S(1)}, bf16[384,128]{1,0:T(8,128)(2,1)S(1)}, u32[]{:S(2)}, u32[]{:S(2)}) collective-permute-start(bf16[384,128]{1,0:T(8,128)(2,1)S(1)} %add_convert_fusion.1), channel_id=1, source_target_pairs={{0,2},{1,3},{2,0},{3,1},{4,6},{5,7},{6,4},{7,5},{8,10},{9,11},{10,... | collective-permute-start | bytes 294920 | tf_op jit(solution)/shard_map/ppermute | solution.py:593
  60.0 1.6 %collective-permute-done.11._ = bf16[96,512]{1,0:T(8,128)(2,1)S(1)} collective-permute-done((bf16[96,512]{1,0:T(8,128)(2,1)S(1)}, bf16[96,512]{1,0:T(8,128)(2,1)S(1)}, u32[]{:S(2)}, u32[]{:S(2)}) %collective-permute-start.11) | collective-permute-done | bytes 98336 | tf_op jit(solution)/shard_map/ppermute | solution.py:593
  61.5 4.1 %collective-permute-done.9 = bf16[384,128]{1,0:T(8,128)(2,1)S(1)} collective-permute-done((bf16[384,128]{1,0:T(8,128)(2,1)S(1)}, bf16[384,128]{1,0:T(8,128)(2,1)S(1)}, u32[]{:S(2)}, u32[]{:S(2)}) %collective-permute-start.9) | collective-permute-done | bytes 98336 | tf_op jit(solution)/shard_map/ppermute | solution.py:593
  65.6 1.0 %collective-permute-start.13 = (bf16[384,128]{1,0:T(8,128)(2,1)S(1)}, bf16[384,128]{1,0:T(8,128)(2,1)S(1)}, u32[]{:S(2)}, u32[]{:S(2)}) collective-permute-start(bf16[384,128]{1,0:T(8,128)(2,1)S(1)} %add_convert_fusion.rest_0_), channel_id=1, source_target_pairs={{0,8},{4,12},{8,0},{12,4},{16,24},{20,28},{24,16},{28,20},{1,9},{5... | collective-permute-start | bytes 294920 | tf_op jit(solution)/shard_map/ppermute | solution.py:593
  67.0 3.3 %collective-permute-done.13.rest_1_ = bf16[384,128]{1,0:T(8,128)(2,1)S(1)} collective-permute-done((bf16[384,128]{1,0:T(8,128)(2,1)S(1)}, bf16[384,128]{1,0:T(8,128)(2,1)S(1)}, u32[]{:S(2)}, u32[]{:S(2)}) %collective-permute-start.13) | collective-permute-done | bytes 98336 | tf_op jit(solution)/shard_map/ppermute | solution.py:593
  70.3 0.9 %collective-permute-done.16.rest_11_ = bf16[96,512]{1,0:T(8,128)(2,1)S(1)} collective-permute-done((bf16[96,512]{1,0:T(8,128)(2,1)S(1)}, bf16[96,512]{1,0:T(8,128)(2,1)S(1)}, u32[]{:S(2)}, u32[]{:S(2)}) %collective-permute-start.16) | collective-permute-done | bytes 98336 | tf_op jit(solution)/shard_map/ppermute | solution.py:593
  71.6 1.7 %finish.1 = (bf16[96,512]{1,0:T(8,128)(2,1)}, f32[96,512]{1,0:T(8,128)}, f32[96,768]{1,0:T(8,128)}, f32[96]{0:T(128)}, f32[96]{0:T(128)}, /*index=5*/f32[96,96]{...) custom-call(s32[4]{0:T(128)S(1)} %copy-done, ...), custom_call_target="tpu_custom_call" | custom-call | tf_op jit(solution)/shard_map/finish/pallas_call | solution.py:575
  (51 shorter events, 1.5 us)
Async XLA Ops:
  1.6 22.8 %collective-permute-start.2 = (bf16[2,96,512]{2,1,0:T(8,128)(2,1)S(1)}, bf16[2,96,512]{2,1,0:T(8,128)(2,1)S(1)}, u32[]{:S(2)}, u32[]{:S(2)}) collective-permute-start(bf16[2,96,512]{2,1,0:T(8,128)(2,1)S(1)} %pad_maximum_fusion.rest_0_), channel_id=1, source_target_pairs={{0,3},{1,0},{2,1},{3,2},{4,7},{5,4},{6,5},{7,6},{8,11},{9,8},{10,9... | collective-permute-start | bytes 589832 | tf_op jit(solution)/shard_map/ppermute | solution.py:599
  6.7 17.7 %collective-permute-start.1 = (bf16[2,96,512]{2,1,0:T(8,128)(2,1)S(1)}, bf16[2,96,512]{2,1,0:T(8,128)(2,1)S(1)}, u32[]{:S(2)}, u32[]{:S(2)}) collective-permute-start(bf16[2,96,512]{2,1,0:T(8,128)(2,1)S(1)} %pad_maximum_fusion.rest_0_), channel_id=1, source_target_pairs={{0,2},{1,3},{2,0},{3,1},{4,6},{5,7},{6,4},{7,5},{8,10},{9,11},{10,... | collective-permute-start | bytes 589832 | tf_op jit(solution)/shard_map/ppermute | solution.py:599
  6.7 17.7 %collective-permute-start = (bf16[2,96,512]{2,1,0:T(8,128)(2,1)S(1)}, bf16[2,96,512]{2,1,0:T(8,128)(2,1)S(1)}, u32[]{:S(2)}, u32[]{:S(2)}) collective-permute-start(bf16[2,96,512]{2,1,0:T(8,128)(2,1)S(1)} %pad_maximum_fusion.rest_0_), channel_id=1, source_target_pairs={{0,1},{1,2},{2,3},{3,0},{4,5},{5,6},{6,7},{7,4},{8,9},{9,10},{10,1... | collective-permute-start | bytes 589832 | tf_op jit(solution)/shard_map/ppermute | solution.py:599
  7.7 16.7 %copy-start.3 = (bf16[96,96]{1,0:T(8,128)(2,1)S(1)}, bf16[96,96]{1,0:T(8,128)(2,1)}, u32[]{:S(2)}) copy-start(bf16[96,96]{1,0:T(8,128)(2,1)} %rest_8_.1) | copy-start | bytes 55300
  7.7 16.7 %copy-start.4 = (bf16[96,96]{1,0:T(8,128)(2,1)S(1)}, bf16[96,96]{1,0:T(8,128)(2,1)}, u32[]{:S(2)}) copy-start(bf16[96,96]{1,0:T(8,128)(2,1)} %rest_9_.1) | copy-start | bytes 55300
  7.7 16.7 %copy-start.5 = (bf16[96,96]{1,0:T(8,128)(2,1)S(1)}, bf16[96,96]{1,0:T(8,128)(2,1)}, u32[]{:S(2)}) copy-start(bf16[96,96]{1,0:T(8,128)(2,1)} %rest_10_.1) | copy-start | bytes 55300
  7.8 16.7 %copy-start.6 = (bf16[96,96]{1,0:T(8,128)(2,1)S(1)}, bf16[96,96]{1,0:T(8,128)(2,1)}, u32[]{:S(2)}) copy-start(bf16[96,96]{1,0:T(8,128)(2,1)} %rest_13_.1) | copy-start | bytes 55300
  7.8 16.7 %copy-start.7 = (f32[32,12]{0,1:T(8,128)S(1)}, f32[32,12]{0,1:T(8,128)}, u32[]{:S(2)}) copy-start(f32[32,12]{0,1:T(8,128)} %param.47) | copy-start | bytes 4612
  7.8 16.7 %copy-start.8 = (s32[1023]{0:T(1024)S(1)}, s32[1023]{0:T(1024)}, u32[]{:S(2)}) copy-start(s32[1023]{0:T(1024)} %rest_11_.1) | copy-start | bytes 12280
  7.8 16.7 %copy-start.9 = (s32[4]{0:T(128)S(1)}, s32[4]{0:T(128)}, u32[]{:S(2)}) copy-start(s32[4]{0:T(128)} %lengths_ref.3) | copy-start | bytes 52
  39.4 1.5 %collective-permute-start.3 = (bf16[2,384,128]{2,1,0:T(8,128)(2,1)S(1)}, bf16[2,384,128]{2,1,0:T(8,128)(2,1)S(1)}, u32[]{:S(2)}, u32[]{:S(2)}) collective-permute-start(bf16[2,384,128]{2,1,0:T(8,128)(2,1)S(1)} %get-tuple-element.47), channel_id=1, source_target_pairs={{0,4},{4,0},{8,12},{12,8},{16,20},{20,16},{24,28},{28,24},{1,5},{5... | collective-permute-start | bytes 589832 | tf_op jit(solution)/shard_map/ppermute | solution.py:593
  40.9 4.9 %collective-permute-start.4 = (bf16[384,128]{1,0:T(8,128)(2,1)S(1)}, bf16[384,128]{1,0:T(8,128)(2,1)S(1)}, u32[]{:S(2)}, u32[]{:S(2)}) collective-permute-start(bf16[384,128]{1,0:T(8,128)(2,1)S(1)} %fusion.2), channel_id=1, source_target_pairs={{0,8},{4,12},{8,0},{12,4},{16,24},{20,28},{24,16},{28,20},{1,9},{5... | collective-permute-start | bytes 294920 | tf_op jit(solution)/shard_map/ppermute | solution.py:593
  42.5 8.9 %collective-permute-start.6 = (bf16[96,512]{1,0:T(8,128)(2,1)S(1)}, bf16[96,512]{1,0:T(8,128)(2,1)S(1)}, u32[]{:S(2)}, u32[]{:S(2)}) collective-permute-start(bf16[96,512]{1,0:T(8,128)(2,1)S(1)} %get-tuple-element.48.rest_4_), channel_id=1, source_target_pairs={{0,2},{1,3},{2,0},{3,1},{4,6},{5,7},{6,4},{7,5},{8,10},{9,11},{10,... | collective-permute-start | bytes 294920 | tf_op jit(solution)/shard_map/ppermute | solution.py:593
  45.9 6.1 %collective-permute-start.5 = (bf16[384,128]{1,0:T(8,128)(2,1)S(1)}, bf16[384,128]{1,0:T(8,128)(2,1)S(1)}, u32[]{:S(2)}, u32[]{:S(2)}) collective-permute-start(bf16[384,128]{1,0:T(8,128)(2,1)S(1)} %fusion), channel_id=1, source_target_pairs={{0,1},{1,0},{2,3},{3,2},{4,5},{5,4},{6,7},{7,6},{8,9},{9,8},{10,11... | collective-permute-start | bytes 294920 | tf_op jit(solution)/shard_map/ppermute | solution.py:593
  48.4 7.3 %collective-permute-start.10 = (bf16[96,512]{1,0:T(8,128)(2,1)S(1)}, bf16[96,512]{1,0:T(8,128)(2,1)S(1)}, u32[]{:S(2)}, u32[]{:S(2)}) collective-permute-start(bf16[96,512]{1,0:T(8,128)(2,1)S(1)} %get-tuple-element.48.rest_4_), channel_id=1, source_target_pairs={{0,1},{1,0},{2,3},{3,2},{4,5},{5,4},{6,7},{7,6},{8,9},{9,8},{10,11... | collective-permute-start | bytes 294920 | tf_op jit(solution)/shard_map/ppermute | solution.py:593
  48.5 11.5 %collective-permute-start.12 = (bf16[96,512]{1,0:T(8,128)(2,1)S(1)}, bf16[96,512]{1,0:T(8,128)(2,1)S(1)}, u32[]{:S(2)}, u32[]{:S(2)}) collective-permute-start(bf16[96,512]{1,0:T(8,128)(2,1)S(1)} %get-tuple-element.50.rest_8_), channel_id=1, source_target_pairs={{0,1},{1,0},{2,3},{3,2},{4,5},{5,4},{6,7},{7,6},{8,9},{9,8},{10,11... | collective-permute-start | bytes 294920 | tf_op jit(solution)/shard_map/ppermute | solution.py:593
  50.5 6.3 %collective-permute-start.8 = (bf16[96,512]{1,0:T(8,128)(2,1)S(1)}, bf16[96,512]{1,0:T(8,128)(2,1)S(1)}, u32[]{:S(2)}, u32[]{:S(2)}) collective-permute-start(bf16[96,512]{1,0:T(8,128)(2,1)S(1)} %get-tuple-element.50.rest_8_), channel_id=1, source_target_pairs={{0,2},{1,3},{2,0},{3,1},{4,6},{5,7},{6,4},{7,5},{8,10},{9,11},{10,... | collective-permute-start | bytes 294920 | tf_op jit(solution)/shard_map/ppermute | solution.py:593
  52.0 6.9 %collective-permute-start.7 = (bf16[384,128]{1,0:T(8,128)(2,1)S(1)}, bf16[384,128]{1,0:T(8,128)(2,1)S(1)}, u32[]{:S(2)}, u32[]{:S(2)}) collective-permute-start(bf16[384,128]{1,0:T(8,128)(2,1)S(1)} %add_convert_fusion.2), channel_id=1, source_target_pairs={{0,16},{4,20},{8,24},{12,28},{16,0},{20,4},{24,8},{28,12},{1,17},{... | collective-permute-start | bytes 294920 | tf_op jit(solution)/shard_map/ppermute | solution.py:593
  56.7 4.8 %collective-permute-start.11 = (bf16[96,512]{1,0:T(8,128)(2,1)S(1)}, bf16[96,512]{1,0:T(8,128)(2,1)S(1)}, u32[]{:S(2)}, u32[]{:S(2)}) collective-permute-start(bf16[96,512]{1,0:T(8,128)(2,1)S(1)} %settle.5.rest_5_), channel_id=1, source_target_pairs={{0,1},{1,0},{2,3},{3,2},{4,5},{5,4},{6,7},{7,6},{8,9},{9,8},{10,11... | collective-permute-start | bytes 294920 | tf_op jit(solution)/shard_map/ppermute | solution.py:593
  58.9 6.6 %collective-permute-start.9 = (bf16[384,128]{1,0:T(8,128)(2,1)S(1)}, bf16[384,128]{1,0:T(8,128)(2,1)S(1)}, u32[]{:S(2)}, u32[]{:S(2)}) collective-permute-start(bf16[384,128]{1,0:T(8,128)(2,1)S(1)} %add_convert_fusion.1), channel_id=1, source_target_pairs={{0,2},{1,3},{2,0},{3,1},{4,6},{5,7},{6,4},{7,5},{8,10},{9,11},{10,... | collective-permute-start | bytes 294920 | tf_op jit(solution)/shard_map/ppermute | solution.py:593
  65.6 4.7 %collective-permute-start.13 = (bf16[384,128]{1,0:T(8,128)(2,1)S(1)}, bf16[384,128]{1,0:T(8,128)(2,1)S(1)}, u32[]{:S(2)}, u32[]{:S(2)}) collective-permute-start(bf16[384,128]{1,0:T(8,128)(2,1)S(1)} %add_convert_fusion.rest_0_), channel_id=1, source_target_pairs={{0,8},{4,12},{8,0},{12,4},{16,24},{20,28},{24,16},{28,20},{1,9},{5... | collective-permute-start | bytes 294920 | tf_op jit(solution)/shard_map/ppermute | solution.py:593
  66.6 4.6 %collective-permute-start.16 = (bf16[96,512]{1,0:T(8,128)(2,1)S(1)}, bf16[96,512]{1,0:T(8,128)(2,1)S(1)}, u32[]{:S(2)}, u32[]{:S(2)}) collective-permute-start(bf16[96,512]{1,0:T(8,128)(2,1)S(1)} %settle.6.rest_9_), channel_id=1, source_target_pairs={{0,1},{1,0},{2,3},{3,2},{4,5},{5,4},{6,7},{7,6},{8,9},{9,8},{10,11... | collective-permute-start | bytes 294920 | tf_op jit(solution)/shard_map/ppermute | solution.py:593
  67.0 4.2 %collective-permute-start.14 = (bf16[384,128]{1,0:T(8,128)(2,1)S(1)}, bf16[384,128]{1,0:T(8,128)(2,1)S(1)}, u32[]{:S(2)}, u32[]{:S(2)}) collective-permute-start(bf16[384,128]{1,0:T(8,128)(2,1)S(1)} %add_convert_fusion.rest_0_), channel_id=1, source_target_pairs={{0,4},{4,0},{8,12},{12,8},{16,20},{20,16},{24,28},{28,24},{1,5},{5... | collective-permute-start | bytes 294920 | tf_op jit(solution)/shard_map/ppermute | solution.py:593
  70.3 1.3 %collective-permute-start.15 = (bf16[384,128]{1,0:T(8,128)(2,1)S(1)}, bf16[384,128]{1,0:T(8,128)(2,1)S(1)}, u32[]{:S(2)}, u32[]{:S(2)}) collective-permute-start(bf16[384,128]{1,0:T(8,128)(2,1)S(1)} %collective-permute-done.13.rest_1_), channel_id=1, source_target_pairs={{0,4},{4,0},{8,12},{12,8},{16,20},{20,16},{24,28},{28,24},{1,5},{5... | collective-permute-start | bytes 294920 | tf_op jit(solution)/shard_map/ppermute | solution.py:593
  (6 other events, 100.4 us)
